TPU v7x, 512 devices: a whole 4x8x8 slice. The times are simulated.
512 devices in a mesh: dom: 32 (over x, z), slab: 8 (over y), chan: 2 (over core).
Axes of the slice: x: 4, y: 8, z: 8, core: 2. Of those that a mesh axis runs over, the one named last changes fastest.
Arguments:
- point_features: bfloat16 [64, 2097152], P('chan', ('dom', 'slab')), may hold values from -0.8984375 to 0.8984375
- neighbour_cells: int32 [8, 2097152], P(None, ('dom', 'slab')), may hold values from 0 to 127
- neighbour_weights: float32 [8, 2097152], P(None, ('dom', 'slab')), may hold values from 0.1 to 1
- live_points: int32 [256], P(('dom', 'slab')), may hold values from 2048 to 8192, as said below
- tile_target: int32 [16384], P(('dom', 'slab')), may hold values from 0 to 127, as said below
- conv_kernel: bfloat16 [27, 64, 64], replicated, may hold values from -0.15625 to 0.15625
- cotangent: bfloat16 [64, 16, 64, 128], P('chan', 'slab', 'dom'), may hold values from -6 to 6
Outputs:
- latent: bfloat16 [64, 16, 64, 128], P('chan', 'slab', 'dom')
- feature_grad: bfloat16 [64, 2097152], P('chan', ('dom', 'slab'))
- kernel_grad: float32 [27, 64, 64], replicated
Inputs may be any that keep to these rules, and one draw needn't show every extreme that they name: `live_points`: some partition has all its 8192 points live. Among the 64 tiles of one partition at most 4 have tile_target // 4 equal to any one dom index; in every slab some dom index gets exactly 4 tiles from every partition of that slab.
All inputs are finite; a program needn't handle non-finite values.
Results may differ from a plain program's by a relative error of at most 0.014.
Values may be sent and summed in bfloat16 or wider, within the bound.
No kernel may reach another device: no remote copies, remote signals or barrier semaphores. Data moves between devices by JAX's collectives and lax.ppermute only.
A program may use at most 64 MiB of HBM per device.

v0:
```python
import jax
import jax.numpy as jnp
from jax import lax
from jax.sharding import PartitionSpec as P


def padded_2(value, sides, width):
    for axis, dim in sides:
        peers, length = (lax.axis_size(axis), value.shape[dim])
        up = [(i, (i + 1) % peers) for i in range(peers - 1)]
        down = [(j, i) for i, j in up]
        last = lax.slice_in_dim(value, length - width, length, axis=dim)
        first = lax.slice_in_dim(value, 0, width, axis=dim)
        before = lax.ppermute(last, axis, up)
        after = lax.ppermute(first, axis, down)
        value = jnp.concatenate([before, value, after], axis=dim)
    return value


def conv_forward(padded, kernel, zpad):
    rhs = kernel.reshape(3, 3, 3, kernel.shape[1], kernel.shape[2])
    result = lax.conv_general_dilated(
        padded[None],
        rhs,
        (1, 1, 1),
        [(0, 0), (0, 0), (zpad, zpad)],
        dimension_numbers=("NCDHW", "DHWIO", "NCDHW"),
        preferred_element_type=jnp.float32,
    )
    return result[0]


def conv_backward(padded, kernel, zpad):
    rhs = kernel.reshape(3, 3, 3, kernel.shape[1], kernel.shape[2])[::-1, ::-1, ::-1].transpose(
        0, 1, 2, 4, 3
    )
    result = lax.conv_general_dilated(
        padded[None],
        rhs,
        (1, 1, 1),
        [(0, 0), (0, 0), (zpad, zpad)],
        dimension_numbers=("NCDHW", "DHWIO", "NCDHW"),
        preferred_element_type=jnp.float32,
    )
    return result[0]


def kernel_product(padded, grads, zpad):
    result = lax.conv_general_dilated(
        padded[:, None],
        grads[:, None],
        (1, 1, 1),
        [(0, 0), (0, 0), (zpad, zpad)],
        dimension_numbers=("NCDHW", "OIDHW", "NCDHW"),
        preferred_element_type=jnp.float32,
    )
    return result.transpose(2, 3, 4, 0, 1).reshape(27, padded.shape[0], grads.shape[0])


def body(
    point_features,
    neighbour_cells,
    neighbour_weights,
    live_points,
    tile_target,
    conv_kernel,
    cotangent,
):
    half, npts = point_features.shape
    nbrs = neighbour_cells.shape[0]
    xsize, ysize, zsize = (cotangent.shape[1], cotangent.shape[2], cotangent.shape[3])
    tiles = tile_target.shape[0]
    tile = npts // tiles
    groups = tiles // 8
    n_dom = lax.axis_size("dom")
    cap = 2 * tiles // n_dom
    width = xsize * ysize
    live = live_points[0]
    scale = float(width * zsize * n_dom * lax.axis_size("slab")) ** (-0.5)
    cells_g = jnp.moveaxis(neighbour_cells.reshape(nbrs, groups, 8, tile), 1, 0)
    weights_g = jnp.moveaxis(neighbour_weights.reshape(nbrs, groups, 8, tile), 1, 0)
    feats_g = jnp.moveaxis(point_features.reshape(half, groups, 8, tile), 1, 0)
    depth_ids = jnp.arange(zsize, dtype=jnp.int32)

    def group_step(carry, inputs):
        cell_g, weight_g, feat_g, group_id = inputs
        position = group_id * 8 * tile + jnp.arange(8 * tile, dtype=jnp.int32).reshape(8, tile)
        alive = (position < live).astype(jnp.float32)
        total = jnp.zeros((8, tile, zsize), jnp.float32)
        for kk in range(nbrs):
            total = total + jnp.where(
                cell_g[kk][:, :, None] == depth_ids, weight_g[kk][:, :, None], 0.0
            )
        blk = (total * alive[:, :, None]).astype(jnp.bfloat16)
        part = jnp.einsum("ctp,tpz->tcz", feat_g, blk, preferred_element_type=jnp.float32)
        return (carry, (blk, part))

    _, (blocks, contrib) = lax.scan(
        group_step, None, (cells_g, weights_g, feats_g, jnp.arange(groups, dtype=jnp.int32))
    )
    blocks = blocks.reshape(tiles, tile, zsize)
    contrib = contrib.reshape(tiles, half, zsize)
    owner = tile_target // width
    local_col = tile_target % width
    owner_hot = (owner[:, None] == jnp.arange(n_dom, dtype=jnp.int32)[None, :]).astype(jnp.int32)
    rank = jnp.sum((jnp.cumsum(owner_hot, 0) - 1) * owner_hot, 1)
    slot = owner * cap + rank
    send = jnp.zeros((n_dom * cap, half, zsize), jnp.float32).at[slot].set(contrib)
    send_col = jnp.zeros((n_dom * cap,), jnp.int32).at[slot].set(local_col)
    recv, recv_col = (
        lax.all_to_all(send, "dom", split_axis=0, concat_axis=0, tiled=True),
        lax.all_to_all(send_col, "dom", split_axis=0, concat_axis=0, tiled=True),
    )
    pooled_cols = jnp.zeros((width, half, zsize), jnp.float32).at[recv_col].add(recv)
    pooled = (
        pooled_cols.reshape(ysize, xsize, half, zsize).transpose(2, 1, 0, 3).astype(jnp.bfloat16)
    )
    cot = cotangent.astype(jnp.float32)
    first_o = lax.axis_index("chan") * half
    kernel_own = lax.dynamic_slice_in_dim(conv_kernel, first_o, half, 2)
    full_in = lax.all_gather(pooled, "chan", axis=0, tiled=True)
    rim = padded_2(full_in, (("dom", 2), ("slab", 1)), 1)
    h_sum = conv_forward(rim, kernel_own, 1)
    sig = jax.nn.sigmoid(h_sum)
    latent = (pooled.astype(jnp.float32) + h_sum * sig).astype(jnp.bfloat16)
    dh = (cot * sig * (1.0 + h_sum * (1.0 - sig))).astype(jnp.bfloat16)
    drim = padded_2(dh, (("dom", 2), ("slab", 1)), 1)
    dx_part = conv_backward(drim, kernel_own, 1)
    dx = lax.psum_scatter(
        dx_part.astype(jnp.bfloat16), "chan", scatter_dimension=0, tiled=True
    ).astype(jnp.float32)
    dpooled = (cot + dx).astype(jnp.bfloat16)
    kernel_part = kernel_product(rim, dh, 1)
    kernel_sum = lax.psum(kernel_part, ("dom", "slab"))
    kernel_grad = lax.all_gather(
        (kernel_sum * scale).astype(jnp.bfloat16), "chan", axis=2, tiled=True
    ).astype(jnp.float32)
    dcolumns = dpooled.transpose(2, 1, 0, 3).reshape(width, half, zsize)
    slot_grads = dcolumns[recv_col]
    returned = lax.all_to_all(slot_grads, "dom", split_axis=0, concat_axis=0, tiled=True)
    tile_grads = returned[slot]
    feature_grad = jnp.einsum(
        "tcz,tpz->ctp", tile_grads, blocks, preferred_element_type=jnp.float32
    )
    feature_grad = feature_grad.reshape(half, npts).astype(jnp.bfloat16)
    return (latent, feature_grad, kernel_grad)


def solution(mesh):
    placed = (
        P("chan", ("dom", "slab")),
        P(None, ("dom", "slab")),
        P(None, ("dom", "slab")),
        P(("dom", "slab")),
        P(("dom", "slab")),
        P(),
        P("chan", "slab", "dom", None),
    )
    return jax.shard_map(
        body,
        mesh=mesh,
        in_specs=placed,
        out_specs=(P("chan", "slab", "dom", None), P("chan", ("dom", "slab")), P()),
        check_vma=False,
    )
```

profile of v0, /device:TPU:6, one launch (start us, length us, event | category | flops | bytes accessed | tf_op | source)
XLA Modules:
  0.0 500.9 jit_solution(18227725382905394246)
XLA Ops:
  10.6 13.5 %all-to-all-start = ((s32[32,4,1]{1,2,0:T(1,128)}), s32[32,4,1]{1,2,0:T(1,128)S(1)}, u32[]{:S(2)}, u32[]{:S(2)}) async-start(s32[32,4,1]{1,2,0:T(1,128)} %bitcast), calls=%async_computation | async-start | bytes 32768 | tf_op jit(solution)/shard_map/all_to_all | solution.py:112
  24.1 1.2 copy.70
  25.2 1.0 copy.79
  26.2 1.0 copy.80
  27.3 72.9 %while.16 = (s32[]{:T(128)}, bf16[8,8,128,128]{3,2,1,0:T(8,128)(2,1)}, f32[8,8,32,128]{3,2,1,0:T(8,128)S(1)}, s32[8,8,8,128]{3,2,0,1:T(8,128)S(1)}, f32[8,8,8,12...) while((s32[]{:T(128)}, ...), condition=%wide.region_4.5_spmd.clone.clone, body=%wide.region_3.4_spmd.clone.clone.sunk | while | flops 14947331 | bytes 995989 | solution.py:98
  29.2 3.3 fusion.78
  32.6 3.8 fusion.79
  38.3 3.3 fusion.78
  41.6 3.8 fusion.79
  47.4 3.3 fusion.78
  50.8 3.8 fusion.79
  56.6 3.3 fusion.78
  59.9 3.8 fusion.79
  65.7 3.3 fusion.78
  69.0 3.8 fusion.79
  74.8 3.3 fusion.78
  78.1 3.8 fusion.79
  83.9 3.3 fusion.78
  87.2 3.8 fusion.79
  93.0 3.3 fusion.78
  96.3 3.8 fusion.79
  100.1 1.6 broadcast_in_dim.192
  101.7 8.1 %scatter_fusion = f32[128,32,128]{2,1,0:T(8,128)} fusion(f32[128,32,128]{2,1,0:T(8,128)} %broadcast_in_dim.192, s32[64]{0:T(128)S(1)} %compare_select_fusion.1, f32[64,32,128]{2,1,0:T(8,128)S(1)} %bitcast.158), kind=kCustom, calls=%fused_computation.3 | custom fusion | bytes 3145984 | tf_op jit(solution)/shard_map/scatter | solution.py:108
  109.8 9.8 %all-to-all-start.1 = ((f32[128,32,128]{2,1,0:T(8,128)}), f32[128,32,128]{2,1,0:T(8,128)S(1)}, u32[]{:S(2)}, u32[]{:S(2)}) async-start(f32[128,32,128]{2,1,0:T(8,128)} %scatter_fusion), calls=%async_computation.1 | async-start | bytes 4194304 | tf_op jit(solution)/shard_map/all_to_all | solution.py:111
  121.0 46.0 %all-to-all-done.1 = f32[128,32,128]{2,1,0:T(8,128)S(1)} async-done(((f32[128,32,128]{2,1,0:T(8,128)}), f32[128,32,128]{2,1,0:T(8,128)S(1)}, u32[]{:S(2)}, u32[]{:S(2)}) %all-to-all-start.1) | async-done | bytes 2097184 | tf_op jit(solution)/shard_map/all_to_all | solution.py:111
  167.1 5.9 %scatter_fusion.1 = f32[4,32,128]{2,1,0:T(8,128)S(1)} fusion(f32[4,32,128]{2,1,0:T(8,128)S(1)} %broadcast_in_dim.190, s32[128]{0:T(128)S(1)} %fusion.54, f32[128,32,128]{2,1,0:T(8,128)S(1)} %all-to-all-done.1), kind=kCustom, calls=%fused_computation.4 | custom fusion | flops 524288 | bytes 6291968 | tf_op jit(solution)/shard_map/scatter-add | solution.py:114
  173.0 1.9 all_gather.6
  174.9 3.7 collective-permute-start
  178.6 4.2 collective-permute-start.1
  182.9 1.5 collective-permute-done.1
  184.4 3.5 collective-permute-start.2
  187.9 1.3 collective-permute-start.3
  189.8 4.3 collective-permute-done.3
  195.9 3.7 collective-permute-start.4
  199.7 4.5 collective-permute-start.5
  204.2 1.4 collective-permute-done.5
  205.6 3.5 collective-permute-start.6
  209.1 1.3 collective-permute-start.7
  210.7 4.6 collective-permute-done.7
  217.8 14.9 %reduce-scatter.2.cloned.1.call-done = bf16[32,2,2,128]{3,0,1,2:T(8,128)(2,1)} async-done(((bf16[64,2,2,128]{3,0,1,2:T(8,128)(2,1)}), bf16[32,2,2,128]{3,0,1,2:T(8,128)(2,1)}) %reduce-scatter.2.cloned.1.call-update) | async-done | bytes 32784 | tf_op jit(solution)/shard_map/reduce_scatter | solution.py:129
  233.5 1.7 gather_fusion
  235.2 10.5 %all-to-all-start.2 = ((bf16[128,32,128]{2,1,0:T(8,128)(2,1)}), bf16[128,32,128]{2,1,0:T(8,128)(2,1)S(1)}, u32[]{:S(2)}, u32[]{:S(2)}) async-start(bf16[128,32,128]{2,1,0:T(8,128)(2,1)} %gather_fusion), calls=%async_computation.3 | async-start | bytes 2097152 | tf_op jit(solution)/shard_map/all_to_all | solution.py:140
  246.9 5.1 %fusion.67 = f32[3,3,3,64,32]{3,4,2,1,0:T(8,128)} fusion(bf16[64,1,4,4,128]{0,1,4,3,2:T(2,128)(2,1)S(1)} %copy.54, bf16[32,1,2,2,128]{0,1,4,3,2:T(2,128)(2,1)S(1)} %copy.55), kind=kOutput, calls=%fused_computation.141 | convolution fusion | flops 56328192 | bytes 516096 | tf_op jit(solution)/shard_map/transpose | solution.py:57
  252.7 232.1 %all-reduce.2.cloned.1.call-done = f32[27,64,32]{1,2,0:T(8,128)} async-done(((f32[27,64,32]{1,2,0:T(8,128)}), f32[27,64,32]{1,2,0:T(8,128)}) %all-reduce.2.cloned.1.call-update) | async-done | bytes 221200 | tf_op jit(solution)/shard_map/psum | solution.py:134
  484.8 1.1 multiply_convert_fusion.3
  485.9 2.1 all_gather.7
  488.0 1.1 copy.57
  489.8 2.8 fusion.26
  (124 shorter events, 23.6 us)
Async XLA Ops:
  8.0 181.2 %copy-start = (bf16[27,64,64]{2,1,0:T(8,128)(2,1)S(1)}, bf16[27,64,64]{2,1,0:T(8,128)(2,1)}, u32[]{:S(2)}) copy-start(bf16[27,64,64]{2,1,0:T(8,128)(2,1)} %param.14) | copy-start | bytes 663556
  10.6 99.3 %all-to-all-start = ((s32[32,4,1]{1,2,0:T(1,128)}), s32[32,4,1]{1,2,0:T(1,128)S(1)}, u32[]{:S(2)}, u32[]{:S(2)}) async-start(s32[32,4,1]{1,2,0:T(1,128)} %bitcast), calls=%async_computation | async-start | bytes 32768 | tf_op jit(solution)/shard_map/all_to_all | solution.py:112
  109.8 57.2 %all-to-all-start.1 = ((f32[128,32,128]{2,1,0:T(8,128)}), f32[128,32,128]{2,1,0:T(8,128)S(1)}, u32[]{:S(2)}, u32[]{:S(2)}) async-start(f32[128,32,128]{2,1,0:T(8,128)} %scatter_fusion), calls=%async_computation.1 | async-start | bytes 4194304 | tf_op jit(solution)/shard_map/all_to_all | solution.py:111
  119.6 113.1 %reduce-scatter.2.cloned.1.call-start = ((), (), s32[]{:S(2)}) async-start(), calls=%async_computation.4 | async-start | bytes 98304 | tf_op jit(solution)/shard_map/reduce_scatter | solution.py:129
  174.9 8.0 %collective-permute-start = (bf16[64,2,1,128]{3,0,1,2:T(8,128)(2,1)S(1)}, bf16[64,2,1,128]{3,0,1,2:T(8,128)(2,1)S(1)}, u32[]{:S(2)}, u32[]{:S(2)}) collective-permute-start(bf16[64,2,1,128]{3,0,1,2:T(8,128)(2,1)S(1)} %get-tuple-element.284), channel_id=1, source_target_pairs={{0,16},{16,32},{32,48},{48,64},{64,80},{80,96},{96,112},{112,128},... | collective-permute-start | bytes 98312 | tf_op jit(solution)/shard_map/ppermute | solution.py:14
  178.6 5.8 %collective-permute-start.1 = (bf16[64,2,1,128]{3,0,1,2:T(8,128)(2,1)S(1)}, bf16[64,2,1,128]{3,0,1,2:T(8,128)(2,1)S(1)}, u32[]{:S(2)}, u32[]{:S(2)}) collective-permute-start(bf16[64,2,1,128]{3,0,1,2:T(8,128)(2,1)S(1)} %get-tuple-element.283), channel_id=1, source_target_pairs={{16,0},{32,16},{48,32},{64,48},{80,64},{96,80},{112,96},{128,112},... | collective-permute-start | bytes 98312 | tf_op jit(solution)/shard_map/ppermute | solution.py:15
  184.4 5.4 %collective-permute-start.2 = (bf16[64,1,4,128]{3,0,1,2:T(8,128)(2,1)S(1)}, bf16[64,1,4,128]{3,0,1,2:T(8,128)(2,1)S(1)}, u32[]{:S(2)}, u32[]{:S(2)}) collective-permute-start(bf16[64,1,4,128]{3,0,1,2:T(8,128)(2,1)S(1)} %get-tuple-element.277), channel_id=1, source_target_pairs={{0,2},{2,4},{4,6},{6,8},{8,10},{10,12},{12,14},{1,3},{3,5},{5,7},{... | collective-permute-start | bytes 196616 | tf_op jit(solution)/shard_map/ppermute | solution.py:14
  187.9 6.2 %collective-permute-start.3 = (bf16[64,1,4,128]{3,0,1,2:T(8,128)(2,1)S(1)}, bf16[64,1,4,128]{3,0,1,2:T(8,128)(2,1)S(1)}, u32[]{:S(2)}, u32[]{:S(2)}) collective-permute-start(bf16[64,1,4,128]{3,0,1,2:T(8,128)(2,1)S(1)} %get-tuple-element.278), channel_id=1, source_target_pairs={{2,0},{4,2},{6,4},{8,6},{10,8},{12,10},{14,12},{3,1},{5,3},{7,5},{... | collective-permute-start | bytes 196616 | tf_op jit(solution)/shard_map/ppermute | solution.py:15
  189.4 5.4 %copy-start.2 = (pred[8,17]{0,1:T(8,128)(4,1)S(1)}, pred[8,17]{0,1:T(8,128)(4,1)}, u32[]{:S(2)}) copy-start(pred[8,17]{0,1:T(8,128)(4,1)} %constant.113) | copy-start | bytes 412
  194.8 1.0 copy-start.1
  195.9 8.3 %collective-permute-start.4 = (bf16[32,2,1,128]{3,0,1,2:T(8,128)(2,1)S(1)}, bf16[32,2,1,128]{3,0,1,2:T(8,128)(2,1)S(1)}, u32[]{:S(2)}, u32[]{:S(2)}) collective-permute-start(bf16[32,2,1,128]{3,0,1,2:T(8,128)(2,1)S(1)} %get-tuple-element.285), channel_id=1, source_target_pairs={{0,16},{16,32},{32,48},{48,64},{64,80},{80,96},{96,112},{112,128},... | collective-permute-start | bytes 49160 | tf_op jit(solution)/shard_map/ppermute | solution.py:14
  199.7 6.0 %collective-permute-start.5 = (bf16[32,2,1,128]{3,0,1,2:T(8,128)(2,1)S(1)}, bf16[32,2,1,128]{3,0,1,2:T(8,128)(2,1)S(1)}, u32[]{:S(2)}, u32[]{:S(2)}) collective-permute-start(bf16[32,2,1,128]{3,0,1,2:T(8,128)(2,1)S(1)} %get-tuple-element.286), channel_id=1, source_target_pairs={{16,0},{32,16},{48,32},{64,48},{80,64},{96,80},{112,96},{128,112},... | collective-permute-start | bytes 49160 | tf_op jit(solution)/shard_map/ppermute | solution.py:15
  205.6 5.1 %collective-permute-start.6 = (bf16[32,1,4,128]{3,0,1,2:T(8,128)(2,1)S(1)}, bf16[32,1,4,128]{3,0,1,2:T(8,128)(2,1)S(1)}, u32[]{:S(2)}, u32[]{:S(2)}) collective-permute-start(bf16[32,1,4,128]{3,0,1,2:T(8,128)(2,1)S(1)} %get-tuple-element.279), channel_id=1, source_target_pairs={{0,2},{2,4},{4,6},{6,8},{8,10},{10,12},{12,14},{1,3},{3,5},{5,7},{... | collective-permute-start | bytes 98312 | tf_op jit(solution)/shard_map/ppermute | solution.py:14
  209.1 6.1 %collective-permute-start.7 = (bf16[32,1,4,128]{3,0,1,2:T(8,128)(2,1)S(1)}, bf16[32,1,4,128]{3,0,1,2:T(8,128)(2,1)S(1)}, u32[]{:S(2)}, u32[]{:S(2)}) collective-permute-start(bf16[32,1,4,128]{3,0,1,2:T(8,128)(2,1)S(1)} %get-tuple-element.280), channel_id=1, source_target_pairs={{2,0},{4,2},{6,4},{8,6},{10,8},{12,10},{14,12},{3,1},{5,3},{7,5},{... | collective-permute-start | bytes 98312 | tf_op jit(solution)/shard_map/ppermute | solution.py:15
  235.2 253.9 %all-to-all-start.2 = ((bf16[128,32,128]{2,1,0:T(8,128)(2,1)}), bf16[128,32,128]{2,1,0:T(8,128)(2,1)S(1)}, u32[]{:S(2)}, u32[]{:S(2)}) async-start(bf16[128,32,128]{2,1,0:T(8,128)(2,1)} %gather_fusion), calls=%async_computation.3 | async-start | bytes 2097152 | tf_op jit(solution)/shard_map/all_to_all | solution.py:140
  245.7 239.1 %all-reduce.2.cloned.1.call-start = ((), (), s32[]{:S(2)}) async-start(), calls=%async_computation.5 | async-start | bytes 884736 | tf_op jit(solution)/shard_map/psum | solution.py:134
Sparse Core Ops, SparseCore 0:
  217.9 14.7 reduce-scatter.1
Sparse Core Ops, SparseCore 1:
  252.1 232.6 all-reduce.1
where the time goes:
time: 505 us; the launch traced here: 501 us
  waiting for transfers between devices  306 us (61%)
  starting transfers between devices  59.8 us (12%)
  other arithmetic  41.2 us (8%)
  matrix products  40.1 us (8%)
  local copies, waits for them, and re-layouts  28.9 us (6%)
  between operations  15.9 us (3%)
  loops' own time  5.49 us (1%)
    psum x1, waiting for transfers between devices, body(): kernel_sum = lax.psum(kernel_part, ('dom', 'slab'))  232 us
    all_to_all x1, waiting for transfers between devices, body(): lax.all_to_all(send, 'dom', split_axis=0, concat_axis=0, tiled=True)  46 us
    dot_general x8, matrix products, group_step(): jnp.einsum('ctp,tpz->tcz', feat_g, blk, preferred_element_type=jnp.float32)  30.7 us
    dynamic_update_slice x8, other arithmetic, body(): lax.scan(group_step, None, (cells_g, weights_g, feats_g, jnp.arange(group...  26.3 us
    reduce_scatter x1, waiting for transfers between devices, body(): lax.psum_scatter(dx_part.astype(jnp.bfloat16), 'chan', scatter_dimension=...  14.9 us
    ppermute x4, starting transfers between devices, padded_2(): before = lax.ppermute(last, axis, up)  14.4 us
    all_to_all x1, starting transfers between devices, body(): lax.all_to_all(send_col, 'dom', split_axis=0, concat_axis=0, tiled=True)  13.5 us
    ppermute x4, waiting for transfers between devices, padded_2(): after = lax.ppermute(first, axis, down)  11.8 us
  transfers between devices with their start and end apart: 13, of which 9 were waited for; matrix products, arithmetic and copies ran while one was open for 18% of the time, Pallas kernels for 0%

commit v1 on v0

v1 whole, which is shorter than its diff:
```python
import functools

import jax
import jax.numpy as jnp
from jax import lax
from jax.experimental import pallas as pl
from jax.experimental.pallas import tpu as pltpu
from jax.sharding import PartitionSpec as P

GROUP = 8
VMEM_LIMIT = 48 * 1024 * 1024


def pool_kernel(target, live, cells, weights, feats, blocks, send, acc):
    step = pl.program_id(0)
    tile = blocks.shape[2]
    depth = blocks.shape[1]

    @pl.when(step == 0)
    def _():
        acc[...] = jnp.zeros_like(acc)

    span = cells.shape[1]
    position = step * span + lax.broadcasted_iota(jnp.int32, cells.shape, 1)
    masked = jnp.where(position < live[0], weights[...], 0.0)
    cell = cells[...]
    depth_ids = lax.broadcasted_iota(jnp.int32, (depth, tile), 0)
    for t in range(span // tile):
        cols = slice(t * tile, (t + 1) * tile)
        total = jnp.zeros((depth, tile), jnp.float32)
        for k in range(cells.shape[0]):
            total = total + jnp.where(
                cell[k : k + 1, cols] == depth_ids, masked[k : k + 1, cols], 0.0
            )
        block = total.astype(jnp.bfloat16)
        blocks[t] = block
        part = lax.dot_general(
            feats[:, cols], block, (((1,), (1,)), ((), ())), preferred_element_type=jnp.float32
        )
        column = target[step * (span // tile) + t]
        acc[column] = acc[column] + part

    @pl.when(step == pl.num_programs(0) - 1)
    def _():
        send[...] = acc[...].astype(jnp.bfloat16)


def pool(target, live, cells, weights, feats, n_columns, depth):
    nbrs, npts = cells.shape
    half = feats.shape[0]
    tiles = target.shape[0]
    tile = npts // tiles
    group = min(GROUP, tiles)
    span = group * tile
    smem = pl.BlockSpec(memory_space=pltpu.SMEM)
    return pl.pallas_call(
        pool_kernel,
        grid=(tiles // group,),
        in_specs=[
            smem,
            smem,
            pl.BlockSpec((nbrs, span), lambda i: (0, i)),
            pl.BlockSpec((nbrs, span), lambda i: (0, i)),
            pl.BlockSpec((half, span), lambda i: (0, i)),
        ],
        out_specs=[
            pl.BlockSpec((group, depth, tile), lambda i: (i, 0, 0)),
            pl.BlockSpec((n_columns, half, depth), lambda i: (0, 0, 0)),
        ],
        out_shape=[
            jax.ShapeDtypeStruct((tiles, depth, tile), jnp.bfloat16),
            jax.ShapeDtypeStruct((n_columns, half, depth), jnp.bfloat16),
        ],
        scratch_shapes=[pltpu.VMEM((n_columns, half, depth), jnp.float32)],
        compiler_params=pltpu.CompilerParams(vmem_limit_bytes=VMEM_LIMIT),
        name="pool",
    )(target, live, cells, weights, feats)


def spread_kernel(target, columns, blocks, out):
    step = pl.program_id(0)
    group, _, tile = blocks.shape
    for t in range(group):
        column = target[step * group + t]
        part = jnp.dot(columns[column], blocks[t], preferred_element_type=jnp.float32)
        out[:, t * tile : (t + 1) * tile] = part.astype(jnp.bfloat16)


def spread(target, columns, blocks):
    tiles, depth, tile = blocks.shape
    n_columns, half, _ = columns.shape
    group = min(GROUP, tiles)
    return pl.pallas_call(
        spread_kernel,
        grid=(tiles // group,),
        in_specs=[
            pl.BlockSpec(memory_space=pltpu.SMEM),
            pl.BlockSpec((n_columns, half, depth), lambda i: (0, 0, 0)),
            pl.BlockSpec((group, depth, tile), lambda i: (i, 0, 0)),
        ],
        out_specs=pl.BlockSpec((half, group * tile), lambda i: (0, i)),
        out_shape=jax.ShapeDtypeStruct((half, tiles * tile), jnp.bfloat16),
        compiler_params=pltpu.CompilerParams(vmem_limit_bytes=VMEM_LIMIT),
        name="spread",
    )(target, columns, blocks)


def later(value, lane):
    return jnp.where(lane == 0, 0.0, pltpu.roll(value, 1, 1))


def earlier(value, lane):
    depth = value.shape[1]
    return jnp.where(lane == depth - 1, 0.0, pltpu.roll(value, depth - 1, 1))


def conv_kernel_body(chan, pooled, cot, wf, wb, latent, dpooled, kgrad, pp, dd, hh):
    half, depth = pooled.shape[4], pooled.shape[5]
    full = 2 * half
    first = pl.multiple_of(chan[0] * half, half)
    for s in range(3):
        for y in range(6):
            for x in range(2):
                for c in range(2):
                    pp[2 * s + x, y * full + c * half : y * full + (c + 1) * half, :] = pooled[
                        c, s, y, x
                    ]
    lane = lax.broadcasted_iota(jnp.int32, (full, depth), 1)
    for x in range(4):
        for y in range(4):
            grown = jnp.zeros((3 * full, depth), jnp.float32)
            for a in range(3):
                grown = grown + jnp.dot(
                    wf[a],
                    pp[x + a, y * full : (y + 3) * full, :],
                    preferred_element_type=jnp.float32,
                )
            h = (
                grown[full : 2 * full]
                + later(grown[:full], lane)
                + earlier(grown[2 * full :], lane)
            )
            sig = jax.nn.sigmoid(h)
            upper = jnp.concatenate([cot[0, y, x], cot[1, y, x]], 0).astype(jnp.float32)
            dd[x, y * full : (y + 1) * full, :] = (upper * sig * (1.0 + h * (1.0 - sig))).astype(
                jnp.bfloat16
            )
            if x in (1, 2) and y in (1, 2):
                hh[...] = h * sig
                mine = pp[x + 1, pl.ds((y + 1) * full + first, half), :].astype(jnp.float32)
                latent[:, x - 1, y - 1, :] = (mine + hh[pl.ds(first, half), :]).astype(jnp.bfloat16)
    lane = lax.broadcasted_iota(jnp.int32, (half, depth), 1)
    for x in range(2):
        for y in range(2):
            grown = jnp.zeros((3 * half, depth), jnp.float32)
            for a in range(3):
                grown = grown + jnp.dot(
                    wb[a],
                    dd[x + a, y * full : (y + 3) * full, :],
                    preferred_element_type=jnp.float32,
                )
            dx = (
                grown[half : 2 * half]
                + earlier(grown[:half], lane)
                + later(grown[2 * half :], lane)
            )
            own = cot[chan[0], y + 1, x + 1].astype(jnp.float32)
            dpooled[y, x] = (own + dx).astype(jnp.bfloat16)
    moved = []
    for x in range(2):
        for y in range(2):
            own = dd[x + 1, pl.ds((y + 1) * full + first, half), :].astype(jnp.float32)
            moved.append(
                jnp.concatenate(
                    [earlier(own, lane), own, later(own, lane), jnp.zeros_like(own)], 0
                ).astype(jnp.bfloat16)
            )
    for a in range(3):
        total = jnp.zeros((3 * full, 4 * half), jnp.float32)
        for x in range(2):
            for y in range(2):
                total = total + lax.dot_general(
                    pp[x + 1 + a, (y + 1) * full : (y + 4) * full, :],
                    moved[2 * x + y],
                    (((1,), (1,)), ((), ())),
                    preferred_element_type=jnp.float32,
                )
        kgrad[a * 3 * full : (a + 1) * 3 * full, :] = total.astype(jnp.bfloat16)
    rest = kgrad.shape[0] - 9 * full
    if rest:
        kgrad[9 * full :, :] = jnp.zeros((rest, 4 * half), jnp.bfloat16)


def conv_layer(chan, pooled, cot, wf, wb, rows):
    half, depth = pooled.shape[4], pooled.shape[5]
    full = 2 * half
    vmem = pl.BlockSpec(memory_space=pltpu.VMEM)
    return pl.pallas_call(
        conv_kernel_body,
        in_specs=[pl.BlockSpec(memory_space=pltpu.SMEM), vmem, vmem, vmem, vmem],
        out_specs=[vmem, vmem, vmem],
        out_shape=[
            jax.ShapeDtypeStruct((half, 2, 2, depth), jnp.bfloat16),
            jax.ShapeDtypeStruct((2, 2, half, depth), jnp.bfloat16),
            jax.ShapeDtypeStruct((rows, 4 * half), jnp.bfloat16),
        ],
        scratch_shapes=[
            pltpu.VMEM((6, 6 * full, depth), jnp.bfloat16),
            pltpu.VMEM((4, 4 * full, depth), jnp.bfloat16),
            pltpu.VMEM((full, depth), jnp.float32),
        ],
        compiler_params=pltpu.CompilerParams(vmem_limit_bytes=VMEM_LIMIT),
        name="conv_layer",
    )(chan, pooled, cot, wf, wb)


def neighbours(first, last, axis):
    peers = lax.axis_size(axis)
    up = [(i, i + 1) for i in range(peers - 1)]
    down = [(j, i) for i, j in up]
    return lax.ppermute(last, axis, up), lax.ppermute(first, axis, down)


def body(
    point_features,
    neighbour_cells,
    neighbour_weights,
    live_points,
    tile_target,
    conv_kernel,
    cotangent,
):
    half = point_features.shape[0]
    full = 2 * half
    xsize, ysize, depth = cotangent.shape[1:]
    n_dom, n_slab = lax.axis_size("dom"), lax.axis_size("slab")
    devices = n_dom * n_slab
    width = xsize * ysize
    chan = lax.axis_index("chan").astype(jnp.int32)
    scale = float(width * depth * devices) ** (-0.5)

    blocks, send = pool(
        tile_target,
        live_points,
        neighbour_cells,
        neighbour_weights,
        point_features,
        n_dom * width,
        depth,
    )

    cot = cotangent.transpose(2, 1, 0, 3)
    before, after = neighbours(cot[:1], cot[-1:], "dom")
    cot = jnp.concatenate([before, cot, after], 0)
    before, after = neighbours(cot[:, :1], cot[:, -1:], "slab")
    cot = jnp.concatenate([before, cot, after], 1)
    cot = lax.all_gather(cot, "chan", axis=0, tiled=False)

    kernel = conv_kernel.reshape(3, 3, 3, full, full)
    wf = kernel.transpose(0, 2, 4, 1, 3).reshape(3, 3 * full, 3 * full)
    wb = lax.dynamic_slice_in_dim(kernel[::-1, ::-1], chan * half, half, 3)
    wb = wb.transpose(0, 2, 3, 1, 4).reshape(3, 3 * half, 3 * full)

    recv = lax.all_to_all(send, "dom", split_axis=0, concat_axis=0, tiled=True)
    pooled = recv.reshape(n_dom, ysize, xsize, half, depth).astype(jnp.float32).sum(0)
    pooled = pooled.astype(jnp.bfloat16)
    before, after = neighbours(pooled, pooled, "dom")
    pooled = jnp.concatenate([before, pooled, after], 0)
    before, after = neighbours(pooled, pooled, "slab")
    pooled = jnp.stack([before, pooled, after], 0)
    pooled = lax.all_gather(pooled, "chan", axis=0, tiled=False)

    per = -(-9 * full // (4 * devices)) * 4
    latent, dpooled, kgrad = conv_layer(chan[None], pooled, cot, wf, wb, per * devices)

    columns = jnp.broadcast_to(dpooled.reshape(1, width, half, depth), (n_dom, width, half, depth))
    columns = lax.all_to_all(
        columns.reshape(n_dom * width, half, depth), "dom", split_axis=0, concat_axis=0, tiled=True
    )
    feature_grad = spread(tile_target, columns, blocks)

    kgrad = lax.all_to_all(
        kgrad.reshape(devices, per, 4 * half), ("dom", "slab"), split_axis=0, concat_axis=0, tiled=True
    )
    kgrad = (kgrad.astype(jnp.float32).sum(0) * scale).astype(jnp.bfloat16)
    kgrad = jnp.broadcast_to(kgrad[None], (2 * devices, per, 4 * half))
    kgrad = lax.all_to_all(kgrad, ("dom", "slab", "chan"), split_axis=0, concat_axis=0, tiled=True)
    kgrad = kgrad.reshape(devices, 2, per, 4 * half).transpose(0, 2, 1, 3)
    kgrad = kgrad.reshape(devices * per, 2, 4 * half)[: 9 * full, :, : 3 * half]
    kgrad = kgrad.reshape(9, full, 2, 3, half).transpose(0, 3, 1, 2, 4)
    kernel_grad = kgrad.reshape(27, full, full).astype(jnp.float32)
    return (latent, feature_grad, kernel_grad)


def solution(mesh):
    placed = (
        P("chan", ("dom", "slab")),
        P(None, ("dom", "slab")),
        P(None, ("dom", "slab")),
        P(("dom", "slab")),
        P(("dom", "slab")),
        P(),
        P("chan", "slab", "dom", None),
    )
    return jax.shard_map(
        body,
        mesh=mesh,
        in_specs=placed,
        out_specs=(P("chan", "slab", "dom", None), P("chan", ("dom", "slab")), P()),
        check_vma=False,
    )
```

time: 505 us -> 185 us (0.37)
  waiting for transfers between devices: 306 us -> 34.5 us
  blocking collectives: 3.98 us -> 66.3 us
  matrix products: 40.1 us -> 0 us
  other arithmetic: 41.2 us -> 1.76 us
  between operations: 15.9 us -> 1.54 us
  starting transfers between devices: 59.8 us -> 46.9 us
  Pallas kernels: 0 us -> 12.6 us
  local copies, waits for them, and re-layouts: 28.9 us -> 19.2 us
  loops' own time: 5.49 us -> 0 us
    psum x1 -> x0, waiting for transfers between devices: 232 us -> none  [body(): kernel_sum = lax.psum(kernel_part, ('dom', 'slab'))]
    all_to_all x0 -> x2, blocking collectives: none -> 62.1 us  [the longest x1 31.8 us: body(): lax.all_to_all(kgrad, ('dom', 'slab', 'chan'), split_axis=0, concat_axis=...]
    dot_general x9 -> x0, matrix products: 33.5 us -> none  [the longest x8 30.7 us: group_step(): jnp.einsum('ctp,tpz->tcz', feat_g, blk, preferred_element_type=jnp.float32)]
    all_to_all x3 -> x2, waiting for transfers between devices: 46.1 us -> 18.2 us  [the longest x1 17.1 us: body(): lax.all_to_all(columns.reshape(n_dom * width, half, depth), 'dom', split_...]
    dynamic_update_slice x8 -> x0, other arithmetic: 26.3 us -> none  [body(): lax.scan(group_step, None, (cells_g, weights_g, feats_g, jnp.arange(group...]
    reduce_scatter x1 -> x0, waiting for transfers between devices: 14.9 us -> none  [body(): lax.psum_scatter(dx_part.astype(jnp.bfloat16), 'chan', scatter_dimension=...]
    all_to_all x3 -> x2, starting transfers between devices: 33.8 us -> 20.4 us  [the longest x1 13.5 us: body(): recv = lax.all_to_all(send, 'dom', split_axis=0, concat_axis=0, tiled=True)]
    pallas_call x0 -> x3, Pallas kernels: none -> 12.6 us  [the longest x1 6.53 us: pool(): pl.pallas_call(pool_kernel, grid=(tiles // group,), in_specs=[smem, smem,...]
  transfers between devices with their start and end apart: 13 -> 10, of which waited for: 9 -> 4; matrix products, arithmetic and copies ran while one was open for 18% -> 8% of each run, Pallas kernels for 0% -> 0%
where the time goes in v1:
time: 185 us; the launch traced here: 183 us
  blocking collectives  66.3 us (36%)
  starting transfers between devices  46.9 us (25%)
  waiting for transfers between devices  34.5 us (19%)
  local copies, waits for them, and re-layouts  19.2 us (10%)
  Pallas kernels  12.6 us (7%)
    all_to_all x1, blocking collectives, body(): lax.all_to_all(kgrad, ('dom', 'slab', 'chan'), split_axis=0, concat_axis=...  31.8 us
    all_to_all x1, blocking collectives, body(): lax.all_to_all(kgrad.reshape(devices, per, 4 * half), ('dom', 'slab'), sp...  30.4 us
    ppermute x8, starting transfers between devices, neighbours(): return (lax.ppermute(last, axis, up), lax.ppermute(first, axis, down))  26.5 us
    all_to_all x1, waiting for transfers between devices, body(): lax.all_to_all(columns.reshape(n_dom * width, half, depth), 'dom', split_...  17.1 us
    ppermute x8, waiting for transfers between devices, neighbours(): return (lax.ppermute(last, axis, up), lax.ppermute(first, axis, down))  16.3 us
    all_to_all x1, starting transfers between devices, body(): recv = lax.all_to_all(send, 'dom', split_axis=0, concat_axis=0, tiled=True)  13.5 us
    all_to_all x1, starting transfers between devices, body(): lax.all_to_all(columns.reshape(n_dom * width, half, depth), 'dom', split_...  6.9 us
    unnamed x17, local copies, waits for them, and re-layouts  6.85 us
  transfers between devices with their start and end apart: 10, of which 4 were waited for; matrix products, arithmetic and copies ran while one was open for 8% of the time, Pallas kernels for 0%

profile of v1, /device:TPU:6, one launch (start us, length us, event | category | flops | bytes accessed | tf_op | source)
XLA Modules:
  0.0 182.9 jit_solution(17234186866617090290)
XLA Ops:
  1.3 1.0 copy-done
  2.3 0.9 copy-done.1
  3.3 0.9 copy-done.2
  4.2 0.7 copy-done.3
  4.9 6.5 %pool.1 = (bf16[64,128,128]{2,1,0:T(8,128)(2,1)S(1)}, bf16[128,32,128]{2,1,0:T(8,128)(2,1)}) custom-call(s32[64]{0:T(128)S(1)} %copy-done.3, s32[1]{0:T(128)S(6)} %copy.45.live, s32[8,8192]{1,0:T(8,128)S(1)} %copy-done.1, f32[8,8192]{1,0:T(8,128)S(1)} %copy-done.2, bf16[32,8192]{1,0:T(8,128)(2,1)S(1)} %copy-done), custom_call_target="tpu_custom_call" | custom-call | tf_op jit(solution)/shard_map/pool/pallas_call | solution.py:56
  11.4 13.5 %all-to-all-start = ((bf16[128,32,128]{2,1,0:T(8,128)(2,1)}), bf16[128,32,128]{2,1,0:T(8,128)(2,1)}, u32[]{:S(2)}, u32[]{:S(2)}) async-start(bf16[128,32,128]{2,1,0:T(8,128)(2,1)} %get-tuple-element.8), calls=%async_computation | async-start | bytes 2097152 | tf_op jit(solution)/shard_map/all_to_all | solution.py:264
  25.0 3.4 %collective-permute-start.4 = (bf16[1,2,32,128]{3,2,1,0:T(8,128)(2,1)S(1)}, bf16[1,2,32,128]{3,2,1,0:T(8,128)(2,1)S(1)}, u32[]{:S(2)}, u32[]{:S(2)}) collective-permute-start(bf16[1,2,32,128]{3,2,1,0:T(8,128)(2,1)S(1)} %get-tuple-element.29), channel_id=1, source_target_pairs={{0,16},{16,32},{32,48},{48,64},{64,80},{80,96},{96,112},{112,128},... | collective-permute-start | bytes 49160 | tf_op jit(solution)/shard_map/ppermute | solution.py:221
  28.4 4.6 %collective-permute-start.5 = (bf16[1,2,32,128]{3,2,1,0:T(8,128)(2,1)S(1)}, bf16[1,2,32,128]{3,2,1,0:T(8,128)(2,1)S(1)}, u32[]{:S(2)}, u32[]{:S(2)}) collective-permute-start(bf16[1,2,32,128]{3,2,1,0:T(8,128)(2,1)S(1)} %get-tuple-element.30), channel_id=1, source_target_pairs={{16,0},{32,16},{48,32},{64,48},{80,64},{96,80},{112,96},{128,112},... | collective-permute-start | bytes 49160 | tf_op jit(solution)/shard_map/ppermute | solution.py:221
  32.9 0.4 copy.36
  33.3 1.6 rev.3
  35.0 0.1 dynamic-slice_bitcast_fusion
  35.1 1.7 copy.35
  36.8 0.2 reshape.45.wb
  37.0 0.4 reshape.44.wf
  37.4 13.1 %collective-permute-done.4 = bf16[1,2,32,128]{3,2,1,0:T(8,128)(2,1)S(1)} collective-permute-done((bf16[1,2,32,128]{3,2,1,0:T(8,128)(2,1)S(1)}, bf16[1,2,32,128]{3,2,1,0:T(8,128)(2,1)S(1)}, u32[]{:S(2)}, u32[]{:S(2)}) %collective-permute-start.4) | collective-permute-done | bytes 16416 | tf_op jit(solution)/shard_map/ppermute | solution.py:221
  50.5 0.0 collective-permute-done.5
  50.5 1.1 all-to-all-done
  51.7 1.4 reduce_sum.21
  53.1 4.0 %collective-permute-start = (bf16[2,2,32,128]{3,2,1,0:T(8,128)(2,1)S(1)}, bf16[2,2,32,128]{3,2,1,0:T(8,128)(2,1)S(1)}, u32[]{:S(2)}, u32[]{:S(2)}) collective-permute-start(bf16[2,2,32,128]{3,2,1,0:T(8,128)(2,1)S(1)} %reduce_sum.21), channel_id=1, source_target_pairs={{0,16},{16,32},{32,48},{48,64},{64,80},{80,96},{96,112},{112,128},... | collective-permute-start | bytes 98312 | tf_op jit(solution)/shard_map/ppermute | solution.py:221
  57.0 4.0 %collective-permute-start.1 = (bf16[2,2,32,128]{3,2,1,0:T(8,128)(2,1)S(1)}, bf16[2,2,32,128]{3,2,1,0:T(8,128)(2,1)S(1)}, u32[]{:S(2)}, u32[]{:S(2)}) collective-permute-start(bf16[2,2,32,128]{3,2,1,0:T(8,128)(2,1)S(1)} %reduce_sum.21), channel_id=1, source_target_pairs={{16,0},{32,16},{48,32},{64,48},{80,64},{96,80},{112,96},{128,112},... | collective-permute-start | bytes 98312 | tf_op jit(solution)/shard_map/ppermute | solution.py:221
  61.0 3.5 %collective-permute-start.6 = (bf16[4,1,32,128]{3,2,1,0:T(8,128)(2,1)S(1)}, bf16[4,1,32,128]{3,2,1,0:T(8,128)(2,1)S(1)}, u32[]{:S(2)}, u32[]{:S(2)}) collective-permute-start(bf16[4,1,32,128]{3,2,1,0:T(8,128)(2,1)S(1)} %get-tuple-element.27), channel_id=1, source_target_pairs={{0,2},{2,4},{4,6},{6,8},{8,10},{10,12},{12,14},{1,3},{3,5},{5,7},{... | collective-permute-start | bytes 98312 | tf_op jit(solution)/shard_map/ppermute | solution.py:221
  64.5 1.3 collective-permute-start.7
  65.8 0.0 collective-permute-done
  65.8 0.0 collective-permute-done.1
  65.9 4.6 %collective-permute-start.2 = (bf16[6,2,32,128]{3,2,1,0:T(8,128)(2,1)S(1)}, bf16[6,2,32,128]{3,2,1,0:T(8,128)(2,1)S(1)}, u32[]{:S(2)}, u32[]{:S(2)}) collective-permute-start(bf16[6,2,32,128]{3,2,1,0:T(8,128)(2,1)S(1)} %get-tuple-element.26), channel_id=1, source_target_pairs={{0,2},{2,4},{4,6},{6,8},{8,10},{10,12},{12,14},{1,3},{3,5},{5,7},{... | collective-permute-start | bytes 294920 | tf_op jit(solution)/shard_map/ppermute | solution.py:221
  70.4 1.3 collective-permute-start.3
  71.7 0.0 collective-permute-done.6
  71.7 0.0 collective-permute-done.7
  71.8 2.0 %all-gather.1 = bf16[8,4,32,128]{3,2,1,0:T(8,128)(2,1)S(1)} all-gather(bf16[4,4,32,128]{3,2,1,0:T(8,128)(2,1)S(1)} %pad_maximum_fusion.1), channel_id=3, replica_groups=mesh['dom'=32,'slab'=8,'chan'=2] {'chan'}, dimensions={0}, use_global_device_ids=true | all-gather | bytes 393216 | tf_op jit(solution)/shard_map/all_gather | solution.py:257
  73.8 0.0 collective-permute-done.2
  73.8 3.2 %collective-permute-done.3 = bf16[6,2,32,128]{3,2,1,0:T(8,128)(2,1)S(1)} collective-permute-done((bf16[6,2,32,128]{3,2,1,0:T(8,128)(2,1)S(1)}, bf16[6,2,32,128]{3,2,1,0:T(8,128)(2,1)S(1)}, u32[]{:S(2)}, u32[]{:S(2)}) %collective-permute-start.3) | collective-permute-done | bytes 98336 | tf_op jit(solution)/shard_map/ppermute | solution.py:221
  77.0 2.2 %all-gather = bf16[6,6,2,32,128]{4,3,2,1,0:T(8,128)(2,1)S(1)} all-gather(bf16[3,6,2,32,128]{4,3,2,1,0:T(8,128)(2,1)S(1)} %pad_maximum_fusion), channel_id=2, replica_groups=mesh['dom'=32,'slab'=8,'chan'=2] {'chan'}, dimensions={0}, use_global_device_ids=true | all-gather | bytes 884736 | tf_op jit(solution)/shard_map/all_gather | solution.py:271
  79.2 2.0 %conv_layer.1 = (bf16[32,2,2,128]{3,2,1,0:T(2,128)(2,1)}, bf16[2,2,32,128]{3,2,1,0:T(8,128)(2,1)S(1)}, bf16[1024,128]{1,0:T(8,128)(2,1)S(1)}) custom-call(s32[1]{0:T(128)} %bitcast.chan, bf16[2,3,6,2,32,128]{5,4,3,2,1,0:T(8,128)(2,1)S(1)} %bitcast.26, bf16[2,4,4,32,128]{4,3,2,1,0:T(8,128)(2,1)S(1)} %bitcast.27, bf16[3,192,192]{2,1,0:T(8,128)(2,1)S(1)} %reshape.44.wf, ...), custom_call_target="tpu_custom_call" | custom-call | tf_op jit(solution)/shard_map/conv_layer/pallas_call | solution.py:198
  81.2 30.4 %all_to_all.20 = bf16[256,4,128]{2,1,0:T(4,128)(2,1)S(1)} all-to-all(bf16[256,4,128]{2,1,0:T(4,128)(2,1)S(1)} %bitcast.28), channel_id=1, replica_groups=mesh['dom'=32,'slab'=8,'chan'=2] {'dom','slab'}, dimensions={0} | all-to-all | bytes 524288 | tf_op jit(solution)/shard_map/all_to_all | solution.py:282
  111.6 0.3 convert_reduce_fusion
  111.9 0.1 broadcast_in_dim.19
  112.0 31.8 %all_to_all.21 = bf16[512,4,128]{2,1,0:T(4,128)(2,1)} all-to-all(bf16[512,4,128]{2,1,0:T(4,128)(2,1)S(1)} %broadcast_in_dim.19), channel_id=1, replica_groups=mesh['dom'=32,'slab'=8,'chan'=2] {'dom','slab','chan'}, dimensions={0} | all-to-all | bytes 1048576 | tf_op jit(solution)/shard_map/all_to_all | solution.py:287
  143.8 1.2 broadcast_in_dim.18
  145.0 6.9 %all-to-all-start.1 = ((bf16[128,32,128]{2,1,0:T(8,128)(2,1)}), bf16[128,32,128]{2,1,0:T(8,128)(2,1)S(1)}, u32[]{:S(2)}, u32[]{:S(2)}) async-start(bf16[128,32,128]{2,1,0:T(8,128)(2,1)} %bitcast.31), calls=%async_computation.1 | async-start | bytes 2097152 | tf_op jit(solution)/shard_map/all_to_all | solution.py:277
  151.9 1.1 copy.37
  153.0 0.4 copy.38
  153.5 0.9 copy.42
  154.3 2.4 %reshape.51 = f32[9,64,2,3,32]{1,0,4,3,2:T(8,128)} reshape(bf16[576,2,96]{0,2,1:T(8,128)(2,1)} %copy.42) | data formatting | bytes 663552 | tf_op jit(solution)/shard_map/convert_element_type | solution.py:291
  156.7 2.6 %copy.40 = f32[9,3,64,2,32]{2,4,3,1,0:T(8,128)} copy(f32[9,3,64,2,32]{2,0,4,1,3:T(8,128)} %bitcast.30) | data formatting | bytes 884736 | tf_op jit(solution)/shard_map/convert_element_type | solution.py:291
  159.4 2.4 %copy.41 = f32[27,64,64]{2,1,0:T(8,128)} copy(f32[27,64,64]{1,2,0:T(8,128)} %bitcast.32) | data formatting | bytes 884736
  161.7 17.1 %all-to-all-done.1.columns = bf16[128,32,128]{2,1,0:T(8,128)(2,1)S(1)} async-done(((bf16[128,32,128]{2,1,0:T(8,128)(2,1)}), bf16[128,32,128]{2,1,0:T(8,128)(2,1)S(1)}, u32[]{:S(2)}, u32[]{:S(2)}) %all-to-all-start.1) | async-done | bytes 1048608 | tf_op jit(solution)/shard_map/all_to_all | solution.py:277
  178.8 0.0 copy-done.4
  178.8 4.0 %spread.1 = bf16[32,8192]{1,0:T(8,128)(2,1)} custom-call(s32[64]{0:T(128)S(1)} %copy-done.4, bf16[128,32,128]{2,1,0:T(8,128)(2,1)S(1)} %all-to-all-done.1.columns, bf16[64,128,128]{2,1,0:T(8,128)(2,1)S(1)} %get-tuple-element.11.blocks), custom_call_target="tpu_custom_call" | custom-call | tf_op jit(solution)/shard_map/spread/pallas_call | solution.py:93
  (18 shorter events, 0.1 us)
Async XLA Ops:
  1.3 1.0 copy-start
  2.3 0.9 copy-start.1
  3.3 0.9 copy-start.2
  4.2 0.7 copy-start.3
  4.9 20.1 %copy-start.6 = (bf16[32,2,2,128]{3,2,1,0:T(2,128)(2,1)S(1)}, bf16[32,2,2,128]{3,2,1,0:T(2,128)(2,1)}, u32[]{:S(2)}) copy-start(bf16[32,2,2,128]{3,2,1,0:T(2,128)(2,1)} %param.13) | copy-start | bytes 98308
  4.9 28.1 %copy-start.5 = (bf16[27,64,64]{2,1,0:T(8,128)(2,1)S(1)}, bf16[27,64,64]{2,1,0:T(8,128)(2,1)}, u32[]{:S(2)}) copy-start(bf16[27,64,64]{2,1,0:T(8,128)(2,1)} %param.12) | copy-start | bytes 663556
  11.4 40.3 %all-to-all-start = ((bf16[128,32,128]{2,1,0:T(8,128)(2,1)}), bf16[128,32,128]{2,1,0:T(8,128)(2,1)}, u32[]{:S(2)}, u32[]{:S(2)}) async-start(bf16[128,32,128]{2,1,0:T(8,128)(2,1)} %get-tuple-element.8), calls=%async_computation | async-start | bytes 2097152 | tf_op jit(solution)/shard_map/all_to_all | solution.py:264
  25.0 25.6 %collective-permute-start.4 = (bf16[1,2,32,128]{3,2,1,0:T(8,128)(2,1)S(1)}, bf16[1,2,32,128]{3,2,1,0:T(8,128)(2,1)S(1)}, u32[]{:S(2)}, u32[]{:S(2)}) collective-permute-start(bf16[1,2,32,128]{3,2,1,0:T(8,128)(2,1)S(1)} %get-tuple-element.29), channel_id=1, source_target_pairs={{0,16},{16,32},{32,48},{48,64},{64,80},{80,96},{96,112},{112,128},... | collective-permute-start | bytes 49160 | tf_op jit(solution)/shard_map/ppermute | solution.py:221
  28.4 22.2 %collective-permute-start.5 = (bf16[1,2,32,128]{3,2,1,0:T(8,128)(2,1)S(1)}, bf16[1,2,32,128]{3,2,1,0:T(8,128)(2,1)S(1)}, u32[]{:S(2)}, u32[]{:S(2)}) collective-permute-start(bf16[1,2,32,128]{3,2,1,0:T(8,128)(2,1)S(1)} %get-tuple-element.30), channel_id=1, source_target_pairs={{16,0},{32,16},{48,32},{64,48},{80,64},{96,80},{112,96},{128,112},... | collective-permute-start | bytes 49160 | tf_op jit(solution)/shard_map/ppermute | solution.py:221
  53.1 12.8 %collective-permute-start = (bf16[2,2,32,128]{3,2,1,0:T(8,128)(2,1)S(1)}, bf16[2,2,32,128]{3,2,1,0:T(8,128)(2,1)S(1)}, u32[]{:S(2)}, u32[]{:S(2)}) collective-permute-start(bf16[2,2,32,128]{3,2,1,0:T(8,128)(2,1)S(1)} %reduce_sum.21), channel_id=1, source_target_pairs={{0,16},{16,32},{32,48},{48,64},{64,80},{80,96},{96,112},{112,128},... | collective-permute-start | bytes 98312 | tf_op jit(solution)/shard_map/ppermute | solution.py:221
  57.0 8.8 %collective-permute-start.1 = (bf16[2,2,32,128]{3,2,1,0:T(8,128)(2,1)S(1)}, bf16[2,2,32,128]{3,2,1,0:T(8,128)(2,1)S(1)}, u32[]{:S(2)}, u32[]{:S(2)}) collective-permute-start(bf16[2,2,32,128]{3,2,1,0:T(8,128)(2,1)S(1)} %reduce_sum.21), channel_id=1, source_target_pairs={{16,0},{32,16},{48,32},{64,48},{80,64},{96,80},{112,96},{128,112},... | collective-permute-start | bytes 98312 | tf_op jit(solution)/shard_map/ppermute | solution.py:221
  61.0 10.7 %collective-permute-start.6 = (bf16[4,1,32,128]{3,2,1,0:T(8,128)(2,1)S(1)}, bf16[4,1,32,128]{3,2,1,0:T(8,128)(2,1)S(1)}, u32[]{:S(2)}, u32[]{:S(2)}) collective-permute-start(bf16[4,1,32,128]{3,2,1,0:T(8,128)(2,1)S(1)} %get-tuple-element.27), channel_id=1, source_target_pairs={{0,2},{2,4},{4,6},{6,8},{8,10},{10,12},{12,14},{1,3},{3,5},{5,7},{... | collective-permute-start | bytes 98312 | tf_op jit(solution)/shard_map/ppermute | solution.py:221
  64.5 7.2 %collective-permute-start.7 = (bf16[4,1,32,128]{3,2,1,0:T(8,128)(2,1)S(1)}, bf16[4,1,32,128]{3,2,1,0:T(8,128)(2,1)S(1)}, u32[]{:S(2)}, u32[]{:S(2)}) collective-permute-start(bf16[4,1,32,128]{3,2,1,0:T(8,128)(2,1)S(1)} %get-tuple-element.28), channel_id=1, source_target_pairs={{2,0},{4,2},{6,4},{8,6},{10,8},{12,10},{14,12},{3,1},{5,3},{7,5},{... | collective-permute-start | bytes 98312 | tf_op jit(solution)/shard_map/ppermute | solution.py:221
  65.9 7.9 %collective-permute-start.2 = (bf16[6,2,32,128]{3,2,1,0:T(8,128)(2,1)S(1)}, bf16[6,2,32,128]{3,2,1,0:T(8,128)(2,1)S(1)}, u32[]{:S(2)}, u32[]{:S(2)}) collective-permute-start(bf16[6,2,32,128]{3,2,1,0:T(8,128)(2,1)S(1)} %get-tuple-element.26), channel_id=1, source_target_pairs={{0,2},{2,4},{4,6},{6,8},{8,10},{10,12},{12,14},{1,3},{3,5},{5,7},{... | collective-permute-start | bytes 294920 | tf_op jit(solution)/shard_map/ppermute | solution.py:221
  70.4 6.5 %collective-permute-start.3 = (bf16[6,2,32,128]{3,2,1,0:T(8,128)(2,1)S(1)}, bf16[6,2,32,128]{3,2,1,0:T(8,128)(2,1)S(1)}, u32[]{:S(2)}, u32[]{:S(2)}) collective-permute-start(bf16[6,2,32,128]{3,2,1,0:T(8,128)(2,1)S(1)} %get-tuple-element.26), channel_id=1, source_target_pairs={{2,0},{4,2},{6,4},{8,6},{10,8},{12,10},{14,12},{3,1},{5,3},{7,5},{... | collective-permute-start | bytes 294920 | tf_op jit(solution)/shard_map/ppermute | solution.py:221
  145.0 33.8 %all-to-all-start.1 = ((bf16[128,32,128]{2,1,0:T(8,128)(2,1)}), bf16[128,32,128]{2,1,0:T(8,128)(2,1)S(1)}, u32[]{:S(2)}, u32[]{:S(2)}) async-start(bf16[128,32,128]{2,1,0:T(8,128)(2,1)} %bitcast.31), calls=%async_computation.1 | async-start | bytes 2097152 | tf_op jit(solution)/shard_map/all_to_all | solution.py:277
  156.7 22.1 %copy-start.4 = (s32[64]{0:T(128)S(1)}, s32[64]{0:T(128)}, u32[]{:S(2)}) copy-start(s32[64]{0:T(128)} %target.3) | copy-start | bytes 772

commit v2 on v1

--- a/solution.py
+++ b/solution.py
@@ -8,7 +8,13 @@
 from jax.sharding import PartitionSpec as P
 
 GROUP = 8
-VMEM_LIMIT = 48 * 1024 * 1024
+POOL_VMEM = 60 * 1024 * 1024
+VMEM_LIMIT = 16 * 1024 * 1024
+CHUNK = 16
+
+
+def cost(flops, moved):
+    return pl.CostEstimate(flops=flops, bytes_accessed=moved, transcendentals=0)
 
 
 def pool_kernel(target, live, cells, weights, feats, blocks, send, acc):
@@ -72,7 +78,8 @@
             jax.ShapeDtypeStruct((n_columns, half, depth), jnp.bfloat16),
         ],
         scratch_shapes=[pltpu.VMEM((n_columns, half, depth), jnp.float32)],
-        compiler_params=pltpu.CompilerParams(vmem_limit_bytes=VMEM_LIMIT),
+        compiler_params=pltpu.CompilerParams(vmem_limit_bytes=POOL_VMEM),
+        cost_estimate=cost(2 * half * npts * depth, 24 * nbrs * npts * depth // 8),
         name="pool",
     )(target, live, cells, weights, feats)
 
@@ -80,29 +87,58 @@
 def spread_kernel(target, columns, blocks, out):
     step = pl.program_id(0)
     group, _, tile = blocks.shape
+    half = out.shape[0]
     for t in range(group):
         column = target[step * group + t]
-        part = jnp.dot(columns[column], blocks[t], preferred_element_type=jnp.float32)
+        first = pl.multiple_of(column % 4 * half, half)
+        own = columns[column // 4, pl.ds(first, half), :]
+        part = jnp.dot(own, blocks[t], preferred_element_type=jnp.float32)
         out[:, t * tile : (t + 1) * tile] = part.astype(jnp.bfloat16)
 
 
-def spread(target, columns, blocks):
+def spread(target, columns, blocks, half):
     tiles, depth, tile = blocks.shape
-    n_columns, half, _ = columns.shape
     group = min(GROUP, tiles)
     return pl.pallas_call(
         spread_kernel,
         grid=(tiles // group,),
         in_specs=[
             pl.BlockSpec(memory_space=pltpu.SMEM),
-            pl.BlockSpec((n_columns, half, depth), lambda i: (0, 0, 0)),
+            pl.BlockSpec(columns.shape, lambda i: (0, 0, 0)),
             pl.BlockSpec((group, depth, tile), lambda i: (i, 0, 0)),
         ],
         out_specs=pl.BlockSpec((half, group * tile), lambda i: (0, i)),
         out_shape=jax.ShapeDtypeStruct((half, tiles * tile), jnp.bfloat16),
         compiler_params=pltpu.CompilerParams(vmem_limit_bytes=VMEM_LIMIT),
+        cost_estimate=cost(2 * half * tiles * tile * depth, 6 * tiles * tile * depth),
         name="spread",
     )(target, columns, blocks)
+
+
+def unpack_kernel(gathered, out):
+    half = out.shape[2] // 2
+    per = gathered.shape[2] // CHUNK
+    for k in range(out.shape[0]):
+        rows = slice(k % per * CHUNK, (k % per + 1) * CHUNK)
+        first = gathered[k // per, 0, rows, :].astype(jnp.float32)
+        second = gathered[k // per, 1, rows, :].astype(jnp.float32)
+        for g in range(out.shape[1] // CHUNK):
+            lanes = slice(g * half, (g + 1) * half)
+            out[k, g * CHUNK : (g + 1) * CHUNK, :] = jnp.concatenate(
+                [first[:, lanes], second[:, lanes]], 1
+            )
+
+
+def unpack(gathered, offsets, full):
+    vmem = pl.BlockSpec(memory_space=pltpu.VMEM)
+    return pl.pallas_call(
+        unpack_kernel,
+        in_specs=[vmem],
+        out_specs=vmem,
+        out_shape=jax.ShapeDtypeStruct((offsets, full, full), jnp.float32),
+        compiler_params=pltpu.CompilerParams(vmem_limit_bytes=VMEM_LIMIT),
+        name="unpack",
+    )(gathered)
 
 
 def later(value, lane):
@@ -114,9 +150,11 @@
     return jnp.where(lane == depth - 1, 0.0, pltpu.roll(value, depth - 1, 1))
 
 
-def conv_kernel_body(chan, pooled, cot, wf, wb, latent, dpooled, kgrad, pp, dd, hh):
+def conv_kernel_body(chan, pooled, cot, wf, wb, latent, message, pp, dd, hh):
     half, depth = pooled.shape[4], pooled.shape[5]
     full = 2 * half
+    n_dom = message.shape[0]
+    per = message.shape[1] // CHUNK - 4 * half // CHUNK
     first = pl.multiple_of(chan[0] * half, half)
     for s in range(3):
         for y in range(6):
@@ -165,7 +203,9 @@
                 + later(grown[2 * half :], lane)
             )
             own = cot[chan[0], y + 1, x + 1].astype(jnp.float32)
-            dpooled[y, x] = (own + dx).astype(jnp.bfloat16)
+            column = (own + dx).astype(jnp.bfloat16)
+            for d in range(n_dom):
+                message[d, (2 * y + x) * half : (2 * y + x + 1) * half, :] = column
     moved = []
     for x in range(2):
         for y in range(2):
@@ -185,24 +225,34 @@
                     (((1,), (1,)), ((), ())),
                     preferred_element_type=jnp.float32,
                 )
-        kgrad[a * 3 * full : (a + 1) * 3 * full, :] = total.astype(jnp.bfloat16)
-    rest = kgrad.shape[0] - 9 * full
-    if rest:
-        kgrad[9 * full :, :] = jnp.zeros((rest, 4 * half), jnp.bfloat16)
-
-
-def conv_layer(chan, pooled, cot, wf, wb, rows):
+        for b in range(3):
+            for e in range(3):
+                k = 9 * a + 3 * b + e
+                pieces = [
+                    total[b * full + g * CHUNK : b * full + (g + 1) * CHUNK, e * half : (e + 1) * half]
+                    for g in range(full // CHUNK)
+                ]
+                row = 4 * half + k % per * CHUNK
+                message[k // per, row : row + CHUNK, :] = jnp.concatenate(pieces, 1).astype(
+                    jnp.bfloat16
+                )
+    for k in range(27, n_dom * per):
+        row = 4 * half + k % per * CHUNK
+        message[k // per, row : row + CHUNK, :] = jnp.zeros((CHUNK, depth), jnp.bfloat16)
+
+
+def conv_layer(chan, pooled, cot, wf, wb, n_dom):
     half, depth = pooled.shape[4], pooled.shape[5]
     full = 2 * half
+    per = -(-27 // n_dom)
     vmem = pl.BlockSpec(memory_space=pltpu.VMEM)
     return pl.pallas_call(
         conv_kernel_body,
         in_specs=[pl.BlockSpec(memory_space=pltpu.SMEM), vmem, vmem, vmem, vmem],
-        out_specs=[vmem, vmem, vmem],
+        out_specs=[vmem, vmem],
         out_shape=[
             jax.ShapeDtypeStruct((half, 2, 2, depth), jnp.bfloat16),
-            jax.ShapeDtypeStruct((2, 2, half, depth), jnp.bfloat16),
-            jax.ShapeDtypeStruct((rows, 4 * half), jnp.bfloat16),
+            jax.ShapeDtypeStruct((n_dom, 4 * half + per * CHUNK, depth), jnp.bfloat16),
         ],
         scratch_shapes=[
             pltpu.VMEM((6, 6 * full, depth), jnp.bfloat16),
@@ -234,10 +284,9 @@
     full = 2 * half
     xsize, ysize, depth = cotangent.shape[1:]
     n_dom, n_slab = lax.axis_size("dom"), lax.axis_size("slab")
-    devices = n_dom * n_slab
     width = xsize * ysize
     chan = lax.axis_index("chan").astype(jnp.int32)
-    scale = float(width * depth * devices) ** (-0.5)
+    scale = float(width * depth * n_dom * n_slab) ** (-0.5)
 
     blocks, send = pool(
         tile_target,
@@ -252,6 +301,7 @@
     cot = cotangent.transpose(2, 1, 0, 3)
     before, after = neighbours(cot[:1], cot[-1:], "dom")
     cot = jnp.concatenate([before, cot, after], 0)
+    send, cot = lax.optimization_barrier((send, cot))
     before, after = neighbours(cot[:, :1], cot[:, -1:], "slab")
     cot = jnp.concatenate([before, cot, after], 1)
     cot = lax.all_gather(cot, "chan", axis=0, tiled=False)
@@ -262,6 +312,7 @@
     wb = wb.transpose(0, 2, 3, 1, 4).reshape(3, 3 * half, 3 * full)
 
     recv = lax.all_to_all(send, "dom", split_axis=0, concat_axis=0, tiled=True)
+    recv, cot, wf, wb = lax.optimization_barrier((recv, cot, wf, wb))
     pooled = recv.reshape(n_dom, ysize, xsize, half, depth).astype(jnp.float32).sum(0)
     pooled = pooled.astype(jnp.bfloat16)
     before, after = neighbours(pooled, pooled, "dom")
@@ -270,25 +321,16 @@
     pooled = jnp.stack([before, pooled, after], 0)
     pooled = lax.all_gather(pooled, "chan", axis=0, tiled=False)
 
-    per = -(-9 * full // (4 * devices)) * 4
-    latent, dpooled, kgrad = conv_layer(chan[None], pooled, cot, wf, wb, per * devices)
-
-    columns = jnp.broadcast_to(dpooled.reshape(1, width, half, depth), (n_dom, width, half, depth))
-    columns = lax.all_to_all(
-        columns.reshape(n_dom * width, half, depth), "dom", split_axis=0, concat_axis=0, tiled=True
-    )
-    feature_grad = spread(tile_target, columns, blocks)
-
-    kgrad = lax.all_to_all(
-        kgrad.reshape(devices, per, 4 * half), ("dom", "slab"), split_axis=0, concat_axis=0, tiled=True
-    )
-    kgrad = (kgrad.astype(jnp.float32).sum(0) * scale).astype(jnp.bfloat16)
-    kgrad = jnp.broadcast_to(kgrad[None], (2 * devices, per, 4 * half))
-    kgrad = lax.all_to_all(kgrad, ("dom", "slab", "chan"), split_axis=0, concat_axis=0, tiled=True)
-    kgrad = kgrad.reshape(devices, 2, per, 4 * half).transpose(0, 2, 1, 3)
-    kgrad = kgrad.reshape(devices * per, 2, 4 * half)[: 9 * full, :, : 3 * half]
-    kgrad = kgrad.reshape(9, full, 2, 3, half).transpose(0, 3, 1, 2, 4)
-    kernel_grad = kgrad.reshape(27, full, full).astype(jnp.float32)
+    latent, message = conv_layer(chan[None], pooled, cot, wf, wb, n_dom)
+    columns = lax.all_to_all(message, "dom", split_axis=0, concat_axis=0, tiled=True)
+    kgrad = columns[:, width * half :].astype(jnp.float32).sum(0).astype(jnp.bfloat16)
+    kgrad = jnp.broadcast_to(kgrad[None], (2 * n_slab,) + kgrad.shape)
+    kgrad = lax.all_to_all(kgrad, ("slab", "chan"), split_axis=0, concat_axis=0, tiled=True)
+    feature_grad = spread(tile_target, columns, blocks, half)
+    kgrad = kgrad.reshape((n_slab, 2) + kgrad.shape[1:]).astype(jnp.float32).sum(0) * scale
+    kgrad = jnp.broadcast_to(kgrad.astype(jnp.bfloat16)[None], (n_dom,) + kgrad.shape)
+    kgrad = lax.all_to_all(kgrad, "dom", split_axis=0, concat_axis=0, tiled=True)
+    kernel_grad = unpack(kgrad, 27, full)
     return (latent, feature_grad, kernel_grad)
 
 

time: 185 us -> 158 us (0.85)
  local copies, waits for them, and re-layouts: 19.2 us -> 5.22 us
  blocking collectives: 66.3 us -> 58.9 us
  starting transfers between devices: 46.9 us -> 43 us
  waiting for transfers between devices: 34.5 us -> 31 us
  Pallas kernels: 12.6 us -> 16 us
    all_to_all x1, waiting for transfers between devices: 1.12 us -> 12.6 us  [body(): recv = lax.all_to_all(send, 'dom', split_axis=0, concat_axis=0, tiled=True)]
    all_to_all x1, waiting for transfers between devices: 17.1 us -> 7.35 us  [body(): lax.all_to_all(kgrad, 'dom', split_axis=0, concat_axis=0, tiled=True)]
    all_to_all x2, blocking collectives: 62.1 us -> 54.7 us  [the longest x1 37.8 us: body(): lax.all_to_all(message, 'dom', split_axis=0, concat_axis=0, tiled=True)]
    unnamed x17 -> x7, local copies, waits for them, and re-layouts: 6.85 us -> 0.78 us
    all_to_all x1, starting transfers between devices: 13.5 us -> 7.49 us  [body(): recv = lax.all_to_all(send, 'dom', split_axis=0, concat_axis=0, tiled=True)]
    ppermute x8, waiting for transfers between devices: 16.3 us -> 11 us  [neighbours(): return (lax.ppermute(last, axis, up), lax.ppermute(first, axis, down))]
    convert_element_type x2 -> x0, local copies, waits for them, and re-layouts: 5.03 us -> none  [body(): kernel_grad = kgrad.reshape(27, full, full).astype(jnp.float32)]
    ppermute x8, starting transfers between devices: 26.5 us -> 29.7 us  [neighbours(): return (lax.ppermute(last, axis, up), lax.ppermute(first, axis, down))]
  transfers between devices with their start and end apart: 10 -> 10, of which waited for: 4 -> 6; matrix products, arithmetic and copies ran while one was open for 8% -> 2% of each run, Pallas kernels for 0% -> 8%
where the time goes in v2:
time: 158 us; the launch traced here: 156 us
  blocking collectives  58.9 us (37%)
  starting transfers between devices  43 us (27%)
  waiting for transfers between devices  31 us (20%)
  Pallas kernels  16 us (10%)
  local copies, waits for them, and re-layouts  5.22 us (3%)
    all_to_all x1, blocking collectives, body(): lax.all_to_all(message, 'dom', split_axis=0, concat_axis=0, tiled=True)  37.8 us
    ppermute x8, starting transfers between devices, neighbours(): return (lax.ppermute(last, axis, up), lax.ppermute(first, axis, down))  29.7 us
    all_to_all x1, blocking collectives, body(): lax.all_to_all(kgrad, ('slab', 'chan'), split_axis=0, concat_axis=0, tile...  16.9 us
    all_to_all x1, waiting for transfers between devices, body(): recv = lax.all_to_all(send, 'dom', split_axis=0, concat_axis=0, tiled=True)  12.6 us
    ppermute x8, waiting for transfers between devices, neighbours(): return (lax.ppermute(last, axis, up), lax.ppermute(first, axis, down))  11 us
    pallas_call x1, Pallas kernels, pool(): pl.pallas_call(pool_kernel, grid=(tiles // group,), in_specs=[smem, smem,...  8.16 us
    all_to_all x1, starting transfers between devices, body(): recv = lax.all_to_all(send, 'dom', split_axis=0, concat_axis=0, tiled=True)  7.49 us
    all_to_all x1, waiting for transfers between devices, body(): lax.all_to_all(kgrad, 'dom', split_axis=0, concat_axis=0, tiled=True)  7.35 us
  transfers between devices with their start and end apart: 10, of which 6 were waited for; matrix products, arithmetic and copies ran while one was open for 2% of the time, Pallas kernels for 8%

profile of v2, /device:TPU:6, one launch (start us, length us, event | category | flops | bytes accessed | tf_op | source)
XLA Modules:
  0.0 155.9 jit_solution(11311592352019705342)
XLA Ops:
  0.6 0.8 copy.23
  1.4 4.3 %collective-permute-start = (bf16[1,2,32,128]{3,2,1,0:T(8,128)(2,1)S(1)}, bf16[1,2,32,128]{3,2,1,0:T(8,128)(2,1)S(1)}, u32[]{:S(2)}, u32[]{:S(2)}) collective-permute-start(bf16[1,2,32,128]{3,2,1,0:T(8,128)(2,1)S(1)} %get-tuple-element.27), channel_id=1, source_target_pairs={{0,16},{16,32},{32,48},{48,64},{64,80},{80,96},{96,112},{112,128},... | collective-permute-start | bytes 49160 | tf_op jit(solution)/shard_map/ppermute | solution.py:271
  5.7 8.9 %collective-permute-start.1 = (bf16[1,2,32,128]{3,2,1,0:T(8,128)(2,1)S(1)}, bf16[1,2,32,128]{3,2,1,0:T(8,128)(2,1)S(1)}, u32[]{:S(2)}, u32[]{:S(2)}) collective-permute-start(bf16[1,2,32,128]{3,2,1,0:T(8,128)(2,1)S(1)} %get-tuple-element.28), channel_id=1, source_target_pairs={{16,0},{32,16},{48,32},{64,48},{80,64},{96,80},{112,96},{128,112},... | collective-permute-start | bytes 49160 | tf_op jit(solution)/shard_map/ppermute | solution.py:271
  15.2 8.2 %pool.1 = (bf16[64,128,128]{2,1,0:T(8,128)(2,1)}, bf16[128,32,128]{2,1,0:T(8,128)(2,1)}) custom-call(s32[64]{0:T(128)} %target.3, s32[1]{0:T(128)S(6)} %copy.24.live, s32[8,8192]{1,0:T(8,128)} %cells.1, f32[8,8192]{1,0:T(8,128)} %weights.1, bf16[32,8192]{1,0:T(8,128)(2,1)} %feats.1), custom_call_target="tpu_custom_call" | custom-call | flops 67108864 | bytes 25165824 | tf_op jit(solution)/shard_map/pool/pallas_call | solution.py:62
  23.4 0.0 copy-start.2
  23.4 0.0 collective-permute-done
  23.4 0.0 collective-permute-done.1
  23.4 7.5 %all-to-all-start = ((bf16[128,32,128]{2,1,0:T(8,128)(2,1)}), bf16[128,32,128]{2,1,0:T(8,128)(2,1)S(1)}, u32[]{:S(2)}, u32[]{:S(2)}) async-start(bf16[128,32,128]{2,1,0:T(8,128)(2,1)} %get-tuple-element.14), calls=%async_computation | async-start | bytes 2097152 | tf_op jit(solution)/shard_map/all_to_all | solution.py:314
  30.9 0.0 copy-done.2
  30.9 0.4 copy.21
  31.3 1.6 %rev.3 = bf16[3,3,3,64,64]{4,1,3,2,0:T(4,128)(2,1)S(1)} reverse(bf16[3,3,3,64,64]{4,1,3,2,0:T(4,128)(2,1)S(1)} %copy.21), dimensions={0,1} | reverse | bytes 442368 | tf_op jit(solution)/shard_map/rev | solution.py:311
  33.0 3.5 %collective-permute-start.2 = (bf16[4,1,32,128]{3,2,1,0:T(8,128)(2,1)S(1)}, bf16[4,1,32,128]{3,2,1,0:T(8,128)(2,1)S(1)}, u32[]{:S(2)}, u32[]{:S(2)}) collective-permute-start(bf16[4,1,32,128]{3,2,1,0:T(8,128)(2,1)S(1)} %get-tuple-element.25), channel_id=1, source_target_pairs={{0,2},{2,4},{4,6},{6,8},{8,10},{10,12},{12,14},{1,3},{3,5},{5,7},{... | collective-permute-start | bytes 98312 | tf_op jit(solution)/shard_map/ppermute | solution.py:271
  36.5 1.3 collective-permute-start.3
  37.8 0.1 dynamic-slice_bitcast_fusion
  37.9 1.0 copy.20
  38.9 0.2 reshape.28.wb
  39.1 0.4 reshape.27.wf
  39.4 0.0 collective-permute-done.2
  39.4 2.8 %collective-permute-done.3 = bf16[4,1,32,128]{3,2,1,0:T(8,128)(2,1)S(1)} collective-permute-done((bf16[4,1,32,128]{3,2,1,0:T(8,128)(2,1)S(1)}, bf16[4,1,32,128]{3,2,1,0:T(8,128)(2,1)S(1)}, u32[]{:S(2)}, u32[]{:S(2)}) %collective-permute-start.3) | collective-permute-done | bytes 32800 | tf_op jit(solution)/shard_map/ppermute | solution.py:271
  42.3 2.0 %all-gather = bf16[8,4,32,128]{3,2,1,0:T(8,128)(2,1)S(1)} all-gather(bf16[4,4,32,128]{3,2,1,0:T(8,128)(2,1)S(1)} %pad_maximum_fusion.1), channel_id=2, replica_groups=mesh['dom'=32,'slab'=8,'chan'=2] {'chan'}, dimensions={0}, use_global_device_ids=true | all-gather | bytes 393216 | tf_op jit(solution)/shard_map/all_gather | solution.py:307
  44.3 12.6 %all-to-all-done = bf16[128,32,128]{2,1,0:T(8,128)(2,1)S(1)} async-done(((bf16[128,32,128]{2,1,0:T(8,128)(2,1)}), bf16[128,32,128]{2,1,0:T(8,128)(2,1)S(1)}, u32[]{:S(2)}, u32[]{:S(2)}) %all-to-all-start) | async-done | bytes 1048608 | tf_op jit(solution)/shard_map/all_to_all | solution.py:314
  56.9 0.2 reduce_sum.33
  57.1 4.1 %collective-permute-start.5 = (bf16[2,2,32,128]{3,2,1,0:T(8,128)(2,1)S(1)}, bf16[2,2,32,128]{3,2,1,0:T(8,128)(2,1)S(1)}, u32[]{:S(2)}, u32[]{:S(2)}) collective-permute-start(bf16[2,2,32,128]{3,2,1,0:T(8,128)(2,1)S(1)} %reduce_sum.33), channel_id=1, source_target_pairs={{16,0},{32,16},{48,32},{64,48},{80,64},{96,80},{112,96},{128,112},... | collective-permute-start | bytes 98312 | tf_op jit(solution)/shard_map/ppermute | solution.py:271
  61.1 1.9 %collective-permute-start.4 = (bf16[2,2,32,128]{3,2,1,0:T(8,128)(2,1)S(1)}, bf16[2,2,32,128]{3,2,1,0:T(8,128)(2,1)S(1)}, u32[]{:S(2)}, u32[]{:S(2)}) collective-permute-start(bf16[2,2,32,128]{3,2,1,0:T(8,128)(2,1)S(1)} %reduce_sum.33), channel_id=1, source_target_pairs={{0,16},{16,32},{32,48},{48,64},{64,80},{80,96},{96,112},{112,128},... | collective-permute-start | bytes 98312 | tf_op jit(solution)/shard_map/ppermute | solution.py:271
  63.1 0.0 collective-permute-done.5
  63.1 6.0 %collective-permute-done.4 = bf16[2,2,32,128]{3,2,1,0:T(8,128)(2,1)S(1)} collective-permute-done((bf16[2,2,32,128]{3,2,1,0:T(8,128)(2,1)S(1)}, bf16[2,2,32,128]{3,2,1,0:T(8,128)(2,1)S(1)}, u32[]{:S(2)}, u32[]{:S(2)}) %collective-permute-start.4) | collective-permute-done | bytes 32800 | tf_op jit(solution)/shard_map/ppermute | solution.py:271
  69.1 1.3 collective-permute-start.7
  70.4 4.6 %collective-permute-start.6 = (bf16[6,2,32,128]{3,2,1,0:T(8,128)(2,1)S(1)}, bf16[6,2,32,128]{3,2,1,0:T(8,128)(2,1)S(1)}, u32[]{:S(2)}, u32[]{:S(2)}) collective-permute-start(bf16[6,2,32,128]{3,2,1,0:T(8,128)(2,1)S(1)} %get-tuple-element.24), channel_id=1, source_target_pairs={{0,2},{2,4},{4,6},{6,8},{8,10},{10,12},{12,14},{1,3},{3,5},{5,7},{... | collective-permute-start | bytes 294920 | tf_op jit(solution)/shard_map/ppermute | solution.py:271
  74.9 0.7 collective-permute-done.7
  75.6 1.5 collective-permute-done.6
  77.2 2.2 %all-gather.1 = bf16[6,6,2,32,128]{4,3,2,1,0:T(8,128)(2,1)S(1)} all-gather(bf16[3,6,2,32,128]{4,3,2,1,0:T(8,128)(2,1)S(1)} %pad_maximum_fusion), channel_id=3, replica_groups=mesh['dom'=32,'slab'=8,'chan'=2] {'chan'}, dimensions={0}, use_global_device_ids=true | all-gather | bytes 884736 | tf_op jit(solution)/shard_map/all_gather | solution.py:322
  79.4 2.6 %conv_layer.1 = (bf16[32,2,2,128]{3,2,1,0:T(2,128)(2,1)}, bf16[32,144,128]{2,1,0:T(8,128)(2,1)S(1)}) custom-call(s32[1]{0:T(128)} %bitcast.chan, bf16[2,3,6,2,32,128]{5,4,3,2,1,0:T(8,128)(2,1)S(1)} %bitcast.17, bf16[2,4,4,32,128]{4,3,2,1,0:T(8,128)(2,1)S(1)} %bitcast.18, bf16[3,192,192]{2,1,0:T(8,128)(2,1)S(1)} %reshape.27.wf, ...), custom_call_target="tpu_custom_call" | custom-call | tf_op jit(solution)/shard_map/conv_layer/pallas_call | solution.py:249
  82.0 0.0 copy-start
  82.0 37.8 %all_to_all.20.columns = bf16[32,144,128]{2,1,0:T(8,128)(2,1)S(1)} all-to-all(bf16[32,144,128]{2,1,0:T(8,128)(2,1)S(1)} %get-tuple-element.21), channel_id=1, replica_groups=mesh['dom'=32,'slab'=8,'chan'=2] {'dom'}, dimensions={0} | all-to-all | bytes 2359296 | tf_op jit(solution)/shard_map/all_to_all | solution.py:325
  119.8 0.0 copy-start.1
  119.9 16.9 %all_to_all.21 = bf16[16,16,128]{2,1,0:T(8,128)(2,1)S(1)} all-to-all(bf16[16,16,128]{2,1,0:T(8,128)(2,1)S(1)} %broadcast_in_dim.7), channel_id=1, replica_groups=mesh['dom'=32,'slab'=8,'chan'=2] {'slab','chan'}, dimensions={0} | all-to-all | bytes 131072 | tf_op jit(solution)/shard_map/all_to_all | solution.py:328
  136.8 0.7 broadcast_in_dim.8
  137.6 5.8 %all-to-all-start.3 = ((bf16[32,2,16,128]{3,2,1,0:T(8,128)(2,1)}), bf16[32,2,16,128]{3,2,1,0:T(8,128)(2,1)S(1)}, u32[]{:S(2)}, u32[]{:S(2)}) async-start(bf16[32,2,16,128]{3,2,1,0:T(8,128)(2,1)} %broadcast_in_dim.8), calls=%async_computation.3 | async-start | bytes 524288 | tf_op jit(solution)/shard_map/all_to_all | solution.py:332
  143.3 0.0 copy-done
  143.3 0.0 copy-done.1
  143.4 4.1 %spread.1 = bf16[32,8192]{1,0:T(8,128)(2,1)} custom-call(s32[64]{0:T(128)S(1)} %copy-done.1, bf16[32,144,128]{2,1,0:T(8,128)(2,1)S(1)} %all_to_all.20.columns, bf16[64,128,128]{2,1,0:T(8,128)(2,1)S(1)} %copy-done), custom_call_target="tpu_custom_call" | custom-call | flops 67108864 | bytes 6291456 | tf_op jit(solution)/shard_map/spread/pallas_call | solution.py:102
  147.4 7.4 %all-to-all-done.3.gathered = bf16[32,2,16,128]{3,2,1,0:T(8,128)(2,1)S(1)} async-done(((bf16[32,2,16,128]{3,2,1,0:T(8,128)(2,1)}), bf16[32,2,16,128]{3,2,1,0:T(8,128)(2,1)S(1)}, u32[]{:S(2)}, u32[]{:S(2)}) %all-to-all-start.3) | async-done | bytes 262176 | tf_op jit(solution)/shard_map/all_to_all | solution.py:332
  154.8 1.2 unpack.1
  (10 shorter events, 0.2 us)
Async XLA Ops:
  1.4 22.0 %collective-permute-start = (bf16[1,2,32,128]{3,2,1,0:T(8,128)(2,1)S(1)}, bf16[1,2,32,128]{3,2,1,0:T(8,128)(2,1)S(1)}, u32[]{:S(2)}, u32[]{:S(2)}) collective-permute-start(bf16[1,2,32,128]{3,2,1,0:T(8,128)(2,1)S(1)} %get-tuple-element.27), channel_id=1, source_target_pairs={{0,16},{16,32},{32,48},{48,64},{64,80},{80,96},{96,112},{112,128},... | collective-permute-start | bytes 49160 | tf_op jit(solution)/shard_map/ppermute | solution.py:271
  5.7 17.7 %collective-permute-start.1 = (bf16[1,2,32,128]{3,2,1,0:T(8,128)(2,1)S(1)}, bf16[1,2,32,128]{3,2,1,0:T(8,128)(2,1)S(1)}, u32[]{:S(2)}, u32[]{:S(2)}) collective-permute-start(bf16[1,2,32,128]{3,2,1,0:T(8,128)(2,1)S(1)} %get-tuple-element.28), channel_id=1, source_target_pairs={{16,0},{32,16},{48,32},{64,48},{80,64},{96,80},{112,96},{128,112},... | collective-permute-start | bytes 49160 | tf_op jit(solution)/shard_map/ppermute | solution.py:271
  23.4 7.5 %copy-start.2 = (bf16[27,64,64]{2,1,0:T(8,128)(2,1)S(1)}, bf16[27,64,64]{2,1,0:T(8,128)(2,1)}, u32[]{:S(2)}) copy-start(bf16[27,64,64]{2,1,0:T(8,128)(2,1)} %param.12) | copy-start | bytes 663556
  23.4 33.5 %all-to-all-start = ((bf16[128,32,128]{2,1,0:T(8,128)(2,1)}), bf16[128,32,128]{2,1,0:T(8,128)(2,1)S(1)}, u32[]{:S(2)}, u32[]{:S(2)}) async-start(bf16[128,32,128]{2,1,0:T(8,128)(2,1)} %get-tuple-element.14), calls=%async_computation | async-start | bytes 2097152 | tf_op jit(solution)/shard_map/all_to_all | solution.py:314
  33.0 6.5 %collective-permute-start.2 = (bf16[4,1,32,128]{3,2,1,0:T(8,128)(2,1)S(1)}, bf16[4,1,32,128]{3,2,1,0:T(8,128)(2,1)S(1)}, u32[]{:S(2)}, u32[]{:S(2)}) collective-permute-start(bf16[4,1,32,128]{3,2,1,0:T(8,128)(2,1)S(1)} %get-tuple-element.25), channel_id=1, source_target_pairs={{0,2},{2,4},{4,6},{6,8},{8,10},{10,12},{12,14},{1,3},{3,5},{5,7},{... | collective-permute-start | bytes 98312 | tf_op jit(solution)/shard_map/ppermute | solution.py:271
  36.5 5.8 %collective-permute-start.3 = (bf16[4,1,32,128]{3,2,1,0:T(8,128)(2,1)S(1)}, bf16[4,1,32,128]{3,2,1,0:T(8,128)(2,1)S(1)}, u32[]{:S(2)}, u32[]{:S(2)}) collective-permute-start(bf16[4,1,32,128]{3,2,1,0:T(8,128)(2,1)S(1)} %get-tuple-element.26), channel_id=1, source_target_pairs={{2,0},{4,2},{6,4},{8,6},{10,8},{12,10},{14,12},{3,1},{5,3},{7,5},{... | collective-permute-start | bytes 98312 | tf_op jit(solution)/shard_map/ppermute | solution.py:271
  57.1 6.0 %collective-permute-start.5 = (bf16[2,2,32,128]{3,2,1,0:T(8,128)(2,1)S(1)}, bf16[2,2,32,128]{3,2,1,0:T(8,128)(2,1)S(1)}, u32[]{:S(2)}, u32[]{:S(2)}) collective-permute-start(bf16[2,2,32,128]{3,2,1,0:T(8,128)(2,1)S(1)} %reduce_sum.33), channel_id=1, source_target_pairs={{16,0},{32,16},{48,32},{64,48},{80,64},{96,80},{112,96},{128,112},... | collective-permute-start | bytes 98312 | tf_op jit(solution)/shard_map/ppermute | solution.py:271
  61.1 7.9 %collective-permute-start.4 = (bf16[2,2,32,128]{3,2,1,0:T(8,128)(2,1)S(1)}, bf16[2,2,32,128]{3,2,1,0:T(8,128)(2,1)S(1)}, u32[]{:S(2)}, u32[]{:S(2)}) collective-permute-start(bf16[2,2,32,128]{3,2,1,0:T(8,128)(2,1)S(1)} %reduce_sum.33), channel_id=1, source_target_pairs={{0,16},{16,32},{32,48},{48,64},{64,80},{80,96},{96,112},{112,128},... | collective-permute-start | bytes 98312 | tf_op jit(solution)/shard_map/ppermute | solution.py:271
  69.1 6.5 %collective-permute-start.7 = (bf16[6,2,32,128]{3,2,1,0:T(8,128)(2,1)S(1)}, bf16[6,2,32,128]{3,2,1,0:T(8,128)(2,1)S(1)}, u32[]{:S(2)}, u32[]{:S(2)}) collective-permute-start(bf16[6,2,32,128]{3,2,1,0:T(8,128)(2,1)S(1)} %get-tuple-element.24), channel_id=1, source_target_pairs={{2,0},{4,2},{6,4},{8,6},{10,8},{12,10},{14,12},{3,1},{5,3},{7,5},{... | collective-permute-start | bytes 294920 | tf_op jit(solution)/shard_map/ppermute | solution.py:271
  70.4 6.8 %collective-permute-start.6 = (bf16[6,2,32,128]{3,2,1,0:T(8,128)(2,1)S(1)}, bf16[6,2,32,128]{3,2,1,0:T(8,128)(2,1)S(1)}, u32[]{:S(2)}, u32[]{:S(2)}) collective-permute-start(bf16[6,2,32,128]{3,2,1,0:T(8,128)(2,1)S(1)} %get-tuple-element.24), channel_id=1, source_target_pairs={{0,2},{2,4},{4,6},{6,8},{8,10},{10,12},{12,14},{1,3},{3,5},{5,7},{... | collective-permute-start | bytes 294920 | tf_op jit(solution)/shard_map/ppermute | solution.py:271
  82.0 61.3 %copy-start = (bf16[64,128,128]{2,1,0:T(8,128)(2,1)S(1)}, bf16[64,128,128]{2,1,0:T(8,128)(2,1)}, u32[]{:S(2)}) copy-start(bf16[64,128,128]{2,1,0:T(8,128)(2,1)} %get-tuple-element.22.blocks) | copy-start | bytes 6291460
  119.8 23.5 %copy-start.1 = (s32[64]{0:T(128)S(1)}, s32[64]{0:T(128)}, u32[]{:S(2)}) copy-start(s32[64]{0:T(128)} %target.3) | copy-start | bytes 772
  137.6 17.2 %all-to-all-start.3 = ((bf16[32,2,16,128]{3,2,1,0:T(8,128)(2,1)}), bf16[32,2,16,128]{3,2,1,0:T(8,128)(2,1)S(1)}, u32[]{:S(2)}, u32[]{:S(2)}) async-start(bf16[32,2,16,128]{3,2,1,0:T(8,128)(2,1)} %broadcast_in_dim.8), calls=%async_computation.3 | async-start | bytes 524288 | tf_op jit(solution)/shard_map/all_to_all | solution.py:332

commit v3 on v2

--- a/solution.py
+++ b/solution.py
@@ -84,23 +84,23 @@
     )(target, live, cells, weights, feats)
 
 
-def spread_kernel(target, columns, blocks, out):
+def spread_kernel(inner, target, columns, blocks, out):
     step = pl.program_id(0)
     group, _, tile = blocks.shape
     half = out.shape[0]
     for t in range(group):
         column = target[step * group + t]
-        first = pl.multiple_of(column % 4 * half, half)
-        own = columns[column // 4, pl.ds(first, half), :]
+        first = pl.multiple_of(column % inner * half, half)
+        own = columns[column // inner, pl.ds(first, half), :]
         part = jnp.dot(own, blocks[t], preferred_element_type=jnp.float32)
         out[:, t * tile : (t + 1) * tile] = part.astype(jnp.bfloat16)
 
 
-def spread(target, columns, blocks, half):
+def spread(target, columns, blocks, half, inner):
     tiles, depth, tile = blocks.shape
     group = min(GROUP, tiles)
     return pl.pallas_call(
-        spread_kernel,
+        functools.partial(spread_kernel, inner),
         grid=(tiles // group,),
         in_specs=[
             pl.BlockSpec(memory_space=pltpu.SMEM),
@@ -150,19 +150,22 @@
     return jnp.where(lane == depth - 1, 0.0, pltpu.roll(value, depth - 1, 1))
 
 
-def conv_kernel_body(chan, pooled, cot, wf, wb, latent, message, pp, dd, hh):
-    half, depth = pooled.shape[4], pooled.shape[5]
+def conv_kernel_body(chan, grid, wf, wb, latent, message, pp, dd, hh):
+    half, depth = grid.shape[2], grid.shape[3]
     full = 2 * half
     n_dom = message.shape[0]
+
+    def cot(c, y, x):
+        return grid[c, (12 + y, 27 + 2 * y + x, 27 + 2 * y + x, 48 + y)[x]]
+
     per = message.shape[1] // CHUNK - 4 * half // CHUNK
     first = pl.multiple_of(chan[0] * half, half)
     for s in range(3):
         for y in range(6):
             for x in range(2):
                 for c in range(2):
-                    pp[2 * s + x, y * full + c * half : y * full + (c + 1) * half, :] = pooled[
-                        c, s, y, x
-                    ]
+                    rows = slice(y * full + c * half, y * full + (c + 1) * half)
+                    pp[2 * s + x, rows, :] = grid[c, (0, 16, 36)[s] + 2 * y + x]
     lane = lax.broadcasted_iota(jnp.int32, (full, depth), 1)
     for x in range(4):
         for y in range(4):
@@ -179,7 +182,7 @@
                 + earlier(grown[2 * full :], lane)
             )
             sig = jax.nn.sigmoid(h)
-            upper = jnp.concatenate([cot[0, y, x], cot[1, y, x]], 0).astype(jnp.float32)
+            upper = jnp.concatenate([cot(0, y, x), cot(1, y, x)], 0).astype(jnp.float32)
             dd[x, y * full : (y + 1) * full, :] = (upper * sig * (1.0 + h * (1.0 - sig))).astype(
                 jnp.bfloat16
             )
@@ -202,7 +205,7 @@
                 + earlier(grown[:half], lane)
                 + later(grown[2 * half :], lane)
             )
-            own = cot[chan[0], y + 1, x + 1].astype(jnp.float32)
+            own = cot(chan[0], y + 1, x + 1).astype(jnp.float32)
             column = (own + dx).astype(jnp.bfloat16)
             for d in range(n_dom):
                 message[d, (2 * y + x) * half : (2 * y + x + 1) * half, :] = column
@@ -241,14 +244,14 @@
         message[k // per, row : row + CHUNK, :] = jnp.zeros((CHUNK, depth), jnp.bfloat16)
 
 
-def conv_layer(chan, pooled, cot, wf, wb, n_dom):
-    half, depth = pooled.shape[4], pooled.shape[5]
+def conv_layer(chan, grid, wf, wb, n_dom):
+    half, depth = grid.shape[2], grid.shape[3]
     full = 2 * half
     per = -(-27 // n_dom)
     vmem = pl.BlockSpec(memory_space=pltpu.VMEM)
     return pl.pallas_call(
         conv_kernel_body,
-        in_specs=[pl.BlockSpec(memory_space=pltpu.SMEM), vmem, vmem, vmem, vmem],
+        in_specs=[pl.BlockSpec(memory_space=pltpu.SMEM), vmem, vmem, vmem],
         out_specs=[vmem, vmem],
         out_shape=[
             jax.ShapeDtypeStruct((half, 2, 2, depth), jnp.bfloat16),
@@ -261,7 +264,33 @@
         ],
         compiler_params=pltpu.CompilerParams(vmem_limit_bytes=VMEM_LIMIT),
         name="conv_layer",
-    )(chan, pooled, cot, wf, wb)
+    )(chan, grid, wf, wb)
+
+
+def relay_kernel(own, received, message):
+    sources = received.shape[0]
+    outer = message.shape[0]
+    total = received[0, own:, :].astype(jnp.float32)
+    for z in range(1, sources):
+        total = total + received[z, own:, :].astype(jnp.float32)
+    total = total.astype(jnp.bfloat16)
+    for x in range(outer):
+        for z in range(sources):
+            message[x, z * own : (z + 1) * own, :] = received[z, :own, :]
+        message[x, sources * own :, :] = total
+
+
+def relay(received, outer, own):
+    sources, rows, depth = received.shape
+    vmem = pl.BlockSpec(memory_space=pltpu.VMEM)
+    return pl.pallas_call(
+        functools.partial(relay_kernel, own),
+        in_specs=[vmem],
+        out_specs=vmem,
+        out_shape=jax.ShapeDtypeStruct((outer, sources * own + rows - own, depth), jnp.bfloat16),
+        compiler_params=pltpu.CompilerParams(vmem_limit_bytes=VMEM_LIMIT),
+        name="relay",
+    )(received)
 
 
 def neighbours(first, last, axis):
@@ -298,38 +327,49 @@
         depth,
     )
 
-    cot = cotangent.transpose(2, 1, 0, 3)
-    before, after = neighbours(cot[:1], cot[-1:], "dom")
-    cot = jnp.concatenate([before, cot, after], 0)
-    send, cot = lax.optimization_barrier((send, cot))
-    before, after = neighbours(cot[:, :1], cot[:, -1:], "slab")
-    cot = jnp.concatenate([before, cot, after], 1)
-    cot = lax.all_gather(cot, "chan", axis=0, tiled=False)
-
     kernel = conv_kernel.reshape(3, 3, 3, full, full)
     wf = kernel.transpose(0, 2, 4, 1, 3).reshape(3, 3 * full, 3 * full)
     wb = lax.dynamic_slice_in_dim(kernel[::-1, ::-1], chan * half, half, 3)
     wb = wb.transpose(0, 2, 3, 1, 4).reshape(3, 3 * half, 3 * full)
 
-    recv = lax.all_to_all(send, "dom", split_axis=0, concat_axis=0, tiled=True)
-    recv, cot, wf, wb = lax.optimization_barrier((recv, cot, wf, wb))
-    pooled = recv.reshape(n_dom, ysize, xsize, half, depth).astype(jnp.float32).sum(0)
-    pooled = pooled.astype(jnp.bfloat16)
-    before, after = neighbours(pooled, pooled, "dom")
-    pooled = jnp.concatenate([before, pooled, after], 0)
-    before, after = neighbours(pooled, pooled, "slab")
-    pooled = jnp.stack([before, pooled, after], 0)
-    pooled = lax.all_gather(pooled, "chan", axis=0, tiled=False)
-
-    latent, message = conv_layer(chan[None], pooled, cot, wf, wb, n_dom)
-    columns = lax.all_to_all(message, "dom", split_axis=0, concat_axis=0, tiled=True)
-    kgrad = columns[:, width * half :].astype(jnp.float32).sum(0).astype(jnp.bfloat16)
-    kgrad = jnp.broadcast_to(kgrad[None], (2 * n_slab,) + kgrad.shape)
-    kgrad = lax.all_to_all(kgrad, ("slab", "chan"), split_axis=0, concat_axis=0, tiled=True)
-    feature_grad = spread(tile_target, columns, blocks, half)
-    kgrad = kgrad.reshape((n_slab, 2) + kgrad.shape[1:]).astype(jnp.float32).sum(0) * scale
-    kgrad = jnp.broadcast_to(kgrad.astype(jnp.bfloat16)[None], (n_dom,) + kgrad.shape)
-    kgrad = lax.all_to_all(kgrad, "dom", split_axis=0, concat_axis=0, tiled=True)
+    inner = min(8, n_dom // 2)
+    outer = n_dom // inner
+    same_z = [[x * inner + z for x in range(outer)] for z in range(inner)]
+    same_x = [[x * inner + z for z in range(inner)] for x in range(outer)]
+
+    def exchange(value, axis, groups=None):
+        return lax.all_to_all(
+            value, axis, split_axis=0, concat_axis=0, tiled=True, axis_index_groups=groups
+        )
+
+    def total(value, parts):
+        return value.reshape((parts, -1) + value.shape[1:]).astype(jnp.float32).sum(0)
+
+    part = total(exchange(send, "dom", same_z), outer).astype(jnp.bfloat16)
+    part = exchange(part, "dom", same_x)
+    part, wf, wb = lax.optimization_barrier((part, wf, wb))
+    pooled = total(part, inner).astype(jnp.bfloat16)
+
+    cot = cotangent.transpose(2, 1, 0, 3)
+    before, after = neighbours(
+        jnp.concatenate([pooled, cot[0]], 0), jnp.concatenate([pooled, cot[-1]], 0), "dom"
+    )
+    pooled = jnp.concatenate([before[:width], pooled, after[:width]], 0)
+    cot = jnp.concatenate([before[None, width:], cot, after[None, width:]], 0)
+    before, after = neighbours(
+        jnp.concatenate([pooled, cot[:, 0]], 0), jnp.concatenate([pooled, cot[:, -1]], 0), "slab"
+    )
+    grid = jnp.concatenate([before, pooled, cot.reshape((-1,) + cot.shape[2:]), after], 0)
+    grid = lax.all_gather(grid, "chan", axis=0, tiled=False)
+
+    latent, message = conv_layer(chan[None], grid, wf, wb, inner)
+    message = relay(exchange(message, "dom", same_x), outer, width * half)
+    columns = exchange(message, "dom", same_z)
+    kgrad = columns[:, inner * width * half :].astype(jnp.float32).sum(0).astype(jnp.bfloat16)
+    kgrad = exchange(jnp.broadcast_to(kgrad[None], (2 * n_slab,) + kgrad.shape), ("slab", "chan"))
+    feature_grad = spread(tile_target, columns, blocks, half, inner * width)
+    kgrad = (total(kgrad, n_slab) * scale).astype(jnp.bfloat16)
+    kgrad = exchange(jnp.broadcast_to(kgrad[None], (inner,) + kgrad.shape), "dom", same_x)
     kernel_grad = unpack(kgrad, 27, full)
     return (latent, feature_grad, kernel_grad)
 

time: 158 us -> 153 us (0.968)
  the two profiles are of different devices: /device:TPU:6 before, /device:TPU:1 now
where the time goes in v3:
time: 153 us; the launch traced here: 152 us
  blocking collectives  81.8 us (53%)
  starting transfers between devices  27.7 us (18%)
  waiting for transfers between devices  19.3 us (13%)
  Pallas kernels  16.1 us (11%)
  local copies, waits for them, and re-layouts  4.61 us (3%)
  between operations  1.54 us (1%)
    all_to_all x4, blocking collectives, exchange(): lax.all_to_all(value, axis, split_axis=0, concat_axis=0, tiled=True, axis...  73.6 us
    all_to_all x2, starting transfers between devices, exchange(): lax.all_to_all(value, axis, split_axis=0, concat_axis=0, tiled=True, axis...  17.9 us
    all_to_all x2, waiting for transfers between devices, exchange(): lax.all_to_all(value, axis, split_axis=0, concat_axis=0, tiled=True, axis...  13.8 us
    ppermute x4, starting transfers between devices, neighbours(): return (lax.ppermute(last, axis, up), lax.ppermute(first, axis, down))  9.78 us
    pallas_call x1, Pallas kernels, pool(): pl.pallas_call(pool_kernel, grid=(tiles // group,), in_specs=[smem, smem,...  8.17 us
    all_gather x1, blocking collectives, body(): grid = lax.all_gather(grid, 'chan', axis=0, tiled=False)  8.12 us
    ppermute x4, waiting for transfers between devices, neighbours(): return (lax.ppermute(last, axis, up), lax.ppermute(first, axis, down))  5.47 us
    pallas_call x1, Pallas kernels, spread(): pl.pallas_call(functools.partial(spread_kernel, inner), grid=(tiles // gr...  4.05 us
  transfers between devices with their start and end apart: 6, of which 5 were waited for; matrix products, arithmetic and copies ran while one was open for 2% of the time, Pallas kernels for 3%

profile of v3, /device:TPU:1, one launch (start us, length us, event | category | flops | bytes accessed | tf_op | source)
XLA Modules:
  0.0 152.1 jit_solution(13806323255303363942)
XLA Ops:
  1.3 8.2 %pool.1 = (bf16[64,128,128]{2,1,0:T(8,128)(2,1)}, bf16[128,32,128]{2,1,0:T(8,128)(2,1)}) custom-call(s32[64]{0:T(128)} %target.3, s32[1]{0:T(128)S(6)} %copy.41.live, s32[8,8192]{1,0:T(8,128)} %cells.1, f32[8,8192]{1,0:T(8,128)} %weights.1, bf16[32,8192]{1,0:T(8,128)(2,1)} %feats.1), custom_call_target="tpu_custom_call" | custom-call | flops 67108864 | bytes 25165824 | tf_op jit(solution)/shard_map/pool/pallas_call | solution.py:62
  9.4 14.6 %all_to_all.30 = bf16[128,32,128]{2,1,0:T(8,128)(2,1)S(1)} all-to-all(bf16[128,32,128]{2,1,0:T(8,128)(2,1)} %get-tuple-element.10), channel_id=1, replica_groups={{0,128,256,384},{16,144,272,400},{32,160,288,416},{48,176,304,432},{64,..., dimensions={0} | all-to-all | bytes 2097152 | tf_op jit(solution)/shard_map/all_to_all | solution.py:341
  24.0 0.0 copy-start.2
  24.0 0.9 reduce_sum.45
  24.9 14.5 %all-to-all-start.1 = ((bf16[32,32,128]{2,1,0:T(8,128)(2,1)}), bf16[32,32,128]{2,1,0:T(8,128)(2,1)S(1)}, u32[]{:S(2)}, u32[]{:S(2)}) async-start(bf16[32,32,128]{2,1,0:T(8,128)(2,1)} %reduce_sum.45), calls=%async_computation.1 | async-start | bytes 524288 | tf_op jit(solution)/shard_map/all_to_all | solution.py:341
  39.4 0.0 copy-done.2
  39.4 1.0 copy.26
  40.4 0.4 copy.27
  40.8 0.4 reshape.34.wf
  41.1 0.0 copy-start.3
  41.2 1.6 %rev.3 = bf16[3,3,3,64,64]{4,1,3,2,0:T(4,128)(2,1)S(1)} reverse(bf16[3,3,3,64,64]{4,1,3,2,0:T(4,128)(2,1)S(1)} %copy.27), dimensions={0,1} | reverse | bytes 442368 | tf_op jit(solution)/shard_map/rev | solution.py:332
  42.8 0.1 dynamic-slice_bitcast_fusion
  42.9 0.2 reshape.35.wb
  43.1 0.0 copy-done.3
  43.2 5.6 %all-to-all-done.1 = bf16[32,32,128]{2,1,0:T(8,128)(2,1)S(1)} async-done(((bf16[32,32,128]{2,1,0:T(8,128)(2,1)}), bf16[32,32,128]{2,1,0:T(8,128)(2,1)S(1)}, u32[]{:S(2)}, u32[]{:S(2)}) %all-to-all-start.1) | async-done | bytes 262176 | tf_op jit(solution)/shard_map/all_to_all | solution.py:341
  48.8 1.3 collective-permute-start.1
  50.1 4.0 %collective-permute-start = (bf16[6,32,128]{2,1,0:T(8,128)(2,1)S(1)}, bf16[6,32,128]{2,1,0:T(8,128)(2,1)S(1)}, u32[]{:S(2)}, u32[]{:S(2)}) collective-permute-start(bf16[6,32,128]{2,1,0:T(8,128)(2,1)S(1)} %get-tuple-element.21), channel_id=1, source_target_pairs={{0,16},{16,32},{32,48},{48,64},{64,80},{80,96},{96,112},{112,128},... | collective-permute-start | bytes 147464 | tf_op jit(solution)/shard_map/ppermute | solution.py:300
  54.1 0.0 collective-permute-done.1
  54.1 1.1 collective-permute-done
  55.4 3.2 %collective-permute-start.2 = (bf16[16,32,128]{2,1,0:T(8,128)(2,1)S(1)}, bf16[16,32,128]{2,1,0:T(8,128)(2,1)S(1)}, u32[]{:S(2)}, u32[]{:S(2)}) collective-permute-start(bf16[16,32,128]{2,1,0:T(8,128)(2,1)S(1)} %get-tuple-element.18), channel_id=1, source_target_pairs={{0,2},{2,4},{4,6},{6,8},{8,10},{10,12},{12,14},{1,3},{3,5},{5,7},{... | collective-permute-start | bytes 393224 | tf_op jit(solution)/shard_map/ppermute | solution.py:300
  58.6 1.3 collective-permute-start.3
  59.9 0.6 collective-permute-done.2
  60.6 3.7 %collective-permute-done.3 = bf16[16,32,128]{2,1,0:T(8,128)(2,1)S(1)} collective-permute-done((bf16[16,32,128]{2,1,0:T(8,128)(2,1)S(1)}, bf16[16,32,128]{2,1,0:T(8,128)(2,1)S(1)}, u32[]{:S(2)}, u32[]{:S(2)}) %collective-permute-start.3) | collective-permute-done | bytes 131104 | tf_op jit(solution)/shard_map/ppermute | solution.py:300
  64.3 8.1 %all-gather = bf16[104,32,128]{2,1,0:T(8,128)(2,1)S(1)} all-gather(bf16[52,32,128]{2,1,0:T(8,128)(2,1)S(1)} %constant_dynamic-update-slice_fusion), channel_id=2, replica_groups=mesh['dom'=32,'slab'=8,'chan'=2] {'chan'}, dimensions={0}, use_global_device_ids=true | all-gather | bytes 1277952 | tf_op jit(solution)/shard_map/all_gather | solution.py:363
  72.4 2.6 %conv_layer.1 = (bf16[32,2,2,128]{3,2,1,0:T(2,128)(2,1)}, bf16[8,192,128]{2,1,0:T(8,128)(2,1)S(1)}) custom-call(s32[1]{0:T(128)} %bitcast.chan, bf16[2,52,32,128]{3,2,1,0:T(8,128)(2,1)S(1)} %bitcast.29, bf16[3,192,192]{2,1,0:T(8,128)(2,1)S(1)} %reshape.34.wf, bf16[3,96,192]{2,1,0:T(8,128)(2,1)S(1)} %reshape.35.wb), custom_call_target="tpu_custom_call" | custom-call | tf_op jit(solution)/shard_map/conv_layer/pallas_call | solution.py:252
  75.1 19.1 %all_to_all.31.received = bf16[8,192,128]{2,1,0:T(8,128)(2,1)S(1)} all-to-all(bf16[8,192,128]{2,1,0:T(8,128)(2,1)S(1)} %get-tuple-element.15), channel_id=1, replica_groups={{0,16,32,48,64,80,96,112},{128,144,160,176,192,208,224,240},{256,272,28..., dimensions={0} | all-to-all | bytes 786432 | tf_op jit(solution)/shard_map/all_to_all | solution.py:341
  94.2 0.1 relay.1
  94.3 19.3 %all_to_all.32.columns = bf16[4,1088,128]{2,1,0:T(8,128)(2,1)S(1)} all-to-all(bf16[4,1088,128]{2,1,0:T(8,128)(2,1)S(1)} %relay.1), channel_id=1, replica_groups={{0,128,256,384},{16,144,272,400},{32,160,288,416},{48,176,304,432},{64,..., dimensions={0} | all-to-all | bytes 2228224 | tf_op jit(solution)/shard_map/all_to_all | solution.py:341
  113.7 0.0 copy-start
  113.7 0.0 copy-start.1
  113.8 20.6 %all_to_all.33 = bf16[16,64,128]{2,1,0:T(8,128)(2,1)S(1)} all-to-all(bf16[16,64,128]{2,1,0:T(8,128)(2,1)S(1)} %broadcast_in_dim.24), channel_id=1, replica_groups=mesh['dom'=32,'slab'=8,'chan'=2] {'slab','chan'}, dimensions={0} | all-to-all | bytes 524288 | tf_op jit(solution)/shard_map/all_to_all | solution.py:341
  134.4 0.8 broadcast_in_dim.25
  135.2 3.4 %all-to-all-start.5 = ((bf16[8,2,64,128]{3,2,1,0:T(8,128)(2,1)}), bf16[8,2,64,128]{3,2,1,0:T(8,128)(2,1)S(1)}, u32[]{:S(2)}, u32[]{:S(2)}) async-start(bf16[8,2,64,128]{3,2,1,0:T(8,128)(2,1)} %broadcast_in_dim.25), calls=%async_computation.5 | async-start | bytes 524288 | tf_op jit(solution)/shard_map/all_to_all | solution.py:341
  138.6 0.0 copy-done
  138.6 0.0 copy-done.1
  138.6 4.1 %spread.1 = bf16[32,8192]{1,0:T(8,128)(2,1)} custom-call(s32[64]{0:T(128)S(1)} %copy-done.1, bf16[4,1088,128]{2,1,0:T(8,128)(2,1)S(1)} %all_to_all.32.columns, bf16[64,128,128]{2,1,0:T(8,128)(2,1)S(1)} %copy-done), custom_call_target="tpu_custom_call" | custom-call | flops 67108864 | bytes 6291456 | tf_op jit(solution)/shard_map/spread/pallas_call | solution.py:102
  142.7 8.3 %all-to-all-done.5.gathered = bf16[8,2,64,128]{3,2,1,0:T(8,128)(2,1)S(1)} async-done(((bf16[8,2,64,128]{3,2,1,0:T(8,128)(2,1)}), bf16[8,2,64,128]{3,2,1,0:T(8,128)(2,1)S(1)}, u32[]{:S(2)}, u32[]{:S(2)}) %all-to-all-start.5) | async-done | bytes 262176 | tf_op jit(solution)/shard_map/all_to_all | solution.py:341
  150.9 1.2 unpack.1
  (23 shorter events, 0.3 us)
Async XLA Ops:
  24.0 15.4 %copy-start.2 = (bf16[27,64,64]{2,1,0:T(8,128)(2,1)S(1)}, bf16[27,64,64]{2,1,0:T(8,128)(2,1)}, u32[]{:S(2)}) copy-start(bf16[27,64,64]{2,1,0:T(8,128)(2,1)} %param.12) | copy-start | bytes 663556
  24.9 23.8 %all-to-all-start.1 = ((bf16[32,32,128]{2,1,0:T(8,128)(2,1)}), bf16[32,32,128]{2,1,0:T(8,128)(2,1)S(1)}, u32[]{:S(2)}, u32[]{:S(2)}) async-start(bf16[32,32,128]{2,1,0:T(8,128)(2,1)} %reduce_sum.45), calls=%async_computation.1 | async-start | bytes 524288 | tf_op jit(solution)/shard_map/all_to_all | solution.py:341
  41.1 2.0 %copy-start.3 = (bf16[32,2,2,128]{3,2,1,0:T(2,128)(2,1)S(1)}, bf16[32,2,2,128]{3,2,1,0:T(2,128)(2,1)}, u32[]{:S(2)}) copy-start(bf16[32,2,2,128]{3,2,1,0:T(2,128)(2,1)} %param.13) | copy-start | bytes 98308
  48.8 5.3 %collective-permute-start.1 = (bf16[6,32,128]{2,1,0:T(8,128)(2,1)S(1)}, bf16[6,32,128]{2,1,0:T(8,128)(2,1)S(1)}, u32[]{:S(2)}, u32[]{:S(2)}) collective-permute-start(bf16[6,32,128]{2,1,0:T(8,128)(2,1)S(1)} %get-tuple-element.22), channel_id=1, source_target_pairs={{16,0},{32,16},{48,32},{64,48},{80,64},{96,80},{112,96},{128,112},... | collective-permute-start | bytes 147464 | tf_op jit(solution)/shard_map/ppermute | solution.py:300
  50.1 5.2 %collective-permute-start = (bf16[6,32,128]{2,1,0:T(8,128)(2,1)S(1)}, bf16[6,32,128]{2,1,0:T(8,128)(2,1)S(1)}, u32[]{:S(2)}, u32[]{:S(2)}) collective-permute-start(bf16[6,32,128]{2,1,0:T(8,128)(2,1)S(1)} %get-tuple-element.21), channel_id=1, source_target_pairs={{0,16},{16,32},{32,48},{48,64},{64,80},{80,96},{96,112},{112,128},... | collective-permute-start | bytes 147464 | tf_op jit(solution)/shard_map/ppermute | solution.py:300
  55.4 5.1 %collective-permute-start.2 = (bf16[16,32,128]{2,1,0:T(8,128)(2,1)S(1)}, bf16[16,32,128]{2,1,0:T(8,128)(2,1)S(1)}, u32[]{:S(2)}, u32[]{:S(2)}) collective-permute-start(bf16[16,32,128]{2,1,0:T(8,128)(2,1)S(1)} %get-tuple-element.18), channel_id=1, source_target_pairs={{0,2},{2,4},{4,6},{6,8},{8,10},{10,12},{12,14},{1,3},{3,5},{5,7},{... | collective-permute-start | bytes 393224 | tf_op jit(solution)/shard_map/ppermute | solution.py:300
  58.6 5.7 %collective-permute-start.3 = (bf16[16,32,128]{2,1,0:T(8,128)(2,1)S(1)}, bf16[16,32,128]{2,1,0:T(8,128)(2,1)S(1)}, u32[]{:S(2)}, u32[]{:S(2)}) collective-permute-start(bf16[16,32,128]{2,1,0:T(8,128)(2,1)S(1)} %get-tuple-element.17), channel_id=1, source_target_pairs={{2,0},{4,2},{6,4},{8,6},{10,8},{12,10},{14,12},{3,1},{5,3},{7,5},{... | collective-permute-start | bytes 393224 | tf_op jit(solution)/shard_map/ppermute | solution.py:300
  113.7 24.9 %copy-start = (bf16[64,128,128]{2,1,0:T(8,128)(2,1)S(1)}, bf16[64,128,128]{2,1,0:T(8,128)(2,1)}, u32[]{:S(2)}) copy-start(bf16[64,128,128]{2,1,0:T(8,128)(2,1)} %get-tuple-element.16.blocks) | copy-start | bytes 6291460
  113.7 24.9 %copy-start.1 = (s32[64]{0:T(128)S(1)}, s32[64]{0:T(128)}, u32[]{:S(2)}) copy-start(s32[64]{0:T(128)} %target.3) | copy-start | bytes 772
  135.2 15.8 %all-to-all-start.5 = ((bf16[8,2,64,128]{3,2,1,0:T(8,128)(2,1)}), bf16[8,2,64,128]{3,2,1,0:T(8,128)(2,1)S(1)}, u32[]{:S(2)}, u32[]{:S(2)}) async-start(bf16[8,2,64,128]{3,2,1,0:T(8,128)(2,1)} %broadcast_in_dim.25), calls=%async_computation.5 | async-start | bytes 524288 | tf_op jit(solution)/shard_map/all_to_all | solution.py:341

commit v4 on v3

--- a/solution.py
+++ b/solution.py
@@ -84,23 +84,21 @@
     )(target, live, cells, weights, feats)
 
 
-def spread_kernel(inner, target, columns, blocks, out):
+def spread_kernel(target, columns, blocks, out):
     step = pl.program_id(0)
     group, _, tile = blocks.shape
-    half = out.shape[0]
     for t in range(group):
         column = target[step * group + t]
-        first = pl.multiple_of(column % inner * half, half)
-        own = columns[column // inner, pl.ds(first, half), :]
-        part = jnp.dot(own, blocks[t], preferred_element_type=jnp.float32)
+        part = jnp.dot(columns[column], blocks[t], preferred_element_type=jnp.float32)
         out[:, t * tile : (t + 1) * tile] = part.astype(jnp.bfloat16)
 
 
-def spread(target, columns, blocks, half, inner):
+def spread(target, columns, blocks):
     tiles, depth, tile = blocks.shape
+    half = columns.shape[1]
     group = min(GROUP, tiles)
     return pl.pallas_call(
-        functools.partial(spread_kernel, inner),
+        spread_kernel,
         grid=(tiles // group,),
         in_specs=[
             pl.BlockSpec(memory_space=pltpu.SMEM),
@@ -115,13 +113,17 @@
     )(target, columns, blocks)
 
 
-def unpack_kernel(gathered, out):
+def unpack_kernel(inner, gathered, out):
+    n_dom = gathered.shape[0]
+    outer = n_dom // inner
     half = out.shape[2] // 2
-    per = gathered.shape[2] // CHUNK
+    each = gathered.shape[2] // CHUNK
     for k in range(out.shape[0]):
-        rows = slice(k % per * CHUNK, (k % per + 1) * CHUNK)
-        first = gathered[k // per, 0, rows, :].astype(jnp.float32)
-        second = gathered[k // per, 1, rows, :].astype(jnp.float32)
+        place = k // each
+        source = place % outer * inner + place // outer
+        rows = slice(k % each * CHUNK, (k % each + 1) * CHUNK)
+        first = gathered[source, 0, rows, :].astype(jnp.float32)
+        second = gathered[source, 1, rows, :].astype(jnp.float32)
         for g in range(out.shape[1] // CHUNK):
             lanes = slice(g * half, (g + 1) * half)
             out[k, g * CHUNK : (g + 1) * CHUNK, :] = jnp.concatenate(
@@ -129,10 +131,10 @@
             )
 
 
-def unpack(gathered, offsets, full):
+def unpack(gathered, offsets, full, inner):
     vmem = pl.BlockSpec(memory_space=pltpu.VMEM)
     return pl.pallas_call(
-        unpack_kernel,
+        functools.partial(unpack_kernel, inner),
         in_specs=[vmem],
         out_specs=vmem,
         out_shape=jax.ShapeDtypeStruct((offsets, full, full), jnp.float32),
@@ -244,10 +246,9 @@
         message[k // per, row : row + CHUNK, :] = jnp.zeros((CHUNK, depth), jnp.bfloat16)
 
 
-def conv_layer(chan, grid, wf, wb, n_dom):
+def conv_layer(chan, grid, wf, wb, n_dom, per):
     half, depth = grid.shape[2], grid.shape[3]
     full = 2 * half
-    per = -(-27 // n_dom)
     vmem = pl.BlockSpec(memory_space=pltpu.VMEM)
     return pl.pallas_call(
         conv_kernel_body,
@@ -265,32 +266,6 @@
         compiler_params=pltpu.CompilerParams(vmem_limit_bytes=VMEM_LIMIT),
         name="conv_layer",
     )(chan, grid, wf, wb)
-
-
-def relay_kernel(own, received, message):
-    sources = received.shape[0]
-    outer = message.shape[0]
-    total = received[0, own:, :].astype(jnp.float32)
-    for z in range(1, sources):
-        total = total + received[z, own:, :].astype(jnp.float32)
-    total = total.astype(jnp.bfloat16)
-    for x in range(outer):
-        for z in range(sources):
-            message[x, z * own : (z + 1) * own, :] = received[z, :own, :]
-        message[x, sources * own :, :] = total
-
-
-def relay(received, outer, own):
-    sources, rows, depth = received.shape
-    vmem = pl.BlockSpec(memory_space=pltpu.VMEM)
-    return pl.pallas_call(
-        functools.partial(relay_kernel, own),
-        in_specs=[vmem],
-        out_specs=vmem,
-        out_shape=jax.ShapeDtypeStruct((outer, sources * own + rows - own, depth), jnp.bfloat16),
-        compiler_params=pltpu.CompilerParams(vmem_limit_bytes=VMEM_LIMIT),
-        name="relay",
-    )(received)
 
 
 def neighbours(first, last, axis):
@@ -362,15 +337,28 @@
     grid = jnp.concatenate([before, pooled, cot.reshape((-1,) + cot.shape[2:]), after], 0)
     grid = lax.all_gather(grid, "chan", axis=0, tiled=False)
 
-    latent, message = conv_layer(chan[None], grid, wf, wb, inner)
-    message = relay(exchange(message, "dom", same_x), outer, width * half)
-    columns = exchange(message, "dom", same_z)
-    kgrad = columns[:, inner * width * half :].astype(jnp.float32).sum(0).astype(jnp.bfloat16)
-    kgrad = exchange(jnp.broadcast_to(kgrad[None], (2 * n_slab,) + kgrad.shape), ("slab", "chan"))
-    feature_grad = spread(tile_target, columns, blocks, half, inner * width)
-    kgrad = (total(kgrad, n_slab) * scale).astype(jnp.bfloat16)
-    kgrad = exchange(jnp.broadcast_to(kgrad[None], (inner,) + kgrad.shape), "dom", same_x)
-    kernel_grad = unpack(kgrad, 27, full)
+    each = -(-27 // n_dom)
+    latent, message = conv_layer(chan[None], grid, wf, wb, inner, outer * each)
+    message = exchange(message, "dom", same_x)
+    columns = message[:, : width * half].reshape(inner * width, half, depth)
+    columns = lax.all_gather(columns, "dom", axis=0, tiled=True, axis_index_groups=same_z)
+
+    peers = 2 * n_slab
+    same_z_all = [
+        [(x * inner + z) * peers + p for x in range(outer) for p in range(peers)]
+        for z in range(inner)
+    ]
+    kgrad = message[:, width * half :].astype(jnp.float32).sum(0).astype(jnp.bfloat16)
+    kgrad = kgrad.reshape(outer, 1, each * CHUNK, depth)
+    kgrad = jnp.broadcast_to(kgrad, (outer, peers, each * CHUNK, depth))
+    kgrad = exchange(
+        kgrad.reshape(outer * peers, each * CHUNK, depth), ("dom", "slab", "chan"), same_z_all
+    )
+    kgrad = (total(kgrad, outer * n_slab) * scale).astype(jnp.bfloat16)
+    kgrad = exchange(jnp.broadcast_to(kgrad[None], (n_dom,) + kgrad.shape), "dom")
+    feature_grad = spread(tile_target, columns, blocks)
+    kgrad, feature_grad = lax.optimization_barrier((kgrad, feature_grad))
+    kernel_grad = unpack(kgrad, 27, full, inner)
     return (latent, feature_grad, kernel_grad)
 
 

time: 153 us -> 150 us (0.980)
  the two profiles are of different devices: /device:TPU:1 before, /device:TPU:6 now
where the time goes in v4:
time: 150 us; the launch traced here: 148 us
  blocking collectives  62 us (41%)
  starting transfers between devices  25.5 us (17%)
  waiting for transfers between devices  22.1 us (15%)
  Pallas kernels  16 us (11%)
  between operations  14.9 us (10%)
  local copies, waits for them, and re-layouts  6.52 us (4%)
    all_to_all x3, blocking collectives, exchange(): lax.all_to_all(value, axis, split_axis=0, concat_axis=0, tiled=True, axis...  59.6 us
    all_to_all x2, starting transfers between devices, exchange(): lax.all_to_all(value, axis, split_axis=0, concat_axis=0, tiled=True, axis...  14.9 us
    all_to_all x2, waiting for transfers between devices, exchange(): lax.all_to_all(value, axis, split_axis=0, concat_axis=0, tiled=True, axis...  12.4 us
    ppermute x4, starting transfers between devices, neighbours(): return (lax.ppermute(last, axis, up), lax.ppermute(first, axis, down))  10.6 us
    ppermute x4, waiting for transfers between devices, neighbours(): return (lax.ppermute(last, axis, up), lax.ppermute(first, axis, down))  9.64 us
    pallas_call x1, Pallas kernels, pool(): pl.pallas_call(pool_kernel, grid=(tiles // group,), in_specs=[smem, smem,...  8.17 us
    pallas_call x1, Pallas kernels, spread(): pl.pallas_call(spread_kernel, grid=(tiles // group,), in_specs=[pl.BlockS...  4.05 us
  transfers between devices with their start and end apart: 7, of which 6 were waited for; matrix products, arithmetic and copies ran while one was open for 3% of the time, Pallas kernels for 3%

profile of v4, /device:TPU:6, one launch (start us, length us, event | category | flops | bytes accessed | tf_op | source)
XLA Modules:
  0.0 148.1 jit_solution(8007879435413409585)
XLA Ops:
  7.8 8.2 %pool.1 = (bf16[64,128,128]{2,1,0:T(8,128)(2,1)}, bf16[128,32,128]{2,1,0:T(8,128)(2,1)}) custom-call(s32[64]{0:T(128)} %target.3, s32[1]{0:T(128)S(6)} %copy.41.live, s32[8,8192]{1,0:T(8,128)} %cells.1, f32[8,8192]{1,0:T(8,128)} %weights.1, bf16[32,8192]{1,0:T(8,128)(2,1)} %feats.1), custom_call_target="tpu_custom_call" | custom-call | flops 67108864 | bytes 25165824 | tf_op jit(solution)/shard_map/pool/pallas_call | solution.py:62
  16.0 0.0 copy-start.3
  16.0 18.3 %all_to_all.25 = bf16[128,32,128]{2,1,0:T(8,128)(2,1)S(1)} all-to-all(bf16[128,32,128]{2,1,0:T(8,128)(2,1)} %get-tuple-element.12), channel_id=1, replica_groups={{0,128,256,384},{16,144,272,400},{32,160,288,416},{48,176,304,432},{64,..., dimensions={0} | all-to-all | bytes 2097152 | tf_op jit(solution)/shard_map/all_to_all | solution.py:316
  34.3 0.9 reduce_sum.45
  35.2 10.0 %all-to-all-start.1 = ((bf16[32,32,128]{2,1,0:T(8,128)(2,1)}), bf16[32,32,128]{2,1,0:T(8,128)(2,1)S(1)}, u32[]{:S(2)}, u32[]{:S(2)}) async-start(bf16[32,32,128]{2,1,0:T(8,128)(2,1)} %reduce_sum.45), calls=%async_computation.1 | async-start | bytes 524288 | tf_op jit(solution)/shard_map/all_to_all | solution.py:316
  45.1 0.0 all-gather.3.cloned.1.call-start
  45.2 0.0 copy-done.3
  45.2 1.0 copy.26
  46.2 0.0 copy-start.4
  46.2 0.4 copy.27
  46.6 0.4 reshape.41.wf
  46.9 1.6 %rev.3 = bf16[3,3,3,64,64]{4,1,3,2,0:T(4,128)(2,1)S(1)} reverse(bf16[3,3,3,64,64]{4,1,3,2,0:T(4,128)(2,1)S(1)} %copy.27), dimensions={0,1} | reverse | bytes 442368 | tf_op jit(solution)/shard_map/rev | solution.py:307
  48.6 0.1 dynamic-slice_bitcast_fusion
  48.7 0.2 reshape.42.wb
  48.9 0.0 copy-done.4
  49.0 6.9 %all-to-all-done.1 = bf16[32,32,128]{2,1,0:T(8,128)(2,1)S(1)} async-done(((bf16[32,32,128]{2,1,0:T(8,128)(2,1)}), bf16[32,32,128]{2,1,0:T(8,128)(2,1)S(1)}, u32[]{:S(2)}, u32[]{:S(2)}) %all-to-all-start.1) | async-done | bytes 262176 | tf_op jit(solution)/shard_map/all_to_all | solution.py:316
  55.9 1.9 %collective-permute-start.1 = (bf16[6,32,128]{2,1,0:T(8,128)(2,1)S(1)}, bf16[6,32,128]{2,1,0:T(8,128)(2,1)S(1)}, u32[]{:S(2)}, u32[]{:S(2)}) collective-permute-start(bf16[6,32,128]{2,1,0:T(8,128)(2,1)S(1)} %get-tuple-element.26), channel_id=1, source_target_pairs={{16,0},{32,16},{48,32},{64,48},{80,64},{96,80},{112,96},{128,112},... | collective-permute-start | bytes 147464 | tf_op jit(solution)/shard_map/ppermute | solution.py:275
  57.8 3.9 %collective-permute-start = (bf16[6,32,128]{2,1,0:T(8,128)(2,1)S(1)}, bf16[6,32,128]{2,1,0:T(8,128)(2,1)S(1)}, u32[]{:S(2)}, u32[]{:S(2)}) collective-permute-start(bf16[6,32,128]{2,1,0:T(8,128)(2,1)S(1)} %get-tuple-element.25), channel_id=1, source_target_pairs={{0,16},{16,32},{32,48},{48,64},{64,80},{80,96},{96,112},{112,128},... | collective-permute-start | bytes 147464 | tf_op jit(solution)/shard_map/ppermute | solution.py:275
  61.8 0.1 collective-permute-done.1
  61.9 4.0 %collective-permute-done = bf16[6,32,128]{2,1,0:T(8,128)(2,1)S(1)} collective-permute-done((bf16[6,32,128]{2,1,0:T(8,128)(2,1)S(1)}, bf16[6,32,128]{2,1,0:T(8,128)(2,1)S(1)}, u32[]{:S(2)}, u32[]{:S(2)}) %collective-permute-start) | collective-permute-done | bytes 49184 | tf_op jit(solution)/shard_map/ppermute | solution.py:275
  66.0 3.5 %collective-permute-start.2 = (bf16[16,32,128]{2,1,0:T(8,128)(2,1)S(1)}, bf16[16,32,128]{2,1,0:T(8,128)(2,1)S(1)}, u32[]{:S(2)}, u32[]{:S(2)}) collective-permute-start(bf16[16,32,128]{2,1,0:T(8,128)(2,1)S(1)} %get-tuple-element.22), channel_id=1, source_target_pairs={{0,2},{2,4},{4,6},{6,8},{8,10},{10,12},{12,14},{1,3},{3,5},{5,7},{... | collective-permute-start | bytes 393224 | tf_op jit(solution)/shard_map/ppermute | solution.py:275
  69.5 1.3 collective-permute-start.3
  70.8 1.2 collective-permute-done.2
  72.1 4.3 %collective-permute-done.3 = bf16[16,32,128]{2,1,0:T(8,128)(2,1)S(1)} collective-permute-done((bf16[16,32,128]{2,1,0:T(8,128)(2,1)S(1)}, bf16[16,32,128]{2,1,0:T(8,128)(2,1)S(1)}, u32[]{:S(2)}, u32[]{:S(2)}) %collective-permute-start.3) | collective-permute-done | bytes 131104 | tf_op jit(solution)/shard_map/ppermute | solution.py:275
  76.4 2.4 %all-gather = bf16[104,32,128]{2,1,0:T(8,128)(2,1)S(1)} all-gather(bf16[52,32,128]{2,1,0:T(8,128)(2,1)S(1)} %constant_dynamic-update-slice_fusion), channel_id=2, replica_groups=mesh['dom'=32,'slab'=8,'chan'=2] {'chan'}, dimensions={0}, use_global_device_ids=true | all-gather | bytes 1277952 | tf_op jit(solution)/shard_map/all_gather | solution.py:338
  78.8 2.6 %conv_layer.1 = (bf16[32,2,2,128]{3,2,1,0:T(2,128)(2,1)}, bf16[8,192,128]{2,1,0:T(8,128)(2,1)S(1)}) custom-call(s32[1]{0:T(128)} %bitcast.chan, bf16[2,52,32,128]{3,2,1,0:T(8,128)(2,1)S(1)} %bitcast.32, bf16[3,192,192]{2,1,0:T(8,128)(2,1)S(1)} %reshape.41.wf, bf16[3,96,192]{2,1,0:T(8,128)(2,1)S(1)} %reshape.42.wb), custom_call_target="tpu_custom_call" | custom-call | tf_op jit(solution)/shard_map/conv_layer/pallas_call | solution.py:253
  81.5 0.0 copy-start
  81.5 0.0 copy-start.2
  81.5 18.2 %all_to_all.26 = bf16[8,192,128]{2,1,0:T(8,128)(2,1)S(1)} all-to-all(bf16[8,192,128]{2,1,0:T(8,128)(2,1)S(1)} %get-tuple-element.17), channel_id=1, replica_groups={{0,16,32,48,64,80,96,112},{128,144,160,176,192,208,224,240},{256,272,28..., dimensions={0} | all-to-all | bytes 786432 | tf_op jit(solution)/shard_map/all_to_all | solution.py:316
  99.6 0.7 slice.49
  100.4 0.0 all-gather.3.cloned.1.call-update
  100.4 23.1 %all_to_all.27 = bf16[64,16,128]{2,1,0:T(8,128)(2,1)S(1)} all-to-all(bf16[64,16,128]{2,1,0:T(8,128)(2,1)S(1)} %bitcast.39), channel_id=1, replica_groups={{0,1,2,3,4,5,6,7,8,9,10,11,12,13,14,15,128,129,130,131,132,133,134,135,..., dimensions={0} | all-to-all | bytes 524288 | tf_op jit(solution)/shard_map/all_to_all | solution.py:316
  123.6 0.7 broadcast_in_dim.27
  124.4 4.9 %all-to-all-start.4 = ((bf16[32,2,16,128]{3,2,1,0:T(8,128)(2,1)}), bf16[32,2,16,128]{3,2,1,0:T(8,128)(2,1)S(1)}, u32[]{:S(2)}, u32[]{:S(2)}) async-start(bf16[32,2,16,128]{3,2,1,0:T(8,128)(2,1)} %broadcast_in_dim.27), calls=%async_computation.4 | async-start | bytes 524288 | tf_op jit(solution)/shard_map/all_to_all | solution.py:316
  129.3 0.0 all-gather.3.cloned.1.call-done.columns
  129.3 0.0 copy-done
  129.3 0.0 copy-done.2
  129.3 0.0 copy-start.1
  129.3 1.2 copy-done.1
  130.6 4.0 %spread.1 = bf16[32,8192]{1,0:T(8,128)(2,1)} custom-call(s32[64]{0:T(128)S(1)} %copy-done.2, bf16[128,32,128]{2,1,0:T(8,128)(2,1)S(1)} %copy-done.1, bf16[64,128,128]{2,1,0:T(8,128)(2,1)S(1)} %copy-done), custom_call_target="tpu_custom_call" | custom-call | flops 67108864 | bytes 6291456 | tf_op jit(solution)/shard_map/spread/pallas_call | solution.py:100
  134.6 5.5 %all-to-all-done.4.gathered = bf16[32,2,16,128]{3,2,1,0:T(8,128)(2,1)S(1)} async-done(((bf16[32,2,16,128]{3,2,1,0:T(8,128)(2,1)}), bf16[32,2,16,128]{3,2,1,0:T(8,128)(2,1)S(1)}, u32[]{:S(2)}, u32[]{:S(2)}) %all-to-all-start.4) | async-done | bytes 262176 | tf_op jit(solution)/shard_map/all_to_all | solution.py:316
  140.1 1.2 unpack.1
  (23 shorter events, 0.3 us)
Async XLA Ops:
  16.0 29.2 %copy-start.3 = (bf16[27,64,64]{2,1,0:T(8,128)(2,1)S(1)}, bf16[27,64,64]{2,1,0:T(8,128)(2,1)}, u32[]{:S(2)}) copy-start(bf16[27,64,64]{2,1,0:T(8,128)(2,1)} %param.12) | copy-start | bytes 663556
  35.2 20.6 %all-to-all-start.1 = ((bf16[32,32,128]{2,1,0:T(8,128)(2,1)}), bf16[32,32,128]{2,1,0:T(8,128)(2,1)S(1)}, u32[]{:S(2)}, u32[]{:S(2)}) async-start(bf16[32,32,128]{2,1,0:T(8,128)(2,1)} %reduce_sum.45), calls=%async_computation.1 | async-start | bytes 524288 | tf_op jit(solution)/shard_map/all_to_all | solution.py:316
  45.1 84.2 %all-gather.3.cloned.1.call-start = ((), (), s32[]{:S(2)}) async-start(), calls=%async_computation.5 | async-start | bytes 1310720 | tf_op jit(solution)/shard_map/all_gather | solution.py:344
  46.2 2.7 %copy-start.4 = (bf16[32,2,2,128]{3,2,1,0:T(2,128)(2,1)S(1)}, bf16[32,2,2,128]{3,2,1,0:T(2,128)(2,1)}, u32[]{:S(2)}) copy-start(bf16[32,2,2,128]{3,2,1,0:T(2,128)(2,1)} %param.13) | copy-start | bytes 98308
  55.9 6.0 %collective-permute-start.1 = (bf16[6,32,128]{2,1,0:T(8,128)(2,1)S(1)}, bf16[6,32,128]{2,1,0:T(8,128)(2,1)S(1)}, u32[]{:S(2)}, u32[]{:S(2)}) collective-permute-start(bf16[6,32,128]{2,1,0:T(8,128)(2,1)S(1)} %get-tuple-element.26), channel_id=1, source_target_pairs={{16,0},{32,16},{48,32},{64,48},{80,64},{96,80},{112,96},{128,112},... | collective-permute-start | bytes 147464 | tf_op jit(solution)/shard_map/ppermute | solution.py:275
  57.8 8.1 %collective-permute-start = (bf16[6,32,128]{2,1,0:T(8,128)(2,1)S(1)}, bf16[6,32,128]{2,1,0:T(8,128)(2,1)S(1)}, u32[]{:S(2)}, u32[]{:S(2)}) collective-permute-start(bf16[6,32,128]{2,1,0:T(8,128)(2,1)S(1)} %get-tuple-element.25), channel_id=1, source_target_pairs={{0,16},{16,32},{32,48},{48,64},{64,80},{80,96},{96,112},{112,128},... | collective-permute-start | bytes 147464 | tf_op jit(solution)/shard_map/ppermute | solution.py:275
  66.0 6.0 %collective-permute-start.2 = (bf16[16,32,128]{2,1,0:T(8,128)(2,1)S(1)}, bf16[16,32,128]{2,1,0:T(8,128)(2,1)S(1)}, u32[]{:S(2)}, u32[]{:S(2)}) collective-permute-start(bf16[16,32,128]{2,1,0:T(8,128)(2,1)S(1)} %get-tuple-element.22), channel_id=1, source_target_pairs={{0,2},{2,4},{4,6},{6,8},{8,10},{10,12},{12,14},{1,3},{3,5},{5,7},{... | collective-permute-start | bytes 393224 | tf_op jit(solution)/shard_map/ppermute | solution.py:275
  69.5 6.9 %collective-permute-start.3 = (bf16[16,32,128]{2,1,0:T(8,128)(2,1)S(1)}, bf16[16,32,128]{2,1,0:T(8,128)(2,1)S(1)}, u32[]{:S(2)}, u32[]{:S(2)}) collective-permute-start(bf16[16,32,128]{2,1,0:T(8,128)(2,1)S(1)} %get-tuple-element.21), channel_id=1, source_target_pairs={{2,0},{4,2},{6,4},{8,6},{10,8},{12,10},{14,12},{3,1},{5,3},{7,5},{... | collective-permute-start | bytes 393224 | tf_op jit(solution)/shard_map/ppermute | solution.py:275
  81.5 47.9 %copy-start = (bf16[64,128,128]{2,1,0:T(8,128)(2,1)S(1)}, bf16[64,128,128]{2,1,0:T(8,128)(2,1)}, u32[]{:S(2)}) copy-start(bf16[64,128,128]{2,1,0:T(8,128)(2,1)} %get-tuple-element.18.blocks) | copy-start | bytes 6291460
  81.5 47.9 %copy-start.2 = (s32[64]{0:T(128)S(1)}, s32[64]{0:T(128)}, u32[]{:S(2)}) copy-start(s32[64]{0:T(128)} %target.3) | copy-start | bytes 772
  124.4 15.7 %all-to-all-start.4 = ((bf16[32,2,16,128]{3,2,1,0:T(8,128)(2,1)}), bf16[32,2,16,128]{3,2,1,0:T(8,128)(2,1)S(1)}, u32[]{:S(2)}, u32[]{:S(2)}) async-start(bf16[32,2,16,128]{3,2,1,0:T(8,128)(2,1)} %broadcast_in_dim.27), calls=%async_computation.4 | async-start | bytes 524288 | tf_op jit(solution)/shard_map/all_to_all | solution.py:316
  129.3 1.2 copy-start.1
Sparse Core Ops, SparseCore 0:
  100.5 27.2 all-gather.2

commit v5 on v4

--- a/solution.py
+++ b/solution.py
@@ -7,7 +7,8 @@
 from jax.experimental.pallas import tpu as pltpu
 from jax.sharding import PartitionSpec as P
 
-GROUP = 8
+POOL_GROUP = 32
+SPREAD_GROUP = 16
 POOL_VMEM = 60 * 1024 * 1024
 VMEM_LIMIT = 16 * 1024 * 1024
 CHUNK = 16
@@ -29,16 +30,23 @@
     span = cells.shape[1]
     position = step * span + lax.broadcasted_iota(jnp.int32, cells.shape, 1)
     masked = jnp.where(position < live[0], weights[...], 0.0)
-    cell = cells[...]
+    cell = cells[...].astype(jnp.float32)
     depth_ids = lax.broadcasted_iota(jnp.int32, (depth, tile), 0)
+    depth_ids = depth_ids.astype(jnp.float32).astype(jnp.bfloat16)
+
+    def spread_rows(row):
+        return jnp.broadcast_to(row, (depth, tile)).astype(jnp.bfloat16)
+
     for t in range(span // tile):
         cols = slice(t * tile, (t + 1) * tile)
-        total = jnp.zeros((depth, tile), jnp.float32)
+        terms = []
         for k in range(cells.shape[0]):
-            total = total + jnp.where(
-                cell[k : k + 1, cols] == depth_ids, masked[k : k + 1, cols], 0.0
-            )
-        block = total.astype(jnp.bfloat16)
+            weight = spread_rows(masked[k : k + 1, cols])
+            here = spread_rows(cell[k : k + 1, cols]) == depth_ids
+            terms.append(jnp.where(here, weight, jnp.zeros_like(weight)))
+        while len(terms) > 1:
+            terms = [one + two for one, two in zip(terms[::2], terms[1::2])]
+        block = terms[0]
         blocks[t] = block
         part = lax.dot_general(
             feats[:, cols], block, (((1,), (1,)), ((), ())), preferred_element_type=jnp.float32
@@ -56,7 +64,7 @@
     half = feats.shape[0]
     tiles = target.shape[0]
     tile = npts // tiles
-    group = min(GROUP, tiles)
+    group = min(POOL_GROUP, tiles)
     span = group * tile
     smem = pl.BlockSpec(memory_space=pltpu.SMEM)
     return pl.pallas_call(
@@ -84,33 +92,42 @@
     )(target, live, cells, weights, feats)
 
 
-def spread_kernel(target, columns, blocks, out):
+def spread_kernel(target, place, *refs):
+    *parts, blocks, out, columns = refs
     step = pl.program_id(0)
     group, _, tile = blocks.shape
+    count = parts[0].shape[0]
+
+    @pl.when(step == 0)
+    def _():
+        for shift, part in enumerate(parts):
+            source = lax.rem(place[0] + (len(parts) - shift), len(parts))
+            columns[pl.ds(source * count, count)] = part[...]
+
     for t in range(group):
         column = target[step * group + t]
-        part = jnp.dot(columns[column], blocks[t], preferred_element_type=jnp.float32)
-        out[:, t * tile : (t + 1) * tile] = part.astype(jnp.bfloat16)
-
-
-def spread(target, columns, blocks):
+        value = jnp.dot(columns[column], blocks[t], preferred_element_type=jnp.float32)
+        out[:, t * tile : (t + 1) * tile] = value.astype(jnp.bfloat16)
+
+
+def spread(target, place, parts, blocks):
     tiles, depth, tile = blocks.shape
-    half = columns.shape[1]
-    group = min(GROUP, tiles)
+    count, half, _ = parts[0].shape
+    group = min(SPREAD_GROUP, tiles)
+    smem = pl.BlockSpec(memory_space=pltpu.SMEM)
     return pl.pallas_call(
         spread_kernel,
         grid=(tiles // group,),
-        in_specs=[
-            pl.BlockSpec(memory_space=pltpu.SMEM),
-            pl.BlockSpec(columns.shape, lambda i: (0, 0, 0)),
-            pl.BlockSpec((group, depth, tile), lambda i: (i, 0, 0)),
-        ],
+        in_specs=[smem, smem]
+        + [pl.BlockSpec(part.shape, lambda i: (0, 0, 0)) for part in parts]
+        + [pl.BlockSpec((group, depth, tile), lambda i: (i, 0, 0))],
         out_specs=pl.BlockSpec((half, group * tile), lambda i: (0, i)),
         out_shape=jax.ShapeDtypeStruct((half, tiles * tile), jnp.bfloat16),
+        scratch_shapes=[pltpu.VMEM((count * len(parts), half, depth), jnp.bfloat16)],
         compiler_params=pltpu.CompilerParams(vmem_limit_bytes=VMEM_LIMIT),
         cost_estimate=cost(2 * half * tiles * tile * depth, 6 * tiles * tile * depth),
         name="spread",
-    )(target, columns, blocks)
+    )(target, place, *parts, blocks)
 
 
 def unpack_kernel(inner, gathered, out):
@@ -290,6 +307,7 @@
     n_dom, n_slab = lax.axis_size("dom"), lax.axis_size("slab")
     width = xsize * ysize
     chan = lax.axis_index("chan").astype(jnp.int32)
+    place = (lax.axis_index("dom") // min(8, n_dom // 2)).astype(jnp.int32)
     scale = float(width * depth * n_dom * n_slab) ** (-0.5)
 
     blocks, send = pool(
@@ -341,7 +359,12 @@
     latent, message = conv_layer(chan[None], grid, wf, wb, inner, outer * each)
     message = exchange(message, "dom", same_x)
     columns = message[:, : width * half].reshape(inner * width, half, depth)
-    columns = lax.all_gather(columns, "dom", axis=0, tiled=True, axis_index_groups=same_z)
+    columns = [columns] + [
+        lax.ppermute(
+            columns, "dom", [(g[x], g[(x + shift) % outer]) for g in same_z for x in range(outer)]
+        )
+        for shift in range(1, outer)
+    ]
 
     peers = 2 * n_slab
     same_z_all = [
@@ -355,8 +378,9 @@
         kgrad.reshape(outer * peers, each * CHUNK, depth), ("dom", "slab", "chan"), same_z_all
     )
     kgrad = (total(kgrad, outer * n_slab) * scale).astype(jnp.bfloat16)
+    kgrad, columns = lax.optimization_barrier((kgrad, columns))
     kgrad = exchange(jnp.broadcast_to(kgrad[None], (n_dom,) + kgrad.shape), "dom")
-    feature_grad = spread(tile_target, columns, blocks)
+    feature_grad = spread(tile_target, place[None], columns, blocks)
     kgrad, feature_grad = lax.optimization_barrier((kgrad, feature_grad))
     kernel_grad = unpack(kgrad, 27, full, inner)
     return (latent, feature_grad, kernel_grad)

time: 150 us -> 142 us (0.947)
  blocking collectives: 62 us -> 38.8 us
  starting transfers between devices: 25.5 us -> 46 us
  waiting for transfers between devices: 22.1 us -> 35.5 us
  between operations: 14.9 us -> 1.56 us
  Pallas kernels: 16 us -> 11.5 us
    all_to_all x3 -> x2, blocking collectives: 59.6 us -> 36.3 us  [exchange(): lax.all_to_all(value, axis, split_axis=0, concat_axis=0, tiled=True, axis...]
    all_to_all x2 -> x3, starting transfers between devices: 14.9 us -> 26.8 us  [exchange(): lax.all_to_all(value, axis, split_axis=0, concat_axis=0, tiled=True, axis...]
    ppermute x0 -> x3, starting transfers between devices: none -> 8.55 us  [body(): lax.ppermute(columns, 'dom', [(g[x], g[(x + shift) % outer]) for g in sam...]
    ppermute x0 -> x3, waiting for transfers between devices: none -> 8.38 us  [body(): lax.ppermute(columns, 'dom', [(g[x], g[(x + shift) % outer]) for g in sam...]
    all_to_all x2 -> x3, waiting for transfers between devices: 12.4 us -> 17.4 us  [exchange(): lax.all_to_all(value, axis, split_axis=0, concat_axis=0, tiled=True, axis...]
    pallas_call x1, Pallas kernels: 8.17 us -> 4.99 us  [pool(): pl.pallas_call(pool_kernel, grid=(tiles // group,), in_specs=[smem, smem,...]
  transfers between devices with their start and end apart: 7 -> 10, of which waited for: 6 -> 10; matrix products, arithmetic and copies ran while one was open for 3% -> 3% of each run, Pallas kernels for 3% -> 2%
where the time goes in v5:
time: 142 us; the launch traced here: 140 us
  starting transfers between devices  46 us (32%)
  blocking collectives  38.8 us (27%)
  waiting for transfers between devices  35.5 us (25%)
  Pallas kernels  11.5 us (8%)
  local copies, waits for them, and re-layouts  5.3 us (4%)
  between operations  1.56 us (1%)
    all_to_all x2, blocking collectives, exchange(): lax.all_to_all(value, axis, split_axis=0, concat_axis=0, tiled=True, axis...  36.3 us
    all_to_all x3, starting transfers between devices, exchange(): lax.all_to_all(value, axis, split_axis=0, concat_axis=0, tiled=True, axis...  26.8 us
    all_to_all x3, waiting for transfers between devices, exchange(): lax.all_to_all(value, axis, split_axis=0, concat_axis=0, tiled=True, axis...  17.4 us
    ppermute x4, starting transfers between devices, neighbours(): return (lax.ppermute(last, axis, up), lax.ppermute(first, axis, down))  10.6 us
    ppermute x4, waiting for transfers between devices, neighbours(): return (lax.ppermute(last, axis, up), lax.ppermute(first, axis, down))  9.64 us
    ppermute x3, starting transfers between devices, body(): lax.ppermute(columns, 'dom', [(g[x], g[(x + shift) % outer]) for g in sam...  8.55 us
    ppermute x3, waiting for transfers between devices, body(): lax.ppermute(columns, 'dom', [(g[x], g[(x + shift) % outer]) for g in sam...  8.38 us
    pallas_call x1, Pallas kernels, pool(): pl.pallas_call(pool_kernel, grid=(tiles // group,), in_specs=[smem, smem,...  4.99 us
  transfers between devices with their start and end apart: 10, of which 10 were waited for; matrix products, arithmetic and copies ran while one was open for 3% of the time, Pallas kernels for 2%

profile of v5, /device:TPU:6, one launch (start us, length us, event | category | flops | bytes accessed | tf_op | source)
XLA Modules:
  0.0 139.6 jit_solution(15232462314697398905)
XLA Ops:
  1.3 5.0 %pool.1 = (bf16[64,128,128]{2,1,0:T(8,128)(2,1)}, bf16[128,32,128]{2,1,0:T(8,128)(2,1)}) custom-call(s32[64]{0:T(128)} %target.3, s32[1]{0:T(128)S(6)} %copy.41.live, s32[8,8192]{1,0:T(8,128)} %cells.1, f32[8,8192]{1,0:T(8,128)} %weights.1, bf16[32,8192]{1,0:T(8,128)(2,1)} %feats.1), custom_call_target="tpu_custom_call" | custom-call | flops 67108864 | bytes 25165824 | tf_op jit(solution)/shard_map/pool/pallas_call | solution.py:70
  6.3 0.0 copy-start.2
  6.3 18.3 %all_to_all.25 = bf16[128,32,128]{2,1,0:T(8,128)(2,1)S(1)} all-to-all(bf16[128,32,128]{2,1,0:T(8,128)(2,1)} %get-tuple-element.17), channel_id=1, replica_groups={{0,128,256,384},{16,144,272,400},{32,160,288,416},{48,176,304,432},{64,..., dimensions={0} | all-to-all | bytes 2097152 | tf_op jit(solution)/shard_map/all_to_all | solution.py:334
  24.6 0.9 reduce_sum.45
  25.5 10.0 %all-to-all-start.1 = ((bf16[32,32,128]{2,1,0:T(8,128)(2,1)}), bf16[32,32,128]{2,1,0:T(8,128)(2,1)S(1)}, u32[]{:S(2)}, u32[]{:S(2)}) async-start(bf16[32,32,128]{2,1,0:T(8,128)(2,1)} %reduce_sum.45), calls=%async_computation.1 | async-start | bytes 524288 | tf_op jit(solution)/shard_map/all_to_all | solution.py:334
  35.4 0.0 copy-done.2
  35.4 1.0 copy.26
  36.4 0.0 copy-start.3
  36.4 0.4 copy.27
  36.8 0.4 reshape.38.wf
  37.2 1.6 %rev.3 = bf16[3,3,3,64,64]{4,1,3,2,0:T(4,128)(2,1)S(1)} reverse(bf16[3,3,3,64,64]{4,1,3,2,0:T(4,128)(2,1)S(1)} %copy.27), dimensions={0,1} | reverse | bytes 442368 | tf_op jit(solution)/shard_map/rev | solution.py:325
  38.8 0.1 dynamic-slice_bitcast_fusion
  38.9 0.2 reshape.39.wb
  39.2 0.0 copy-done.3
  39.2 6.9 %all-to-all-done.1 = bf16[32,32,128]{2,1,0:T(8,128)(2,1)S(1)} async-done(((bf16[32,32,128]{2,1,0:T(8,128)(2,1)}), bf16[32,32,128]{2,1,0:T(8,128)(2,1)S(1)}, u32[]{:S(2)}, u32[]{:S(2)}) %all-to-all-start.1) | async-done | bytes 262176 | tf_op jit(solution)/shard_map/all_to_all | solution.py:334
  46.2 1.9 %collective-permute-start.1 = (bf16[6,32,128]{2,1,0:T(8,128)(2,1)S(1)}, bf16[6,32,128]{2,1,0:T(8,128)(2,1)S(1)}, u32[]{:S(2)}, u32[]{:S(2)}) collective-permute-start(bf16[6,32,128]{2,1,0:T(8,128)(2,1)S(1)} %get-tuple-element.36), channel_id=1, source_target_pairs={{16,0},{32,16},{48,32},{64,48},{80,64},{96,80},{112,96},{128,112},... | collective-permute-start | bytes 147464 | tf_op jit(solution)/shard_map/ppermute | solution.py:292
  48.1 3.9 %collective-permute-start = (bf16[6,32,128]{2,1,0:T(8,128)(2,1)S(1)}, bf16[6,32,128]{2,1,0:T(8,128)(2,1)S(1)}, u32[]{:S(2)}, u32[]{:S(2)}) collective-permute-start(bf16[6,32,128]{2,1,0:T(8,128)(2,1)S(1)} %get-tuple-element.35), channel_id=1, source_target_pairs={{0,16},{16,32},{32,48},{48,64},{64,80},{80,96},{96,112},{112,128},... | collective-permute-start | bytes 147464 | tf_op jit(solution)/shard_map/ppermute | solution.py:292
  52.1 0.1 collective-permute-done.1
  52.2 4.0 %collective-permute-done = bf16[6,32,128]{2,1,0:T(8,128)(2,1)S(1)} collective-permute-done((bf16[6,32,128]{2,1,0:T(8,128)(2,1)S(1)}, bf16[6,32,128]{2,1,0:T(8,128)(2,1)S(1)}, u32[]{:S(2)}, u32[]{:S(2)}) %collective-permute-start) | collective-permute-done | bytes 49184 | tf_op jit(solution)/shard_map/ppermute | solution.py:292
  56.3 3.5 %collective-permute-start.2 = (bf16[16,32,128]{2,1,0:T(8,128)(2,1)S(1)}, bf16[16,32,128]{2,1,0:T(8,128)(2,1)S(1)}, u32[]{:S(2)}, u32[]{:S(2)}) collective-permute-start(bf16[16,32,128]{2,1,0:T(8,128)(2,1)S(1)} %get-tuple-element.32), channel_id=1, source_target_pairs={{0,2},{2,4},{4,6},{6,8},{8,10},{10,12},{12,14},{1,3},{3,5},{5,7},{... | collective-permute-start | bytes 393224 | tf_op jit(solution)/shard_map/ppermute | solution.py:292
  59.8 1.3 collective-permute-start.3
  61.1 1.2 collective-permute-done.2
  62.4 4.3 %collective-permute-done.3 = bf16[16,32,128]{2,1,0:T(8,128)(2,1)S(1)} collective-permute-done((bf16[16,32,128]{2,1,0:T(8,128)(2,1)S(1)}, bf16[16,32,128]{2,1,0:T(8,128)(2,1)S(1)}, u32[]{:S(2)}, u32[]{:S(2)}) %collective-permute-start.3) | collective-permute-done | bytes 131104 | tf_op jit(solution)/shard_map/ppermute | solution.py:292
  66.7 2.4 %all-gather = bf16[104,32,128]{2,1,0:T(8,128)(2,1)S(1)} all-gather(bf16[52,32,128]{2,1,0:T(8,128)(2,1)S(1)} %constant_dynamic-update-slice_fusion), channel_id=2, replica_groups=mesh['dom'=32,'slab'=8,'chan'=2] {'chan'}, dimensions={0}, use_global_device_ids=true | all-gather | bytes 1277952 | tf_op jit(solution)/shard_map/all_gather | solution.py:356
  69.1 0.0 copy-start
  69.1 0.0 copy-start.1
  69.1 2.6 %conv_layer.1 = (bf16[32,2,2,128]{3,2,1,0:T(2,128)(2,1)}, bf16[8,192,128]{2,1,0:T(8,128)(2,1)S(1)}) custom-call(s32[1]{0:T(128)} %bitcast.chan, bf16[2,52,32,128]{3,2,1,0:T(8,128)(2,1)S(1)} %bitcast.33, bf16[3,192,192]{2,1,0:T(8,128)(2,1)S(1)} %reshape.38.wf, bf16[3,96,192]{2,1,0:T(8,128)(2,1)S(1)} %reshape.39.wb), custom_call_target="tpu_custom_call" | custom-call | tf_op jit(solution)/shard_map/conv_layer/pallas_call | solution.py:270
  71.7 18.0 %all_to_all.26 = bf16[8,192,128]{2,1,0:T(8,128)(2,1)S(1)} all-to-all(bf16[8,192,128]{2,1,0:T(8,128)(2,1)S(1)} %get-tuple-element.22), channel_id=1, replica_groups={{0,16,32,48,64,80,96,112},{128,144,160,176,192,208,224,240},{256,272,28..., dimensions={0} | all-to-all | bytes 786432 | tf_op jit(solution)/shard_map/all_to_all | solution.py:334
  89.8 0.7 broadcast_in_dim.29
  90.5 11.8 %all-to-all-start.3 = ((bf16[64,16,128]{2,1,0:T(8,128)(2,1)}), bf16[64,16,128]{2,1,0:T(8,128)(2,1)S(1)}, u32[]{:S(2)}, u32[]{:S(2)}) async-start(bf16[64,16,128]{2,1,0:T(8,128)(2,1)} %bitcast.17), calls=%async_computation.3 | async-start | bytes 524288 | tf_op jit(solution)/shard_map/all_to_all | solution.py:334
  102.3 2.2 %collective-permute-start.4 = (bf16[32,32,128]{2,1,0:T(8,128)(2,1)S(1)}, bf16[32,32,128]{2,1,0:T(8,128)(2,1)S(1)}, u32[]{:S(2)}, u32[]{:S(2)}) collective-permute-start(bf16[32,32,128]{2,1,0:T(8,128)(2,1)S(1)} %bitcast.34), channel_id=1, source_target_pairs={{0,128},{128,256},{256,384},{384,0},{16,144},{144,272},{272,400},{... | collective-permute-start | bytes 786440 | tf_op jit(solution)/shard_map/ppermute | solution.py:363
  104.5 4.5 %collective-permute-start.5 = (bf16[32,32,128]{2,1,0:T(8,128)(2,1)S(1)}, bf16[32,32,128]{2,1,0:T(8,128)(2,1)S(1)}, u32[]{:S(2)}, u32[]{:S(2)}) collective-permute-start(bf16[32,32,128]{2,1,0:T(8,128)(2,1)S(1)} %bitcast.35), channel_id=1, source_target_pairs={{0,256},{128,384},{256,0},{384,128},{16,272},{144,400},{272,16},{4... | collective-permute-start | bytes 786440 | tf_op jit(solution)/shard_map/ppermute | solution.py:363
  109.0 1.9 %collective-permute-start.6 = (bf16[32,32,128]{2,1,0:T(8,128)(2,1)S(1)}, bf16[32,32,128]{2,1,0:T(8,128)(2,1)S(1)}, u32[]{:S(2)}, u32[]{:S(2)}) collective-permute-start(bf16[32,32,128]{2,1,0:T(8,128)(2,1)S(1)} %bitcast.36), channel_id=1, source_target_pairs={{0,384},{128,0},{256,128},{384,256},{16,400},{144,16},{272,144},{4... | collective-permute-start | bytes 786440 | tf_op jit(solution)/shard_map/ppermute | solution.py:363
  110.9 3.0 %all-to-all-done.3 = bf16[64,16,128]{2,1,0:T(8,128)(2,1)S(1)} async-done(((bf16[64,16,128]{2,1,0:T(8,128)(2,1)}), bf16[64,16,128]{2,1,0:T(8,128)(2,1)S(1)}, u32[]{:S(2)}, u32[]{:S(2)}) %all-to-all-start.3) | async-done | bytes 262176 | tf_op jit(solution)/shard_map/all_to_all | solution.py:334
  113.9 1.3 collective-permute-done.4.refs_1_
  115.2 2.2 %collective-permute-done.5.refs_2_ = bf16[32,32,128]{2,1,0:T(8,128)(2,1)S(1)} collective-permute-done((bf16[32,32,128]{2,1,0:T(8,128)(2,1)S(1)}, bf16[32,32,128]{2,1,0:T(8,128)(2,1)S(1)}, u32[]{:S(2)}, u32[]{:S(2)}) %collective-permute-start.5) | collective-permute-done | bytes 262176 | tf_op jit(solution)/shard_map/ppermute | solution.py:363
  117.4 4.9 %collective-permute-done.6.refs_3_ = bf16[32,32,128]{2,1,0:T(8,128)(2,1)S(1)} collective-permute-done((bf16[32,32,128]{2,1,0:T(8,128)(2,1)S(1)}, bf16[32,32,128]{2,1,0:T(8,128)(2,1)S(1)}, u32[]{:S(2)}, u32[]{:S(2)}) %collective-permute-start.6) | collective-permute-done | bytes 262176 | tf_op jit(solution)/shard_map/ppermute | solution.py:363
  122.3 0.7 broadcast_in_dim.30
  123.1 5.1 %all-to-all-start.4 = ((bf16[32,2,16,128]{3,2,1,0:T(8,128)(2,1)}), bf16[32,2,16,128]{3,2,1,0:T(8,128)(2,1)S(1)}, u32[]{:S(2)}, u32[]{:S(2)}) async-start(bf16[32,2,16,128]{3,2,1,0:T(8,128)(2,1)} %broadcast_in_dim.30), calls=%async_computation.4 | async-start | bytes 524288 | tf_op jit(solution)/shard_map/all_to_all | solution.py:334
  128.1 0.0 copy-done
  128.2 0.0 copy-done.1
  128.2 2.8 %spread.1 = bf16[32,8192]{1,0:T(8,128)(2,1)} custom-call(s32[64]{0:T(128)S(1)} %copy-done.1, s32[1]{0:T(128)} %bitcast.20.place, bf16[32,32,128]{2,1,0:T(8,128)(2,1)S(1)} %bitcast.37, bf16[32,32,128]{2,1,0:T(8,128)(2,1)S(1)} %collective-permute-done.4.refs_1_, bf16[32,32,128]{2,1,0:T(8,128)(2,1)S(1)} %collective-permute-done.5.refs_2_, ...), custom_call_target="tpu_custom_call" | custom-call | flops 67108864 | bytes 6291456 | tf_op jit(solution)/shard_map/spread/pallas_call | solution.py:118
  130.9 7.5 %all-to-all-done.4.gathered = bf16[32,2,16,128]{3,2,1,0:T(8,128)(2,1)S(1)} async-done(((bf16[32,2,16,128]{3,2,1,0:T(8,128)(2,1)}), bf16[32,2,16,128]{3,2,1,0:T(8,128)(2,1)S(1)}, u32[]{:S(2)}, u32[]{:S(2)}) %all-to-all-start.4) | async-done | bytes 262176 | tf_op jit(solution)/shard_map/all_to_all | solution.py:334
  138.5 1.2 unpack.1
  (23 shorter events, 0.3 us)
Async XLA Ops:
  6.3 29.2 %copy-start.2 = (bf16[27,64,64]{2,1,0:T(8,128)(2,1)S(1)}, bf16[27,64,64]{2,1,0:T(8,128)(2,1)}, u32[]{:S(2)}) copy-start(bf16[27,64,64]{2,1,0:T(8,128)(2,1)} %param.12) | copy-start | bytes 663556
  25.5 20.6 %all-to-all-start.1 = ((bf16[32,32,128]{2,1,0:T(8,128)(2,1)}), bf16[32,32,128]{2,1,0:T(8,128)(2,1)S(1)}, u32[]{:S(2)}, u32[]{:S(2)}) async-start(bf16[32,32,128]{2,1,0:T(8,128)(2,1)} %reduce_sum.45), calls=%async_computation.1 | async-start | bytes 524288 | tf_op jit(solution)/shard_map/all_to_all | solution.py:334
  36.4 2.7 %copy-start.3 = (bf16[32,2,2,128]{3,2,1,0:T(2,128)(2,1)S(1)}, bf16[32,2,2,128]{3,2,1,0:T(2,128)(2,1)}, u32[]{:S(2)}) copy-start(bf16[32,2,2,128]{3,2,1,0:T(2,128)(2,1)} %param.13) | copy-start | bytes 98308
  46.2 6.0 %collective-permute-start.1 = (bf16[6,32,128]{2,1,0:T(8,128)(2,1)S(1)}, bf16[6,32,128]{2,1,0:T(8,128)(2,1)S(1)}, u32[]{:S(2)}, u32[]{:S(2)}) collective-permute-start(bf16[6,32,128]{2,1,0:T(8,128)(2,1)S(1)} %get-tuple-element.36), channel_id=1, source_target_pairs={{16,0},{32,16},{48,32},{64,48},{80,64},{96,80},{112,96},{128,112},... | collective-permute-start | bytes 147464 | tf_op jit(solution)/shard_map/ppermute | solution.py:292
  48.1 8.1 %collective-permute-start = (bf16[6,32,128]{2,1,0:T(8,128)(2,1)S(1)}, bf16[6,32,128]{2,1,0:T(8,128)(2,1)S(1)}, u32[]{:S(2)}, u32[]{:S(2)}) collective-permute-start(bf16[6,32,128]{2,1,0:T(8,128)(2,1)S(1)} %get-tuple-element.35), channel_id=1, source_target_pairs={{0,16},{16,32},{32,48},{48,64},{64,80},{80,96},{96,112},{112,128},... | collective-permute-start | bytes 147464 | tf_op jit(solution)/shard_map/ppermute | solution.py:292
  56.3 6.0 %collective-permute-start.2 = (bf16[16,32,128]{2,1,0:T(8,128)(2,1)S(1)}, bf16[16,32,128]{2,1,0:T(8,128)(2,1)S(1)}, u32[]{:S(2)}, u32[]{:S(2)}) collective-permute-start(bf16[16,32,128]{2,1,0:T(8,128)(2,1)S(1)} %get-tuple-element.32), channel_id=1, source_target_pairs={{0,2},{2,4},{4,6},{6,8},{8,10},{10,12},{12,14},{1,3},{3,5},{5,7},{... | collective-permute-start | bytes 393224 | tf_op jit(solution)/shard_map/ppermute | solution.py:292
  59.8 6.9 %collective-permute-start.3 = (bf16[16,32,128]{2,1,0:T(8,128)(2,1)S(1)}, bf16[16,32,128]{2,1,0:T(8,128)(2,1)S(1)}, u32[]{:S(2)}, u32[]{:S(2)}) collective-permute-start(bf16[16,32,128]{2,1,0:T(8,128)(2,1)S(1)} %get-tuple-element.31), channel_id=1, source_target_pairs={{2,0},{4,2},{6,4},{8,6},{10,8},{12,10},{14,12},{3,1},{5,3},{7,5},{... | collective-permute-start | bytes 393224 | tf_op jit(solution)/shard_map/ppermute | solution.py:292
  69.1 59.0 %copy-start = (bf16[64,128,128]{2,1,0:T(8,128)(2,1)S(1)}, bf16[64,128,128]{2,1,0:T(8,128)(2,1)}, u32[]{:S(2)}) copy-start(bf16[64,128,128]{2,1,0:T(8,128)(2,1)} %get-tuple-element.28.refs_4_) | copy-start | bytes 6291460
  69.1 59.0 %copy-start.1 = (s32[64]{0:T(128)S(1)}, s32[64]{0:T(128)}, u32[]{:S(2)}) copy-start(s32[64]{0:T(128)} %target.3) | copy-start | bytes 772
  90.5 23.3 %all-to-all-start.3 = ((bf16[64,16,128]{2,1,0:T(8,128)(2,1)}), bf16[64,16,128]{2,1,0:T(8,128)(2,1)S(1)}, u32[]{:S(2)}, u32[]{:S(2)}) async-start(bf16[64,16,128]{2,1,0:T(8,128)(2,1)} %bitcast.17), calls=%async_computation.3 | async-start | bytes 524288 | tf_op jit(solution)/shard_map/all_to_all | solution.py:334
  102.3 12.9 %collective-permute-start.4 = (bf16[32,32,128]{2,1,0:T(8,128)(2,1)S(1)}, bf16[32,32,128]{2,1,0:T(8,128)(2,1)S(1)}, u32[]{:S(2)}, u32[]{:S(2)}) collective-permute-start(bf16[32,32,128]{2,1,0:T(8,128)(2,1)S(1)} %bitcast.34), channel_id=1, source_target_pairs={{0,128},{128,256},{256,384},{384,0},{16,144},{144,272},{272,400},{... | collective-permute-start | bytes 786440 | tf_op jit(solution)/shard_map/ppermute | solution.py:363
  104.5 12.9 %collective-permute-start.5 = (bf16[32,32,128]{2,1,0:T(8,128)(2,1)S(1)}, bf16[32,32,128]{2,1,0:T(8,128)(2,1)S(1)}, u32[]{:S(2)}, u32[]{:S(2)}) collective-permute-start(bf16[32,32,128]{2,1,0:T(8,128)(2,1)S(1)} %bitcast.35), channel_id=1, source_target_pairs={{0,256},{128,384},{256,0},{384,128},{16,272},{144,400},{272,16},{4... | collective-permute-start | bytes 786440 | tf_op jit(solution)/shard_map/ppermute | solution.py:363
  109.0 13.3 %collective-permute-start.6 = (bf16[32,32,128]{2,1,0:T(8,128)(2,1)S(1)}, bf16[32,32,128]{2,1,0:T(8,128)(2,1)S(1)}, u32[]{:S(2)}, u32[]{:S(2)}) collective-permute-start(bf16[32,32,128]{2,1,0:T(8,128)(2,1)S(1)} %bitcast.36), channel_id=1, source_target_pairs={{0,384},{128,0},{256,128},{384,256},{16,400},{144,16},{272,144},{4... | collective-permute-start | bytes 786440 | tf_op jit(solution)/shard_map/ppermute | solution.py:363
  123.1 15.4 %all-to-all-start.4 = ((bf16[32,2,16,128]{3,2,1,0:T(8,128)(2,1)}), bf16[32,2,16,128]{3,2,1,0:T(8,128)(2,1)S(1)}, u32[]{:S(2)}, u32[]{:S(2)}) async-start(bf16[32,2,16,128]{3,2,1,0:T(8,128)(2,1)} %broadcast_in_dim.30), calls=%async_computation.4 | async-start | bytes 524288 | tf_op jit(solution)/shard_map/all_to_all | solution.py:334

commit v6 on v5

--- a/solution.py
+++ b/solution.py
@@ -92,42 +92,88 @@
     )(target, live, cells, weights, feats)
 
 
-def spread_kernel(target, place, *refs):
-    *parts, blocks, out, columns = refs
+def spread_kernel(inner, target, columns, blocks, out):
     step = pl.program_id(0)
     group, _, tile = blocks.shape
-    count = parts[0].shape[0]
-
-    @pl.when(step == 0)
-    def _():
-        for shift, part in enumerate(parts):
-            source = lax.rem(place[0] + (len(parts) - shift), len(parts))
-            columns[pl.ds(source * count, count)] = part[...]
-
+    half = out.shape[0]
     for t in range(group):
         column = target[step * group + t]
-        value = jnp.dot(columns[column], blocks[t], preferred_element_type=jnp.float32)
+        first = pl.multiple_of(column % inner * half, half)
+        own = columns[column // inner, pl.ds(first, half), :]
+        value = jnp.dot(own, blocks[t], preferred_element_type=jnp.float32)
         out[:, t * tile : (t + 1) * tile] = value.astype(jnp.bfloat16)
 
 
-def spread(target, place, parts, blocks):
+def spread(target, columns, blocks, half, inner):
     tiles, depth, tile = blocks.shape
-    count, half, _ = parts[0].shape
     group = min(SPREAD_GROUP, tiles)
-    smem = pl.BlockSpec(memory_space=pltpu.SMEM)
     return pl.pallas_call(
-        spread_kernel,
+        functools.partial(spread_kernel, inner),
         grid=(tiles // group,),
-        in_specs=[smem, smem]
-        + [pl.BlockSpec(part.shape, lambda i: (0, 0, 0)) for part in parts]
-        + [pl.BlockSpec((group, depth, tile), lambda i: (i, 0, 0))],
+        in_specs=[
+            pl.BlockSpec(memory_space=pltpu.SMEM),
+            pl.BlockSpec(columns.shape, lambda i: (0, 0, 0)),
+            pl.BlockSpec((group, depth, tile), lambda i: (i, 0, 0)),
+        ],
         out_specs=pl.BlockSpec((half, group * tile), lambda i: (0, i)),
         out_shape=jax.ShapeDtypeStruct((half, tiles * tile), jnp.bfloat16),
-        scratch_shapes=[pltpu.VMEM((count * len(parts), half, depth), jnp.bfloat16)],
         compiler_params=pltpu.CompilerParams(vmem_limit_bytes=VMEM_LIMIT),
         cost_estimate=cost(2 * half * tiles * tile * depth, 6 * tiles * tile * depth),
         name="spread",
-    )(target, place, *parts, blocks)
+    )(target, columns, blocks)
+
+
+def in_vmem(kernel, name, out_shape, *args):
+    vmem = pl.BlockSpec(memory_space=pltpu.VMEM)
+    return pl.pallas_call(
+        kernel,
+        in_specs=[vmem] * len(args),
+        out_specs=vmem,
+        out_shape=jax.ShapeDtypeStruct(out_shape, jnp.bfloat16),
+        compiler_params=pltpu.CompilerParams(vmem_limit_bytes=VMEM_LIMIT),
+        name=name,
+    )(*args)
+
+
+def added(parts):
+    total = parts[0].astype(jnp.float32)
+    for part in parts[1:]:
+        total = total + part.astype(jnp.float32)
+    return total
+
+
+def add_kernel(received, out):
+    count = out.shape[0]
+    for d in range(count):
+        parts = [received[first + d] for first in range(0, received.shape[0], count)]
+        out[d] = added(parts).astype(jnp.bfloat16)
+
+
+def relay_kernel(own, received, message):
+    sources = received.shape[0]
+    outer = message.shape[0]
+    total = added([received[z, own:, :] for z in range(sources)]).astype(jnp.bfloat16)
+    rows = total.shape[0] // outer
+    for x in range(outer):
+        for z in range(sources):
+            message[x, z * own : (z + 1) * own, :] = received[z, :own, :]
+        message[x, sources * own :, :] = total[x * rows : (x + 1) * rows]
+
+
+def share_kernel(received, message):
+    first = received.shape[1] - message.shape[1]
+    total = added([received[x, first:, :] for x in range(received.shape[0])])
+    total = total.astype(jnp.bfloat16)
+    for peer in range(message.shape[0]):
+        message[peer] = total
+
+
+def finish_kernel(scale, received, message):
+    for c in range(2):
+        total = added([received[s + c] for s in range(0, received.shape[0], 2)]) * scale
+        total = total.astype(jnp.bfloat16)
+        for peer in range(message.shape[0]):
+            message[peer, c] = total
 
 
 def unpack_kernel(inner, gathered, out):
@@ -307,7 +353,6 @@
     n_dom, n_slab = lax.axis_size("dom"), lax.axis_size("slab")
     width = xsize * ysize
     chan = lax.axis_index("chan").astype(jnp.int32)
-    place = (lax.axis_index("dom") // min(8, n_dom // 2)).astype(jnp.int32)
     scale = float(width * depth * n_dom * n_slab) ** (-0.5)
 
     blocks, send = pool(
@@ -338,7 +383,8 @@
     def total(value, parts):
         return value.reshape((parts, -1) + value.shape[1:]).astype(jnp.float32).sum(0)
 
-    part = total(exchange(send, "dom", same_z), outer).astype(jnp.bfloat16)
+    part = exchange(send, "dom", same_z)
+    part = in_vmem(add_kernel, "add_x", (part.shape[0] // outer,) + part.shape[1:], part)
     part = exchange(part, "dom", same_x)
     part, wf, wb = lax.optimization_barrier((part, wf, wb))
     pooled = total(part, inner).astype(jnp.bfloat16)
@@ -358,29 +404,17 @@
     each = -(-27 // n_dom)
     latent, message = conv_layer(chan[None], grid, wf, wb, inner, outer * each)
     message = exchange(message, "dom", same_x)
-    columns = message[:, : width * half].reshape(inner * width, half, depth)
-    columns = [columns] + [
-        lax.ppermute(
-            columns, "dom", [(g[x], g[(x + shift) % outer]) for g in same_z for x in range(outer)]
-        )
-        for shift in range(1, outer)
-    ]
-
-    peers = 2 * n_slab
-    same_z_all = [
-        [(x * inner + z) * peers + p for x in range(outer) for p in range(peers)]
-        for z in range(inner)
-    ]
-    kgrad = message[:, width * half :].astype(jnp.float32).sum(0).astype(jnp.bfloat16)
-    kgrad = kgrad.reshape(outer, 1, each * CHUNK, depth)
-    kgrad = jnp.broadcast_to(kgrad, (outer, peers, each * CHUNK, depth))
-    kgrad = exchange(
-        kgrad.reshape(outer * peers, each * CHUNK, depth), ("dom", "slab", "chan"), same_z_all
-    )
-    kgrad = (total(kgrad, outer * n_slab) * scale).astype(jnp.bfloat16)
-    kgrad, columns = lax.optimization_barrier((kgrad, columns))
-    kgrad = exchange(jnp.broadcast_to(kgrad[None], (n_dom,) + kgrad.shape), "dom")
-    feature_grad = spread(tile_target, place[None], columns, blocks)
+    own, rows = width * half, each * CHUNK
+    shape = (outer, inner * own + rows, depth)
+    message = in_vmem(functools.partial(relay_kernel, own), "relay", shape, message)
+    columns = exchange(message, "dom", same_z)
+
+    kgrad = in_vmem(share_kernel, "share", (2 * n_slab, rows, depth), columns)
+    kgrad = exchange(kgrad, ("slab", "chan"))
+    shape = (n_dom, 2, rows, depth)
+    kgrad = in_vmem(functools.partial(finish_kernel, scale), "finish", shape, kgrad)
+    kgrad = exchange(kgrad, "dom")
+    feature_grad = spread(tile_target, columns, blocks, half, inner * width)
     kgrad, feature_grad = lax.optimization_barrier((kgrad, feature_grad))
     kernel_grad = unpack(kgrad, 27, full, inner)
     return (latent, feature_grad, kernel_grad)

time: 142 us -> 144 us (1.014)
  blocking collectives: 38.8 us -> 72.6 us
  starting transfers between devices: 46 us -> 26.3 us
  waiting for transfers between devices: 35.5 us -> 25.3 us
  Pallas kernels: 11.5 us -> 13.2 us
  local copies, waits for them, and re-layouts: 5.3 us -> 3.79 us
    all_to_all x2 -> x4, blocking collectives: 36.3 us -> 70.1 us  [exchange(): lax.all_to_all(value, axis, split_axis=0, concat_axis=0, tiled=True, axis...]
    all_to_all x3 -> x2, starting transfers between devices: 26.8 us -> 15.7 us  [exchange(): lax.all_to_all(value, axis, split_axis=0, concat_axis=0, tiled=True, axis...]
    ppermute x3 -> x0, starting transfers between devices: 8.55 us -> none  [body(): lax.ppermute(columns, 'dom', [(g[x], g[(x + shift) % outer]) for g in sam...]
    ppermute x3 -> x0, waiting for transfers between devices: 8.38 us -> none  [body(): lax.ppermute(columns, 'dom', [(g[x], g[(x + shift) % outer]) for g in sam...]
    all_to_all x3 -> x2, waiting for transfers between devices: 17.4 us -> 15.7 us  [exchange(): lax.all_to_all(value, axis, split_axis=0, concat_axis=0, tiled=True, axis...]
    pallas_call x1 -> x5, Pallas kernels: 2.75 us -> 4.39 us  [the longest x1 2.66 us: spread(): pl.pallas_call(functools.partial(spread_kernel, inner), grid=(tiles // gr...]
    broadcast_in_dim x2 -> x0, local copies, waits for them, and re-layouts: 1.47 us -> none  [the longest x1 0.74 us: body(): kgrad = jnp.broadcast_to(kgrad, (outer, peers, each * CHUNK, depth))]
  transfers between devices with their start and end apart: 10 -> 6, of which waited for: 10 -> 6; matrix products, arithmetic and copies ran while one was open for 3% -> 3% of each run, Pallas kernels for 2% -> 2%
where the time goes in v6:
time: 144 us; the launch traced here: 143 us
  blocking collectives  72.6 us (50%)
  starting transfers between devices  26.3 us (18%)
  waiting for transfers between devices  25.3 us (18%)
  Pallas kernels  13.2 us (9%)
  local copies, waits for them, and re-layouts  3.79 us (3%)
  between operations  1.48 us (1%)
    all_to_all x4, blocking collectives, exchange(): lax.all_to_all(value, axis, split_axis=0, concat_axis=0, tiled=True, axis...  70.1 us
    all_to_all x2, starting transfers between devices, exchange(): lax.all_to_all(value, axis, split_axis=0, concat_axis=0, tiled=True, axis...  15.7 us
    all_to_all x2, waiting for transfers between devices, exchange(): lax.all_to_all(value, axis, split_axis=0, concat_axis=0, tiled=True, axis...  15.7 us
    ppermute x4, starting transfers between devices, neighbours(): return (lax.ppermute(last, axis, up), lax.ppermute(first, axis, down))  10.6 us
    ppermute x4, waiting for transfers between devices, neighbours(): return (lax.ppermute(last, axis, up), lax.ppermute(first, axis, down))  9.64 us
    pallas_call x1, Pallas kernels, pool(): pl.pallas_call(pool_kernel, grid=(tiles // group,), in_specs=[smem, smem,...  4.99 us
  transfers between devices with their start and end apart: 6, of which 6 were waited for; matrix products, arithmetic and copies ran while one was open for 3% of the time, Pallas kernels for 2%

profile of v6, /device:TPU:6, one launch (start us, length us, event | category | flops | bytes accessed | tf_op | source)
XLA Modules:
  0.0 142.7 jit_solution(7958710152569111623)
XLA Ops:
  1.3 5.0 %pool.1 = (bf16[64,128,128]{2,1,0:T(8,128)(2,1)}, bf16[128,32,128]{2,1,0:T(8,128)(2,1)}) custom-call(s32[64]{0:T(128)} %target.3, s32[1]{0:T(128)S(6)} %copy.34.live, s32[8,8192]{1,0:T(8,128)} %cells.1, f32[8,8192]{1,0:T(8,128)} %weights.1, bf16[32,8192]{1,0:T(8,128)(2,1)} %feats.1), custom_call_target="tpu_custom_call" | custom-call | flops 67108864 | bytes 25165824 | tf_op jit(solution)/shard_map/pool/pallas_call | solution.py:70
  6.3 18.2 %all_to_all.30.received = bf16[128,32,128]{2,1,0:T(8,128)(2,1)S(1)} all-to-all(bf16[128,32,128]{2,1,0:T(8,128)(2,1)} %get-tuple-element.12), channel_id=1, replica_groups={{0,128,256,384},{16,144,272,400},{32,160,288,416},{48,176,304,432},{64,..., dimensions={0} | all-to-all | bytes 2097152 | tf_op jit(solution)/shard_map/all_to_all | solution.py:379
  24.4 0.0 copy-start.2
  24.4 0.8 add_x.1
  25.3 10.0 %all-to-all-start.1 = ((bf16[32,32,128]{2,1,0:T(8,128)(2,1)}), bf16[32,32,128]{2,1,0:T(8,128)(2,1)S(1)}, u32[]{:S(2)}, u32[]{:S(2)}) async-start(bf16[32,32,128]{2,1,0:T(8,128)(2,1)} %add_x.1), calls=%async_computation.1 | async-start | bytes 524288 | tf_op jit(solution)/shard_map/all_to_all | solution.py:379
  35.2 0.0 copy-done.2
  35.2 1.0 copy.22
  36.2 0.4 copy.23
  36.6 0.4 reshape.22.wf
  36.9 0.0 copy-start.3
  37.0 1.6 %rev.3 = bf16[3,3,3,64,64]{4,1,3,2,0:T(4,128)(2,1)S(1)} reverse(bf16[3,3,3,64,64]{4,1,3,2,0:T(4,128)(2,1)S(1)} %copy.23), dimensions={0,1} | reverse | bytes 442368 | tf_op jit(solution)/shard_map/rev | solution.py:370
  38.6 0.1 dynamic-slice_bitcast_fusion
  38.7 0.2 reshape.23.wb
  38.9 0.0 copy-done.3
  39.0 6.9 %all-to-all-done.1 = bf16[32,32,128]{2,1,0:T(8,128)(2,1)S(1)} async-done(((bf16[32,32,128]{2,1,0:T(8,128)(2,1)}), bf16[32,32,128]{2,1,0:T(8,128)(2,1)S(1)}, u32[]{:S(2)}, u32[]{:S(2)}) %all-to-all-start.1) | async-done | bytes 262176 | tf_op jit(solution)/shard_map/all_to_all | solution.py:379
  46.0 1.9 %collective-permute-start.1 = (bf16[6,32,128]{2,1,0:T(8,128)(2,1)S(1)}, bf16[6,32,128]{2,1,0:T(8,128)(2,1)S(1)}, u32[]{:S(2)}, u32[]{:S(2)}) collective-permute-start(bf16[6,32,128]{2,1,0:T(8,128)(2,1)S(1)} %get-tuple-element.26), channel_id=1, source_target_pairs={{16,0},{32,16},{48,32},{64,48},{80,64},{96,80},{112,96},{128,112},... | collective-permute-start | bytes 147464 | tf_op jit(solution)/shard_map/ppermute | solution.py:338
  47.9 3.9 %collective-permute-start = (bf16[6,32,128]{2,1,0:T(8,128)(2,1)S(1)}, bf16[6,32,128]{2,1,0:T(8,128)(2,1)S(1)}, u32[]{:S(2)}, u32[]{:S(2)}) collective-permute-start(bf16[6,32,128]{2,1,0:T(8,128)(2,1)S(1)} %get-tuple-element.25), channel_id=1, source_target_pairs={{0,16},{16,32},{32,48},{48,64},{64,80},{80,96},{96,112},{112,128},... | collective-permute-start | bytes 147464 | tf_op jit(solution)/shard_map/ppermute | solution.py:338
  51.8 0.1 collective-permute-done.1
  52.0 4.0 %collective-permute-done = bf16[6,32,128]{2,1,0:T(8,128)(2,1)S(1)} collective-permute-done((bf16[6,32,128]{2,1,0:T(8,128)(2,1)S(1)}, bf16[6,32,128]{2,1,0:T(8,128)(2,1)S(1)}, u32[]{:S(2)}, u32[]{:S(2)}) %collective-permute-start) | collective-permute-done | bytes 49184 | tf_op jit(solution)/shard_map/ppermute | solution.py:338
  56.1 3.5 %collective-permute-start.2 = (bf16[16,32,128]{2,1,0:T(8,128)(2,1)S(1)}, bf16[16,32,128]{2,1,0:T(8,128)(2,1)S(1)}, u32[]{:S(2)}, u32[]{:S(2)}) collective-permute-start(bf16[16,32,128]{2,1,0:T(8,128)(2,1)S(1)} %get-tuple-element.22), channel_id=1, source_target_pairs={{0,2},{2,4},{4,6},{6,8},{8,10},{10,12},{12,14},{1,3},{3,5},{5,7},{... | collective-permute-start | bytes 393224 | tf_op jit(solution)/shard_map/ppermute | solution.py:338
  59.6 1.3 collective-permute-start.3
  60.9 1.2 collective-permute-done.2
  62.1 4.3 %collective-permute-done.3 = bf16[16,32,128]{2,1,0:T(8,128)(2,1)S(1)} collective-permute-done((bf16[16,32,128]{2,1,0:T(8,128)(2,1)S(1)}, bf16[16,32,128]{2,1,0:T(8,128)(2,1)S(1)}, u32[]{:S(2)}, u32[]{:S(2)}) %collective-permute-start.3) | collective-permute-done | bytes 131104 | tf_op jit(solution)/shard_map/ppermute | solution.py:338
  66.5 2.4 %all-gather = bf16[104,32,128]{2,1,0:T(8,128)(2,1)S(1)} all-gather(bf16[52,32,128]{2,1,0:T(8,128)(2,1)S(1)} %constant_dynamic-update-slice_fusion), channel_id=2, replica_groups=mesh['dom'=32,'slab'=8,'chan'=2] {'chan'}, dimensions={0}, use_global_device_ids=true | all-gather | bytes 1277952 | tf_op jit(solution)/shard_map/all_gather | solution.py:402
  68.9 2.6 %conv_layer.1 = (bf16[32,2,2,128]{3,2,1,0:T(2,128)(2,1)}, bf16[8,192,128]{2,1,0:T(8,128)(2,1)S(1)}) custom-call(s32[1]{0:T(128)} %bitcast.chan, bf16[2,52,32,128]{3,2,1,0:T(8,128)(2,1)S(1)} %bitcast.25, bf16[3,192,192]{2,1,0:T(8,128)(2,1)S(1)} %reshape.22.wf, bf16[3,96,192]{2,1,0:T(8,128)(2,1)S(1)} %reshape.23.wb), custom_call_target="tpu_custom_call" | custom-call | tf_op jit(solution)/shard_map/conv_layer/pallas_call | solution.py:316
  71.5 18.0 %all_to_all.31.received = bf16[8,192,128]{2,1,0:T(8,128)(2,1)S(1)} all-to-all(bf16[8,192,128]{2,1,0:T(8,128)(2,1)S(1)} %get-tuple-element.17), channel_id=1, replica_groups={{0,16,32,48,64,80,96,112},{128,144,160,176,192,208,224,240},{256,272,28..., dimensions={0} | all-to-all | bytes 786432 | tf_op jit(solution)/shard_map/all_to_all | solution.py:379
  89.5 0.1 relay.1
  89.7 18.7 %all_to_all.32.received.columns = bf16[4,1040,128]{2,1,0:T(8,128)(2,1)S(1)} all-to-all(bf16[4,1040,128]{2,1,0:T(8,128)(2,1)S(1)} %relay.1), channel_id=1, replica_groups={{0,128,256,384},{16,144,272,400},{32,160,288,416},{48,176,304,432},{64,..., dimensions={0} | all-to-all | bytes 2129920 | tf_op jit(solution)/shard_map/all_to_all | solution.py:379
  108.4 0.0 copy-start
  108.4 0.0 copy-start.1
  108.5 15.2 %all_to_all.33.received = bf16[16,16,128]{2,1,0:T(8,128)(2,1)S(1)} all-to-all(bf16[16,16,128]{2,1,0:T(8,128)(2,1)S(1)} %share.1), channel_id=1, replica_groups=mesh['dom'=32,'slab'=8,'chan'=2] {'slab','chan'}, dimensions={0} | all-to-all | bytes 131072 | tf_op jit(solution)/shard_map/all_to_all | solution.py:379
  123.7 0.7 finish.1
  124.4 5.7 %all-to-all-start.5 = ((bf16[32,2,16,128]{3,2,1,0:T(8,128)(2,1)}), bf16[32,2,16,128]{3,2,1,0:T(8,128)(2,1)S(1)}, u32[]{:S(2)}, u32[]{:S(2)}) async-start(bf16[32,2,16,128]{3,2,1,0:T(8,128)(2,1)} %finish.1), calls=%async_computation.5 | async-start | bytes 524288 | tf_op jit(solution)/shard_map/all_to_all | solution.py:379
  130.1 0.0 copy-done
  130.2 0.0 copy-done.1
  130.2 2.7 %spread.1 = bf16[32,8192]{1,0:T(8,128)(2,1)} custom-call(s32[64]{0:T(128)S(1)} %copy-done.1, bf16[4,1040,128]{2,1,0:T(8,128)(2,1)S(1)} %all_to_all.32.received.columns, bf16[64,128,128]{2,1,0:T(8,128)(2,1)S(1)} %copy-done), custom_call_target="tpu_custom_call" | custom-call | flops 67108864 | bytes 6291456 | tf_op jit(solution)/shard_map/spread/pallas_call | solution.py:110
  132.8 8.7 %all-to-all-done.5.gathered = bf16[32,2,16,128]{3,2,1,0:T(8,128)(2,1)S(1)} async-done(((bf16[32,2,16,128]{3,2,1,0:T(8,128)(2,1)}), bf16[32,2,16,128]{3,2,1,0:T(8,128)(2,1)S(1)}, u32[]{:S(2)}, u32[]{:S(2)}) %all-to-all-start.5) | async-done | bytes 262176 | tf_op jit(solution)/shard_map/all_to_all | solution.py:379
  141.6 1.2 unpack.1
  (18 shorter events, 0.2 us)
Async XLA Ops:
  24.4 10.8 %copy-start.2 = (bf16[27,64,64]{2,1,0:T(8,128)(2,1)S(1)}, bf16[27,64,64]{2,1,0:T(8,128)(2,1)}, u32[]{:S(2)}) copy-start(bf16[27,64,64]{2,1,0:T(8,128)(2,1)} %param.12) | copy-start | bytes 663556
  25.3 20.6 %all-to-all-start.1 = ((bf16[32,32,128]{2,1,0:T(8,128)(2,1)}), bf16[32,32,128]{2,1,0:T(8,128)(2,1)S(1)}, u32[]{:S(2)}, u32[]{:S(2)}) async-start(bf16[32,32,128]{2,1,0:T(8,128)(2,1)} %add_x.1), calls=%async_computation.1 | async-start | bytes 524288 | tf_op jit(solution)/shard_map/all_to_all | solution.py:379
  36.9 2.0 %copy-start.3 = (bf16[32,2,2,128]{3,2,1,0:T(2,128)(2,1)S(1)}, bf16[32,2,2,128]{3,2,1,0:T(2,128)(2,1)}, u32[]{:S(2)}) copy-start(bf16[32,2,2,128]{3,2,1,0:T(2,128)(2,1)} %param.13) | copy-start | bytes 98308
  46.0 6.0 %collective-permute-start.1 = (bf16[6,32,128]{2,1,0:T(8,128)(2,1)S(1)}, bf16[6,32,128]{2,1,0:T(8,128)(2,1)S(1)}, u32[]{:S(2)}, u32[]{:S(2)}) collective-permute-start(bf16[6,32,128]{2,1,0:T(8,128)(2,1)S(1)} %get-tuple-element.26), channel_id=1, source_target_pairs={{16,0},{32,16},{48,32},{64,48},{80,64},{96,80},{112,96},{128,112},... | collective-permute-start | bytes 147464 | tf_op jit(solution)/shard_map/ppermute | solution.py:338
  47.9 8.1 %collective-permute-start = (bf16[6,32,128]{2,1,0:T(8,128)(2,1)S(1)}, bf16[6,32,128]{2,1,0:T(8,128)(2,1)S(1)}, u32[]{:S(2)}, u32[]{:S(2)}) collective-permute-start(bf16[6,32,128]{2,1,0:T(8,128)(2,1)S(1)} %get-tuple-element.25), channel_id=1, source_target_pairs={{0,16},{16,32},{32,48},{48,64},{64,80},{80,96},{96,112},{112,128},... | collective-permute-start | bytes 147464 | tf_op jit(solution)/shard_map/ppermute | solution.py:338
  56.1 6.0 %collective-permute-start.2 = (bf16[16,32,128]{2,1,0:T(8,128)(2,1)S(1)}, bf16[16,32,128]{2,1,0:T(8,128)(2,1)S(1)}, u32[]{:S(2)}, u32[]{:S(2)}) collective-permute-start(bf16[16,32,128]{2,1,0:T(8,128)(2,1)S(1)} %get-tuple-element.22), channel_id=1, source_target_pairs={{0,2},{2,4},{4,6},{6,8},{8,10},{10,12},{12,14},{1,3},{3,5},{5,7},{... | collective-permute-start | bytes 393224 | tf_op jit(solution)/shard_map/ppermute | solution.py:338
  59.6 6.9 %collective-permute-start.3 = (bf16[16,32,128]{2,1,0:T(8,128)(2,1)S(1)}, bf16[16,32,128]{2,1,0:T(8,128)(2,1)S(1)}, u32[]{:S(2)}, u32[]{:S(2)}) collective-permute-start(bf16[16,32,128]{2,1,0:T(8,128)(2,1)S(1)} %get-tuple-element.21), channel_id=1, source_target_pairs={{2,0},{4,2},{6,4},{8,6},{10,8},{12,10},{14,12},{3,1},{5,3},{7,5},{... | collective-permute-start | bytes 393224 | tf_op jit(solution)/shard_map/ppermute | solution.py:338
  108.4 21.7 %copy-start = (bf16[64,128,128]{2,1,0:T(8,128)(2,1)S(1)}, bf16[64,128,128]{2,1,0:T(8,128)(2,1)}, u32[]{:S(2)}) copy-start(bf16[64,128,128]{2,1,0:T(8,128)(2,1)} %get-tuple-element.18.blocks) | copy-start | bytes 6291460
  108.4 21.7 %copy-start.1 = (s32[64]{0:T(128)S(1)}, s32[64]{0:T(128)}, u32[]{:S(2)}) copy-start(s32[64]{0:T(128)} %target.3) | copy-start | bytes 772
  124.4 17.2 %all-to-all-start.5 = ((bf16[32,2,16,128]{3,2,1,0:T(8,128)(2,1)}), bf16[32,2,16,128]{3,2,1,0:T(8,128)(2,1)S(1)}, u32[]{:S(2)}, u32[]{:S(2)}) async-start(bf16[32,2,16,128]{3,2,1,0:T(8,128)(2,1)} %finish.1), calls=%async_computation.5 | async-start | bytes 524288 | tf_op jit(solution)/shard_map/all_to_all | solution.py:379

commit v7 on v6

--- a/solution.py
+++ b/solution.py
@@ -92,35 +92,46 @@
     )(target, live, cells, weights, feats)
 
 
-def spread_kernel(inner, target, columns, blocks, out):
+def spread_kernel(target, place, *refs):
+    *parts, blocks, out, columns = refs
     step = pl.program_id(0)
     group, _, tile = blocks.shape
-    half = out.shape[0]
+    count = parts[0].shape[0]
+
+    @pl.when(step == 0)
+    def _():
+        shift = 0
+        for part in parts:
+            for first in range(0, part.shape[0], count):
+                source = jnp.bitwise_xor(place[0], shift)
+                columns[pl.ds(source * count, count)] = part[first : first + count]
+                shift += 1
+
     for t in range(group):
         column = target[step * group + t]
-        first = pl.multiple_of(column % inner * half, half)
-        own = columns[column // inner, pl.ds(first, half), :]
-        value = jnp.dot(own, blocks[t], preferred_element_type=jnp.float32)
+        value = jnp.dot(columns[column], blocks[t], preferred_element_type=jnp.float32)
         out[:, t * tile : (t + 1) * tile] = value.astype(jnp.bfloat16)
 
 
-def spread(target, columns, blocks, half, inner):
+def spread(target, place, parts, blocks):
     tiles, depth, tile = blocks.shape
+    half = parts[0].shape[1]
     group = min(SPREAD_GROUP, tiles)
-    return pl.pallas_call(
-        functools.partial(spread_kernel, inner),
+    smem = pl.BlockSpec(memory_space=pltpu.SMEM)
+    total = sum(part.shape[0] for part in parts)
+    return pl.pallas_call(
+        spread_kernel,
         grid=(tiles // group,),
-        in_specs=[
-            pl.BlockSpec(memory_space=pltpu.SMEM),
-            pl.BlockSpec(columns.shape, lambda i: (0, 0, 0)),
-            pl.BlockSpec((group, depth, tile), lambda i: (i, 0, 0)),
-        ],
+        in_specs=[smem, smem]
+        + [pl.BlockSpec(part.shape, lambda i: (0, 0, 0)) for part in parts]
+        + [pl.BlockSpec((group, depth, tile), lambda i: (i, 0, 0))],
         out_specs=pl.BlockSpec((half, group * tile), lambda i: (0, i)),
         out_shape=jax.ShapeDtypeStruct((half, tiles * tile), jnp.bfloat16),
+        scratch_shapes=[pltpu.VMEM((total, half, depth), jnp.bfloat16)],
         compiler_params=pltpu.CompilerParams(vmem_limit_bytes=VMEM_LIMIT),
         cost_estimate=cost(2 * half * tiles * tile * depth, 6 * tiles * tile * depth),
         name="spread",
-    )(target, columns, blocks)
+    )(target, place, *parts, blocks)
 
 
 def in_vmem(kernel, name, out_shape, *args):
@@ -149,23 +160,31 @@
         out[d] = added(parts).astype(jnp.bfloat16)
 
 
-def relay_kernel(own, received, message):
-    sources = received.shape[0]
-    outer = message.shape[0]
+def split_kernel(received, columns, message):
+    sources, own, _ = columns.shape
+    outer, peers, rows, _ = message.shape
     total = added([received[z, own:, :] for z in range(sources)]).astype(jnp.bfloat16)
-    rows = total.shape[0] // outer
+    for z in range(sources):
+        columns[z] = received[z, :own, :]
     for x in range(outer):
-        for z in range(sources):
-            message[x, z * own : (z + 1) * own, :] = received[z, :own, :]
-        message[x, sources * own :, :] = total[x * rows : (x + 1) * rows]
-
-
-def share_kernel(received, message):
-    first = received.shape[1] - message.shape[1]
-    total = added([received[x, first:, :] for x in range(received.shape[0])])
-    total = total.astype(jnp.bfloat16)
-    for peer in range(message.shape[0]):
-        message[peer] = total
+        for peer in range(peers):
+            message[x, peer] = total[x * rows : (x + 1) * rows]
+
+
+def split(received, own, outer, peers):
+    sources, rows, depth = received.shape
+    vmem = pl.BlockSpec(memory_space=pltpu.VMEM)
+    return pl.pallas_call(
+        split_kernel,
+        in_specs=[vmem],
+        out_specs=[vmem, vmem],
+        out_shape=[
+            jax.ShapeDtypeStruct((sources, own, depth), jnp.bfloat16),
+            jax.ShapeDtypeStruct((outer, peers, (rows - own) // outer, depth), jnp.bfloat16),
+        ],
+        compiler_params=pltpu.CompilerParams(vmem_limit_bytes=VMEM_LIMIT),
+        name="split",
+    )(received)
 
 
 def finish_kernel(scale, received, message):
@@ -338,6 +357,10 @@
     return lax.ppermute(last, axis, up), lax.ppermute(first, axis, down)
 
 
+def paired(groups, shift):
+    return [(group[i], group[i ^ shift]) for group in groups for i in range(len(group))]
+
+
 def body(
     point_features,
     neighbour_cells,
@@ -404,17 +427,28 @@
     each = -(-27 // n_dom)
     latent, message = conv_layer(chan[None], grid, wf, wb, inner, outer * each)
     message = exchange(message, "dom", same_x)
-    own, rows = width * half, each * CHUNK
-    shape = (outer, inner * own + rows, depth)
-    message = in_vmem(functools.partial(relay_kernel, own), "relay", shape, message)
-    columns = exchange(message, "dom", same_z)
-
-    kgrad = in_vmem(share_kernel, "share", (2 * n_slab, rows, depth), columns)
-    kgrad = exchange(kgrad, ("slab", "chan"))
+    peers, rows = 2 * n_slab, each * CHUNK
+    columns, kgrad = split(message, width * half, outer, peers)
+
+    same_z_all = [
+        [(x * inner + z) * peers + p for x in range(outer) for p in range(peers)]
+        for z in range(inner)
+    ]
+    columns = columns.reshape(inner * width, half, depth)
+    parts = [columns, lax.ppermute(columns, "dom", paired(same_z, 1))]
+    kgrad = exchange(
+        kgrad.reshape(outer * peers, rows, depth), ("dom", "slab", "chan"), same_z_all
+    )
     shape = (n_dom, 2, rows, depth)
     kgrad = in_vmem(functools.partial(finish_kernel, scale), "finish", shape, kgrad)
+    kgrad, parts = lax.optimization_barrier((kgrad, parts))
     kgrad = exchange(kgrad, "dom")
-    feature_grad = spread(tile_target, columns, blocks, half, inner * width)
+    shift = 2
+    while shift < outer:
+        parts.append(lax.ppermute(jnp.concatenate(parts, 0), "dom", paired(same_z, shift)))
+        shift = 2 * shift
+    place = (lax.axis_index("dom") // inner).astype(jnp.int32)
+    feature_grad = spread(tile_target, place[None], parts, blocks)
     kgrad, feature_grad = lax.optimization_barrier((kgrad, feature_grad))
     kernel_grad = unpack(kgrad, 27, full, inner)
     return (latent, feature_grad, kernel_grad)

time: 144 us -> 140 us (0.972)
  blocking collectives: 72.6 us -> 38.9 us
  starting transfers between devices: 26.3 us -> 44.1 us
  waiting for transfers between devices: 25.3 us -> 36.7 us
    all_to_all x4 -> x2, blocking collectives: 70.1 us -> 36.5 us  [exchange(): lax.all_to_all(value, axis, split_axis=0, concat_axis=0, tiled=True, axis...]
    all_to_all x2 -> x3, starting transfers between devices: 15.7 us -> 27.7 us  [exchange(): lax.all_to_all(value, axis, split_axis=0, concat_axis=0, tiled=True, axis...]
    ppermute x0 -> x2, waiting for transfers between devices: none -> 11.3 us  [the longest x1 11.2 us: body(): lax.ppermute(jnp.concatenate(parts, 0), 'dom', paired(same_z, shift))]
    ppermute x0 -> x2, starting transfers between devices: none -> 5.77 us  [the longest x1 3.11 us: body(): lax.ppermute(jnp.concatenate(parts, 0), 'dom', paired(same_z, shift))]
    pallas_call x1 -> x2, Pallas kernels: 2.66 us -> 3.46 us  [the longest x1 2.71 us: spread(): pl.pallas_call(spread_kernel, grid=(tiles // group,), in_specs=[smem, sme...]
    all_to_all x2 -> x3, waiting for transfers between devices: 15.7 us -> 15.8 us  [exchange(): lax.all_to_all(value, axis, split_axis=0, concat_axis=0, tiled=True, axis...]
  transfers between devices with their start and end apart: 6 -> 9, of which waited for: 6 -> 7; matrix products, arithmetic and copies ran while one was open for 3% -> 3% of each run, Pallas kernels for 2% -> 2%
where the time goes in v7:
time: 140 us
  starting transfers between devices  44.1 us (32%)
  blocking collectives  38.9 us (28%)
  waiting for transfers between devices  36.7 us (26%)
  Pallas kernels  13.8 us (10%)
  local copies, waits for them, and re-layouts  3.79 us (3%)
  between operations  1.51 us (1%)
    all_to_all x2, blocking collectives, exchange(): lax.all_to_all(value, axis, split_axis=0, concat_axis=0, tiled=True, axis...  36.5 us
    all_to_all x3, starting transfers between devices, exchange(): lax.all_to_all(value, axis, split_axis=0, concat_axis=0, tiled=True, axis...  27.7 us
    all_to_all x3, waiting for transfers between devices, exchange(): lax.all_to_all(value, axis, split_axis=0, concat_axis=0, tiled=True, axis...  15.8 us
    ppermute x1, waiting for transfers between devices, body(): lax.ppermute(jnp.concatenate(parts, 0), 'dom', paired(same_z, shift))  11.2 us
    ppermute x4, starting transfers between devices, neighbours(): return (lax.ppermute(last, axis, up), lax.ppermute(first, axis, down))  10.6 us
    ppermute x4, waiting for transfers between devices, neighbours(): return (lax.ppermute(last, axis, up), lax.ppermute(first, axis, down))  9.64 us
    pallas_call x1, Pallas kernels, pool(): pl.pallas_call(pool_kernel, grid=(tiles // group,), in_specs=[smem, smem,...  4.99 us
    ppermute x1, starting transfers between devices, body(): lax.ppermute(jnp.concatenate(parts, 0), 'dom', paired(same_z, shift))  3.11 us
  transfers between devices with their start and end apart: 9, of which 7 were waited for; matrix products, arithmetic and copies ran while one was open for 3% of the time, Pallas kernels for 2%

profile of v7, /device:TPU:6, one launch (start us, length us, event | category | flops | bytes accessed | tf_op | source)
XLA Modules:
  0.0 139.7 jit_solution(7660607895810941400)
XLA Ops:
  1.3 5.0 %pool.1 = (bf16[64,128,128]{2,1,0:T(8,128)(2,1)}, bf16[128,32,128]{2,1,0:T(8,128)(2,1)}) custom-call(s32[64]{0:T(128)} %target.3, s32[1]{0:T(128)S(6)} %copy.34.live, s32[8,8192]{1,0:T(8,128)} %cells.1, f32[8,8192]{1,0:T(8,128)} %weights.1, bf16[32,8192]{1,0:T(8,128)(2,1)} %feats.1), custom_call_target="tpu_custom_call" | custom-call | flops 67108864 | bytes 25165824 | tf_op jit(solution)/shard_map/pool/pallas_call | solution.py:70
  6.3 0.0 copy-start.2
  6.3 18.3 %all_to_all.25.received = bf16[128,32,128]{2,1,0:T(8,128)(2,1)S(1)} all-to-all(bf16[128,32,128]{2,1,0:T(8,128)(2,1)} %get-tuple-element.17), channel_id=1, replica_groups={{0,128,256,384},{16,144,272,400},{32,160,288,416},{48,176,304,432},{64,..., dimensions={0} | all-to-all | bytes 2097152 | tf_op jit(solution)/shard_map/all_to_all | solution.py:402
  24.6 0.8 add_x.1
  25.4 10.0 %all-to-all-start.1 = ((bf16[32,32,128]{2,1,0:T(8,128)(2,1)}), bf16[32,32,128]{2,1,0:T(8,128)(2,1)S(1)}, u32[]{:S(2)}, u32[]{:S(2)}) async-start(bf16[32,32,128]{2,1,0:T(8,128)(2,1)} %add_x.1), calls=%async_computation.1 | async-start | bytes 524288 | tf_op jit(solution)/shard_map/all_to_all | solution.py:402
  35.4 0.0 copy-done.2
  35.4 1.0 copy.22
  36.3 0.0 copy-start.3
  36.3 0.4 copy.23
  36.7 0.4 reshape.28.wf
  37.1 1.6 %rev.3 = bf16[3,3,3,64,64]{4,1,3,2,0:T(4,128)(2,1)S(1)} reverse(bf16[3,3,3,64,64]{4,1,3,2,0:T(4,128)(2,1)S(1)} %copy.23), dimensions={0,1} | reverse | bytes 442368 | tf_op jit(solution)/shard_map/rev | solution.py:393
  38.8 0.1 dynamic-slice_bitcast_fusion
  38.9 0.2 reshape.29.wb
  39.1 0.0 copy-done.3
  39.1 6.9 %all-to-all-done.1 = bf16[32,32,128]{2,1,0:T(8,128)(2,1)S(1)} async-done(((bf16[32,32,128]{2,1,0:T(8,128)(2,1)}), bf16[32,32,128]{2,1,0:T(8,128)(2,1)S(1)}, u32[]{:S(2)}, u32[]{:S(2)}) %all-to-all-start.1) | async-done | bytes 262176 | tf_op jit(solution)/shard_map/all_to_all | solution.py:402
  46.1 1.9 %collective-permute-start.1 = (bf16[6,32,128]{2,1,0:T(8,128)(2,1)S(1)}, bf16[6,32,128]{2,1,0:T(8,128)(2,1)S(1)}, u32[]{:S(2)}, u32[]{:S(2)}) collective-permute-start(bf16[6,32,128]{2,1,0:T(8,128)(2,1)S(1)} %get-tuple-element.36), channel_id=1, source_target_pairs={{16,0},{32,16},{48,32},{64,48},{80,64},{96,80},{112,96},{128,112},... | collective-permute-start | bytes 147464 | tf_op jit(solution)/shard_map/ppermute | solution.py:357
  48.0 3.9 %collective-permute-start = (bf16[6,32,128]{2,1,0:T(8,128)(2,1)S(1)}, bf16[6,32,128]{2,1,0:T(8,128)(2,1)S(1)}, u32[]{:S(2)}, u32[]{:S(2)}) collective-permute-start(bf16[6,32,128]{2,1,0:T(8,128)(2,1)S(1)} %get-tuple-element.35), channel_id=1, source_target_pairs={{0,16},{16,32},{32,48},{48,64},{64,80},{80,96},{96,112},{112,128},... | collective-permute-start | bytes 147464 | tf_op jit(solution)/shard_map/ppermute | solution.py:357
  52.0 0.1 collective-permute-done.1
  52.1 4.0 %collective-permute-done = bf16[6,32,128]{2,1,0:T(8,128)(2,1)S(1)} collective-permute-done((bf16[6,32,128]{2,1,0:T(8,128)(2,1)S(1)}, bf16[6,32,128]{2,1,0:T(8,128)(2,1)S(1)}, u32[]{:S(2)}, u32[]{:S(2)}) %collective-permute-start) | collective-permute-done | bytes 49184 | tf_op jit(solution)/shard_map/ppermute | solution.py:357
  56.2 3.5 %collective-permute-start.2 = (bf16[16,32,128]{2,1,0:T(8,128)(2,1)S(1)}, bf16[16,32,128]{2,1,0:T(8,128)(2,1)S(1)}, u32[]{:S(2)}, u32[]{:S(2)}) collective-permute-start(bf16[16,32,128]{2,1,0:T(8,128)(2,1)S(1)} %get-tuple-element.32), channel_id=1, source_target_pairs={{0,2},{2,4},{4,6},{6,8},{8,10},{10,12},{12,14},{1,3},{3,5},{5,7},{... | collective-permute-start | bytes 393224 | tf_op jit(solution)/shard_map/ppermute | solution.py:357
  59.7 1.3 collective-permute-start.3
  61.0 1.2 collective-permute-done.2
  62.3 4.3 %collective-permute-done.3 = bf16[16,32,128]{2,1,0:T(8,128)(2,1)S(1)} collective-permute-done((bf16[16,32,128]{2,1,0:T(8,128)(2,1)S(1)}, bf16[16,32,128]{2,1,0:T(8,128)(2,1)S(1)}, u32[]{:S(2)}, u32[]{:S(2)}) %collective-permute-start.3) | collective-permute-done | bytes 131104 | tf_op jit(solution)/shard_map/ppermute | solution.py:357
  66.6 2.4 %all-gather = bf16[104,32,128]{2,1,0:T(8,128)(2,1)S(1)} all-gather(bf16[52,32,128]{2,1,0:T(8,128)(2,1)S(1)} %constant_dynamic-update-slice_fusion), channel_id=2, replica_groups=mesh['dom'=32,'slab'=8,'chan'=2] {'chan'}, dimensions={0}, use_global_device_ids=true | all-gather | bytes 1277952 | tf_op jit(solution)/shard_map/all_gather | solution.py:425
  69.0 2.6 %conv_layer.1 = (bf16[32,2,2,128]{3,2,1,0:T(2,128)(2,1)}, bf16[8,192,128]{2,1,0:T(8,128)(2,1)S(1)}) custom-call(s32[1]{0:T(128)} %bitcast.chan, bf16[2,52,32,128]{3,2,1,0:T(8,128)(2,1)S(1)} %bitcast.28, bf16[3,192,192]{2,1,0:T(8,128)(2,1)S(1)} %reshape.28.wf, bf16[3,96,192]{2,1,0:T(8,128)(2,1)S(1)} %reshape.29.wb), custom_call_target="tpu_custom_call" | custom-call | tf_op jit(solution)/shard_map/conv_layer/pallas_call | solution.py:335
  71.6 0.0 copy-start
  71.6 0.0 copy-start.1
  71.6 18.2 %all_to_all.26.received = bf16[8,192,128]{2,1,0:T(8,128)(2,1)S(1)} all-to-all(bf16[8,192,128]{2,1,0:T(8,128)(2,1)S(1)} %get-tuple-element.22), channel_id=1, replica_groups={{0,16,32,48,64,80,96,112},{128,144,160,176,192,208,224,240},{256,272,28..., dimensions={0} | all-to-all | bytes 786432 | tf_op jit(solution)/shard_map/all_to_all | solution.py:402
  89.8 0.7 split.1
  90.6 11.8 %all-to-all-start.3 = ((bf16[64,16,128]{2,1,0:T(8,128)(2,1)}), bf16[64,16,128]{2,1,0:T(8,128)(2,1)S(1)}, u32[]{:S(2)}, u32[]{:S(2)}) async-start(bf16[64,16,128]{2,1,0:T(8,128)(2,1)} %bitcast.14), calls=%async_computation.3 | async-start | bytes 524288 | tf_op jit(solution)/shard_map/all_to_all | solution.py:402
  102.3 2.7 %collective-permute-start.4 = (bf16[32,32,128]{2,1,0:T(8,128)(2,1)S(1)}, bf16[32,32,128]{2,1,0:T(8,128)(2,1)S(1)}, u32[]{:S(2)}, u32[]{:S(2)}) collective-permute-start(bf16[32,32,128]{2,1,0:T(8,128)(2,1)S(1)} %bitcast.29), channel_id=1, source_target_pairs={{0,128},{128,0},{256,384},{384,256},{16,144},{144,16},{272,400},{4... | collective-permute-start | bytes 786440 | tf_op jit(solution)/shard_map/ppermute | solution.py:438
  105.0 8.9 %all-to-all-done.3.received = bf16[64,16,128]{2,1,0:T(8,128)(2,1)S(1)} async-done(((bf16[64,16,128]{2,1,0:T(8,128)(2,1)}), bf16[64,16,128]{2,1,0:T(8,128)(2,1)S(1)}, u32[]{:S(2)}, u32[]{:S(2)}) %all-to-all-start.3) | async-done | bytes 262176 | tf_op jit(solution)/shard_map/all_to_all | solution.py:402
  113.9 0.8 finish.1
  114.6 0.0 collective-permute-done.4.refs_1_
  114.7 0.8 pad_maximum_fusion
  115.5 3.1 %collective-permute-start.5 = (bf16[64,32,128]{2,1,0:T(8,128)(2,1)}, bf16[64,32,128]{2,1,0:T(8,128)(2,1)S(1)}, u32[]{:S(2)}, u32[]{:S(2)}) collective-permute-start(bf16[64,32,128]{2,1,0:T(8,128)(2,1)} %pad_maximum_fusion), channel_id=1, source_target_pairs={{0,256},{128,384},{256,0},{384,128},{16,272},{144,400},{272,16},{4... | collective-permute-start | bytes 1572872 | tf_op jit(solution)/shard_map/ppermute | solution.py:448
  118.6 6.0 %all-to-all-start.4 = ((bf16[32,2,16,128]{3,2,1,0:T(8,128)(2,1)}), bf16[32,2,16,128]{3,2,1,0:T(8,128)(2,1)S(1)}, u32[]{:S(2)}, u32[]{:S(2)}) async-start(bf16[32,2,16,128]{3,2,1,0:T(8,128)(2,1)} %finish.1), calls=%async_computation.4 | async-start | bytes 524288 | tf_op jit(solution)/shard_map/all_to_all | solution.py:402
  124.6 11.2 %collective-permute-done.5.refs_2_ = bf16[64,32,128]{2,1,0:T(8,128)(2,1)S(1)} collective-permute-done((bf16[64,32,128]{2,1,0:T(8,128)(2,1)}, bf16[64,32,128]{2,1,0:T(8,128)(2,1)S(1)}, u32[]{:S(2)}, u32[]{:S(2)}) %collective-permute-start.5) | collective-permute-done | bytes 524320 | tf_op jit(solution)/shard_map/ppermute | solution.py:448
  135.9 0.0 copy-done
  135.9 0.0 copy-done.1
  135.9 2.7 %spread.1 = bf16[32,8192]{1,0:T(8,128)(2,1)} custom-call(s32[64]{0:T(128)S(1)} %copy-done.1, s32[1]{0:T(128)} %bitcast.16.place, bf16[32,32,128]{2,1,0:T(8,128)(2,1)S(1)} %bitcast.31, bf16[32,32,128]{2,1,0:T(8,128)(2,1)S(1)} %collective-permute-done.4.refs_1_, bf16[64,32,128]{2,1,0:T(8,128)(2,1)S(1)} %collective-permute-done.5.refs_2_, ...), custom_call_target="tpu_custom_call" | custom-call | flops 67108864 | bytes 6291456 | tf_op jit(solution)/shard_map/spread/pallas_call | solution.py:122
  138.6 0.0 all-to-all-done.4.gathered
  138.6 1.2 unpack.1
  (17 shorter events, 0.2 us)
Async XLA Ops:
  6.3 29.1 %copy-start.2 = (bf16[27,64,64]{2,1,0:T(8,128)(2,1)S(1)}, bf16[27,64,64]{2,1,0:T(8,128)(2,1)}, u32[]{:S(2)}) copy-start(bf16[27,64,64]{2,1,0:T(8,128)(2,1)} %param.12) | copy-start | bytes 663556
  25.4 20.6 %all-to-all-start.1 = ((bf16[32,32,128]{2,1,0:T(8,128)(2,1)}), bf16[32,32,128]{2,1,0:T(8,128)(2,1)S(1)}, u32[]{:S(2)}, u32[]{:S(2)}) async-start(bf16[32,32,128]{2,1,0:T(8,128)(2,1)} %add_x.1), calls=%async_computation.1 | async-start | bytes 524288 | tf_op jit(solution)/shard_map/all_to_all | solution.py:402
  36.3 2.7 %copy-start.3 = (bf16[32,2,2,128]{3,2,1,0:T(2,128)(2,1)S(1)}, bf16[32,2,2,128]{3,2,1,0:T(2,128)(2,1)}, u32[]{:S(2)}) copy-start(bf16[32,2,2,128]{3,2,1,0:T(2,128)(2,1)} %param.13) | copy-start | bytes 98308
  46.1 6.0 %collective-permute-start.1 = (bf16[6,32,128]{2,1,0:T(8,128)(2,1)S(1)}, bf16[6,32,128]{2,1,0:T(8,128)(2,1)S(1)}, u32[]{:S(2)}, u32[]{:S(2)}) collective-permute-start(bf16[6,32,128]{2,1,0:T(8,128)(2,1)S(1)} %get-tuple-element.36), channel_id=1, source_target_pairs={{16,0},{32,16},{48,32},{64,48},{80,64},{96,80},{112,96},{128,112},... | collective-permute-start | bytes 147464 | tf_op jit(solution)/shard_map/ppermute | solution.py:357
  48.0 8.1 %collective-permute-start = (bf16[6,32,128]{2,1,0:T(8,128)(2,1)S(1)}, bf16[6,32,128]{2,1,0:T(8,128)(2,1)S(1)}, u32[]{:S(2)}, u32[]{:S(2)}) collective-permute-start(bf16[6,32,128]{2,1,0:T(8,128)(2,1)S(1)} %get-tuple-element.35), channel_id=1, source_target_pairs={{0,16},{16,32},{32,48},{48,64},{64,80},{80,96},{96,112},{112,128},... | collective-permute-start | bytes 147464 | tf_op jit(solution)/shard_map/ppermute | solution.py:357
  56.2 6.0 %collective-permute-start.2 = (bf16[16,32,128]{2,1,0:T(8,128)(2,1)S(1)}, bf16[16,32,128]{2,1,0:T(8,128)(2,1)S(1)}, u32[]{:S(2)}, u32[]{:S(2)}) collective-permute-start(bf16[16,32,128]{2,1,0:T(8,128)(2,1)S(1)} %get-tuple-element.32), channel_id=1, source_target_pairs={{0,2},{2,4},{4,6},{6,8},{8,10},{10,12},{12,14},{1,3},{3,5},{5,7},{... | collective-permute-start | bytes 393224 | tf_op jit(solution)/shard_map/ppermute | solution.py:357
  59.7 6.9 %collective-permute-start.3 = (bf16[16,32,128]{2,1,0:T(8,128)(2,1)S(1)}, bf16[16,32,128]{2,1,0:T(8,128)(2,1)S(1)}, u32[]{:S(2)}, u32[]{:S(2)}) collective-permute-start(bf16[16,32,128]{2,1,0:T(8,128)(2,1)S(1)} %get-tuple-element.31), channel_id=1, source_target_pairs={{2,0},{4,2},{6,4},{8,6},{10,8},{12,10},{14,12},{3,1},{5,3},{7,5},{... | collective-permute-start | bytes 393224 | tf_op jit(solution)/shard_map/ppermute | solution.py:357
  71.6 64.2 %copy-start = (bf16[64,128,128]{2,1,0:T(8,128)(2,1)S(1)}, bf16[64,128,128]{2,1,0:T(8,128)(2,1)}, u32[]{:S(2)}) copy-start(bf16[64,128,128]{2,1,0:T(8,128)(2,1)} %get-tuple-element.28.refs_3_) | copy-start | bytes 6291460
  71.6 64.2 %copy-start.1 = (s32[64]{0:T(128)S(1)}, s32[64]{0:T(128)}, u32[]{:S(2)}) copy-start(s32[64]{0:T(128)} %target.3) | copy-start | bytes 772
  90.6 23.3 %all-to-all-start.3 = ((bf16[64,16,128]{2,1,0:T(8,128)(2,1)}), bf16[64,16,128]{2,1,0:T(8,128)(2,1)S(1)}, u32[]{:S(2)}, u32[]{:S(2)}) async-start(bf16[64,16,128]{2,1,0:T(8,128)(2,1)} %bitcast.14), calls=%async_computation.3 | async-start | bytes 524288 | tf_op jit(solution)/shard_map/all_to_all | solution.py:402
  102.3 12.3 %collective-permute-start.4 = (bf16[32,32,128]{2,1,0:T(8,128)(2,1)S(1)}, bf16[32,32,128]{2,1,0:T(8,128)(2,1)S(1)}, u32[]{:S(2)}, u32[]{:S(2)}) collective-permute-start(bf16[32,32,128]{2,1,0:T(8,128)(2,1)S(1)} %bitcast.29), channel_id=1, source_target_pairs={{0,128},{128,0},{256,384},{384,256},{16,144},{144,16},{272,400},{4... | collective-permute-start | bytes 786440 | tf_op jit(solution)/shard_map/ppermute | solution.py:438
  115.5 20.3 %collective-permute-start.5 = (bf16[64,32,128]{2,1,0:T(8,128)(2,1)}, bf16[64,32,128]{2,1,0:T(8,128)(2,1)S(1)}, u32[]{:S(2)}, u32[]{:S(2)}) collective-permute-start(bf16[64,32,128]{2,1,0:T(8,128)(2,1)} %pad_maximum_fusion), channel_id=1, source_target_pairs={{0,256},{128,384},{256,0},{384,128},{16,272},{144,400},{272,16},{4... | collective-permute-start | bytes 1572872 | tf_op jit(solution)/shard_map/ppermute | solution.py:448
  118.6 19.9 %all-to-all-start.4 = ((bf16[32,2,16,128]{3,2,1,0:T(8,128)(2,1)}), bf16[32,2,16,128]{3,2,1,0:T(8,128)(2,1)S(1)}, u32[]{:S(2)}, u32[]{:S(2)}) async-start(bf16[32,2,16,128]{3,2,1,0:T(8,128)(2,1)} %finish.1), calls=%async_computation.4 | async-start | bytes 524288 | tf_op jit(solution)/shard_map/all_to_all | solution.py:402

commit v8 on v7

--- a/solution.py
+++ b/solution.py
@@ -234,6 +234,21 @@
     return jnp.where(lane == depth - 1, 0.0, pltpu.roll(value, depth - 1, 1))
 
 
+def wide_products(weights, values, size, full):
+    depth = values.shape[2]
+    for x in range(size):
+        for y in range(0, size, 2):
+            total = None
+            for a in range(3):
+                window = jnp.concatenate(
+                    [values[x + a, (y + i) * full : (y + i + 3) * full, :] for i in range(2)], 1
+                )
+                product = jnp.dot(weights[a], window, preferred_element_type=jnp.float32)
+                total = product if total is None else total + product
+            for i in range(2):
+                yield x, y + i, total[:, i * depth : (i + 1) * depth]
+
+
 def conv_kernel_body(chan, grid, wf, wb, latent, message, pp, dd, hh):
     half, depth = grid.shape[2], grid.shape[3]
     full = 2 * half
@@ -251,48 +266,32 @@
                     rows = slice(y * full + c * half, y * full + (c + 1) * half)
                     pp[2 * s + x, rows, :] = grid[c, (0, 16, 36)[s] + 2 * y + x]
     lane = lax.broadcasted_iota(jnp.int32, (full, depth), 1)
-    for x in range(4):
-        for y in range(4):
-            grown = jnp.zeros((3 * full, depth), jnp.float32)
-            for a in range(3):
-                grown = grown + jnp.dot(
-                    wf[a],
-                    pp[x + a, y * full : (y + 3) * full, :],
-                    preferred_element_type=jnp.float32,
-                )
-            h = (
-                grown[full : 2 * full]
-                + later(grown[:full], lane)
-                + earlier(grown[2 * full :], lane)
-            )
-            sig = jax.nn.sigmoid(h)
-            upper = jnp.concatenate([cot(0, y, x), cot(1, y, x)], 0).astype(jnp.float32)
-            dd[x, y * full : (y + 1) * full, :] = (upper * sig * (1.0 + h * (1.0 - sig))).astype(
-                jnp.bfloat16
-            )
-            if x in (1, 2) and y in (1, 2):
-                hh[...] = h * sig
-                mine = pp[x + 1, pl.ds((y + 1) * full + first, half), :].astype(jnp.float32)
-                latent[:, x - 1, y - 1, :] = (mine + hh[pl.ds(first, half), :]).astype(jnp.bfloat16)
+    for x, y, grown in wide_products(wf, pp, 4, full):
+        h = (
+            grown[full : 2 * full]
+            + later(grown[:full], lane)
+            + earlier(grown[2 * full :], lane)
+        )
+        sig = jax.nn.sigmoid(h)
+        upper = jnp.concatenate([cot(0, y, x), cot(1, y, x)], 0).astype(jnp.float32)
+        dd[x, y * full : (y + 1) * full, :] = (upper * sig * (1.0 + h * (1.0 - sig))).astype(
+            jnp.bfloat16
+        )
+        if x in (1, 2) and y in (1, 2):
+            hh[...] = h * sig
+            mine = pp[x + 1, pl.ds((y + 1) * full + first, half), :].astype(jnp.float32)
+            latent[:, x - 1, y - 1, :] = (mine + hh[pl.ds(first, half), :]).astype(jnp.bfloat16)
     lane = lax.broadcasted_iota(jnp.int32, (half, depth), 1)
-    for x in range(2):
-        for y in range(2):
-            grown = jnp.zeros((3 * half, depth), jnp.float32)
-            for a in range(3):
-                grown = grown + jnp.dot(
-                    wb[a],
-                    dd[x + a, y * full : (y + 3) * full, :],
-                    preferred_element_type=jnp.float32,
-                )
-            dx = (
-                grown[half : 2 * half]
-                + earlier(grown[:half], lane)
-                + later(grown[2 * half :], lane)
-            )
-            own = cot(chan[0], y + 1, x + 1).astype(jnp.float32)
-            column = (own + dx).astype(jnp.bfloat16)
-            for d in range(n_dom):
-                message[d, (2 * y + x) * half : (2 * y + x + 1) * half, :] = column
+    for x, y, grown in wide_products(wb, dd, 2, full):
+        dx = (
+            grown[half : 2 * half]
+            + earlier(grown[:half], lane)
+            + later(grown[2 * half :], lane)
+        )
+        own = cot(chan[0], y + 1, x + 1).astype(jnp.float32)
+        column = (own + dx).astype(jnp.bfloat16)
+        for d in range(n_dom):
+            message[d, (2 * y + x) * half : (2 * y + x + 1) * half, :] = column
     moved = []
     for x in range(2):
         for y in range(2):
@@ -302,16 +301,17 @@
                     [earlier(own, lane), own, later(own, lane), jnp.zeros_like(own)], 0
                 ).astype(jnp.bfloat16)
             )
+    moved = jnp.concatenate(moved, 1)
     for a in range(3):
-        total = jnp.zeros((3 * full, 4 * half), jnp.float32)
-        for x in range(2):
-            for y in range(2):
-                total = total + lax.dot_general(
-                    pp[x + 1 + a, (y + 1) * full : (y + 4) * full, :],
-                    moved[2 * x + y],
-                    (((1,), (1,)), ((), ())),
-                    preferred_element_type=jnp.float32,
-                )
+        windows = [
+            pp[x + 1 + a, (y + 1) * full : (y + 4) * full, :] for x in range(2) for y in range(2)
+        ]
+        total = lax.dot_general(
+            jnp.concatenate(windows, 1),
+            moved,
+            (((1,), (1,)), ((), ())),
+            preferred_element_type=jnp.float32,
+        )
         for b in range(3):
             for e in range(3):
                 k = 9 * a + 3 * b + e
@@ -441,7 +441,6 @@
     )
     shape = (n_dom, 2, rows, depth)
     kgrad = in_vmem(functools.partial(finish_kernel, scale), "finish", shape, kgrad)
-    kgrad, parts = lax.optimization_barrier((kgrad, parts))
     kgrad = exchange(kgrad, "dom")
     shift = 2
     while shift < outer:

time: 140 us -> 139 us (level)
    ppermute x1, waiting for transfers between devices: 0.03 us -> 9.68 us  [body(): parts = [columns, lax.ppermute(columns, 'dom', paired(same_z, 1))]]
    all_to_all x3, waiting for transfers between devices: 15.8 us -> 6.93 us  [exchange(): lax.all_to_all(value, axis, split_axis=0, concat_axis=0, tiled=True, axis...]
  transfers between devices with their start and end apart: 9 -> 9, of which waited for: 7 -> 7; matrix products, arithmetic and copies ran while one was open for 3% -> 3% of each run, Pallas kernels for 2% -> 3%
where the time goes in v8:
time: 139 us; the launch traced here: 138 us
  starting transfers between devices  44.1 us (32%)
  blocking collectives  38.9 us (28%)
  waiting for transfers between devices  36.2 us (26%)
  Pallas kernels  12.8 us (9%)
  local copies, waits for them, and re-layouts  3.79 us (3%)
  between operations  1.51 us (1%)
    all_to_all x2, blocking collectives, exchange(): lax.all_to_all(value, axis, split_axis=0, concat_axis=0, tiled=True, axis...  36.5 us
    all_to_all x3, starting transfers between devices, exchange(): lax.all_to_all(value, axis, split_axis=0, concat_axis=0, tiled=True, axis...  27.7 us
    ppermute x4, starting transfers between devices, neighbours(): return (lax.ppermute(last, axis, up), lax.ppermute(first, axis, down))  10.6 us
    ppermute x1, waiting for transfers between devices, body(): lax.ppermute(jnp.concatenate(parts, 0), 'dom', paired(same_z, shift))  9.93 us
    ppermute x1, waiting for transfers between devices, body(): parts = [columns, lax.ppermute(columns, 'dom', paired(same_z, 1))]  9.68 us
    ppermute x4, waiting for transfers between devices, neighbours(): return (lax.ppermute(last, axis, up), lax.ppermute(first, axis, down))  9.64 us
    all_to_all x3, waiting for transfers between devices, exchange(): lax.all_to_all(value, axis, split_axis=0, concat_axis=0, tiled=True, axis...  6.93 us
    pallas_call x1, Pallas kernels, pool(): pl.pallas_call(pool_kernel, grid=(tiles // group,), in_specs=[smem, smem,...  4.99 us
  transfers between devices with their start and end apart: 9, of which 7 were waited for; matrix products, arithmetic and copies ran while one was open for 3% of the time, Pallas kernels for 3%

profile of v8, /device:TPU:6, one launch (start us, length us, event | category | flops | bytes accessed | tf_op | source)
XLA Modules:
  0.0 138.2 jit_solution(6752023735573936954)
XLA Ops:
  1.3 5.0 %pool.1 = (bf16[64,128,128]{2,1,0:T(8,128)(2,1)}, bf16[128,32,128]{2,1,0:T(8,128)(2,1)}) custom-call(s32[64]{0:T(128)} %target.3, s32[1]{0:T(128)S(6)} %copy.34.live, s32[8,8192]{1,0:T(8,128)} %cells.1, f32[8,8192]{1,0:T(8,128)} %weights.1, bf16[32,8192]{1,0:T(8,128)(2,1)} %feats.1), custom_call_target="tpu_custom_call" | custom-call | flops 67108864 | bytes 25165824 | tf_op jit(solution)/shard_map/pool/pallas_call | solution.py:70
  6.3 0.0 copy-start.2
  6.3 18.3 %all_to_all.25.received = bf16[128,32,128]{2,1,0:T(8,128)(2,1)S(1)} all-to-all(bf16[128,32,128]{2,1,0:T(8,128)(2,1)} %get-tuple-element.14), channel_id=1, replica_groups={{0,128,256,384},{16,144,272,400},{32,160,288,416},{48,176,304,432},{64,..., dimensions={0} | all-to-all | bytes 2097152 | tf_op jit(solution)/shard_map/all_to_all | solution.py:402
  24.6 0.8 add_x.1
  25.4 10.0 %all-to-all-start.1 = ((bf16[32,32,128]{2,1,0:T(8,128)(2,1)}), bf16[32,32,128]{2,1,0:T(8,128)(2,1)S(1)}, u32[]{:S(2)}, u32[]{:S(2)}) async-start(bf16[32,32,128]{2,1,0:T(8,128)(2,1)} %add_x.1), calls=%async_computation.1 | async-start | bytes 524288 | tf_op jit(solution)/shard_map/all_to_all | solution.py:402
  35.4 0.0 copy-done.2
  35.4 1.0 copy.22
  36.3 0.0 copy-start.3
  36.4 0.4 copy.23
  36.7 0.4 reshape.28.wf
  37.1 1.6 %rev.3 = bf16[3,3,3,64,64]{4,1,3,2,0:T(4,128)(2,1)S(1)} reverse(bf16[3,3,3,64,64]{4,1,3,2,0:T(4,128)(2,1)S(1)} %copy.23), dimensions={0,1} | reverse | bytes 442368 | tf_op jit(solution)/shard_map/rev | solution.py:393
  38.8 0.1 dynamic-slice_bitcast_fusion
  38.9 0.2 reshape.29.wb
  39.1 0.0 copy-done.3
  39.1 6.9 %all-to-all-done.1 = bf16[32,32,128]{2,1,0:T(8,128)(2,1)S(1)} async-done(((bf16[32,32,128]{2,1,0:T(8,128)(2,1)}), bf16[32,32,128]{2,1,0:T(8,128)(2,1)S(1)}, u32[]{:S(2)}, u32[]{:S(2)}) %all-to-all-start.1) | async-done | bytes 262176 | tf_op jit(solution)/shard_map/all_to_all | solution.py:402
  46.1 1.9 %collective-permute-start.1 = (bf16[6,32,128]{2,1,0:T(8,128)(2,1)S(1)}, bf16[6,32,128]{2,1,0:T(8,128)(2,1)S(1)}, u32[]{:S(2)}, u32[]{:S(2)}) collective-permute-start(bf16[6,32,128]{2,1,0:T(8,128)(2,1)S(1)} %get-tuple-element.30), channel_id=1, source_target_pairs={{16,0},{32,16},{48,32},{64,48},{80,64},{96,80},{112,96},{128,112},... | collective-permute-start | bytes 147464 | tf_op jit(solution)/shard_map/ppermute | solution.py:357
  48.0 3.9 %collective-permute-start = (bf16[6,32,128]{2,1,0:T(8,128)(2,1)S(1)}, bf16[6,32,128]{2,1,0:T(8,128)(2,1)S(1)}, u32[]{:S(2)}, u32[]{:S(2)}) collective-permute-start(bf16[6,32,128]{2,1,0:T(8,128)(2,1)S(1)} %get-tuple-element.29), channel_id=1, source_target_pairs={{0,16},{16,32},{32,48},{48,64},{64,80},{80,96},{96,112},{112,128},... | collective-permute-start | bytes 147464 | tf_op jit(solution)/shard_map/ppermute | solution.py:357
  52.0 0.1 collective-permute-done.1
  52.1 4.0 %collective-permute-done = bf16[6,32,128]{2,1,0:T(8,128)(2,1)S(1)} collective-permute-done((bf16[6,32,128]{2,1,0:T(8,128)(2,1)S(1)}, bf16[6,32,128]{2,1,0:T(8,128)(2,1)S(1)}, u32[]{:S(2)}, u32[]{:S(2)}) %collective-permute-start) | collective-permute-done | bytes 49184 | tf_op jit(solution)/shard_map/ppermute | solution.py:357
  56.2 3.5 %collective-permute-start.2 = (bf16[16,32,128]{2,1,0:T(8,128)(2,1)S(1)}, bf16[16,32,128]{2,1,0:T(8,128)(2,1)S(1)}, u32[]{:S(2)}, u32[]{:S(2)}) collective-permute-start(bf16[16,32,128]{2,1,0:T(8,128)(2,1)S(1)} %get-tuple-element.26), channel_id=1, source_target_pairs={{0,2},{2,4},{4,6},{6,8},{8,10},{10,12},{12,14},{1,3},{3,5},{5,7},{... | collective-permute-start | bytes 393224 | tf_op jit(solution)/shard_map/ppermute | solution.py:357
  59.7 1.3 collective-permute-start.3
  61.0 1.2 collective-permute-done.2
  62.3 4.3 %collective-permute-done.3 = bf16[16,32,128]{2,1,0:T(8,128)(2,1)S(1)} collective-permute-done((bf16[16,32,128]{2,1,0:T(8,128)(2,1)S(1)}, bf16[16,32,128]{2,1,0:T(8,128)(2,1)S(1)}, u32[]{:S(2)}, u32[]{:S(2)}) %collective-permute-start.3) | collective-permute-done | bytes 131104 | tf_op jit(solution)/shard_map/ppermute | solution.py:357
  66.6 2.4 %all-gather = bf16[104,32,128]{2,1,0:T(8,128)(2,1)S(1)} all-gather(bf16[52,32,128]{2,1,0:T(8,128)(2,1)S(1)} %constant_dynamic-update-slice_fusion), channel_id=2, replica_groups=mesh['dom'=32,'slab'=8,'chan'=2] {'chan'}, dimensions={0}, use_global_device_ids=true | all-gather | bytes 1277952 | tf_op jit(solution)/shard_map/all_gather | solution.py:425
  69.0 1.6 %conv_layer.1 = (bf16[32,2,2,128]{3,2,1,0:T(2,128)(2,1)}, bf16[8,192,128]{2,1,0:T(8,128)(2,1)S(1)}) custom-call(s32[1]{0:T(128)} %bitcast.chan, bf16[2,52,32,128]{3,2,1,0:T(8,128)(2,1)S(1)} %bitcast.28, bf16[3,192,192]{2,1,0:T(8,128)(2,1)S(1)} %reshape.28.wf, bf16[3,96,192]{2,1,0:T(8,128)(2,1)S(1)} %reshape.29.wb), custom_call_target="tpu_custom_call" | custom-call | tf_op jit(solution)/shard_map/conv_layer/pallas_call | solution.py:335
  70.6 0.0 copy-start
  70.6 0.0 copy-start.1
  70.6 18.2 %all_to_all.26.received = bf16[8,192,128]{2,1,0:T(8,128)(2,1)S(1)} all-to-all(bf16[8,192,128]{2,1,0:T(8,128)(2,1)S(1)} %get-tuple-element.19), channel_id=1, replica_groups={{0,16,32,48,64,80,96,112},{128,144,160,176,192,208,224,240},{256,272,28..., dimensions={0} | all-to-all | bytes 786432 | tf_op jit(solution)/shard_map/all_to_all | solution.py:402
  88.8 0.7 split.1
  89.5 11.8 %all-to-all-start.3 = ((bf16[64,16,128]{2,1,0:T(8,128)(2,1)}), bf16[64,16,128]{2,1,0:T(8,128)(2,1)S(1)}, u32[]{:S(2)}, u32[]{:S(2)}) async-start(bf16[64,16,128]{2,1,0:T(8,128)(2,1)} %bitcast.14), calls=%async_computation.3 | async-start | bytes 524288 | tf_op jit(solution)/shard_map/all_to_all | solution.py:402
  101.3 2.7 %collective-permute-start.4 = (bf16[32,32,128]{2,1,0:T(8,128)(2,1)S(1)}, bf16[32,32,128]{2,1,0:T(8,128)(2,1)S(1)}, u32[]{:S(2)}, u32[]{:S(2)}) collective-permute-start(bf16[32,32,128]{2,1,0:T(8,128)(2,1)S(1)} %bitcast.29), channel_id=1, source_target_pairs={{0,128},{128,0},{256,384},{384,256},{16,144},{144,16},{272,400},{4... | collective-permute-start | bytes 786440 | tf_op jit(solution)/shard_map/ppermute | solution.py:438
  104.0 9.7 %collective-permute-done.4.refs_1_ = bf16[32,32,128]{2,1,0:T(8,128)(2,1)S(1)} collective-permute-done((bf16[32,32,128]{2,1,0:T(8,128)(2,1)S(1)}, bf16[32,32,128]{2,1,0:T(8,128)(2,1)S(1)}, u32[]{:S(2)}, u32[]{:S(2)}) %collective-permute-start.4) | collective-permute-done | bytes 262176 | tf_op jit(solution)/shard_map/ppermute | solution.py:438
  113.7 0.8 pad_maximum_fusion
  114.5 3.0 %collective-permute-start.5 = (bf16[64,32,128]{2,1,0:T(8,128)(2,1)}, bf16[64,32,128]{2,1,0:T(8,128)(2,1)S(1)}, u32[]{:S(2)}, u32[]{:S(2)}) collective-permute-start(bf16[64,32,128]{2,1,0:T(8,128)(2,1)} %pad_maximum_fusion), channel_id=1, source_target_pairs={{0,256},{128,384},{256,0},{384,128},{16,272},{144,400},{272,16},{4... | collective-permute-start | bytes 1572872 | tf_op jit(solution)/shard_map/ppermute | solution.py:447
  117.6 0.0 all-to-all-done.3.received
  117.6 0.8 finish.1
  118.3 6.0 %all-to-all-start.4 = ((bf16[32,2,16,128]{3,2,1,0:T(8,128)(2,1)}), bf16[32,2,16,128]{3,2,1,0:T(8,128)(2,1)S(1)}, u32[]{:S(2)}, u32[]{:S(2)}) async-start(bf16[32,2,16,128]{3,2,1,0:T(8,128)(2,1)} %finish.1), calls=%async_computation.4 | async-start | bytes 524288 | tf_op jit(solution)/shard_map/all_to_all | solution.py:402
  124.4 9.9 %collective-permute-done.5.refs_2_ = bf16[64,32,128]{2,1,0:T(8,128)(2,1)S(1)} collective-permute-done((bf16[64,32,128]{2,1,0:T(8,128)(2,1)}, bf16[64,32,128]{2,1,0:T(8,128)(2,1)S(1)}, u32[]{:S(2)}, u32[]{:S(2)}) %collective-permute-start.5) | collective-permute-done | bytes 524320 | tf_op jit(solution)/shard_map/ppermute | solution.py:447
  134.3 0.0 copy-done
  134.3 0.0 copy-done.1
  134.3 2.7 %spread.1 = bf16[32,8192]{1,0:T(8,128)(2,1)} custom-call(s32[64]{0:T(128)S(1)} %copy-done.1, s32[1]{0:T(128)} %bitcast.15.place, bf16[32,32,128]{2,1,0:T(8,128)(2,1)S(1)} %bitcast.31, bf16[32,32,128]{2,1,0:T(8,128)(2,1)S(1)} %collective-permute-done.4.refs_1_, bf16[64,32,128]{2,1,0:T(8,128)(2,1)S(1)} %collective-permute-done.5.refs_2_, ...), custom_call_target="tpu_custom_call" | custom-call | flops 67108864 | bytes 6291456 | tf_op jit(solution)/shard_map/spread/pallas_call | solution.py:122
  137.0 0.0 all-to-all-done.4.gathered
  137.0 1.2 unpack.1
  (17 shorter events, 0.2 us)
Async XLA Ops:
  6.3 29.1 %copy-start.2 = (bf16[27,64,64]{2,1,0:T(8,128)(2,1)S(1)}, bf16[27,64,64]{2,1,0:T(8,128)(2,1)}, u32[]{:S(2)}) copy-start(bf16[27,64,64]{2,1,0:T(8,128)(2,1)} %param.12) | copy-start | bytes 663556
  25.4 20.6 %all-to-all-start.1 = ((bf16[32,32,128]{2,1,0:T(8,128)(2,1)}), bf16[32,32,128]{2,1,0:T(8,128)(2,1)S(1)}, u32[]{:S(2)}, u32[]{:S(2)}) async-start(bf16[32,32,128]{2,1,0:T(8,128)(2,1)} %add_x.1), calls=%async_computation.1 | async-start | bytes 524288 | tf_op jit(solution)/shard_map/all_to_all | solution.py:402
  36.3 2.7 %copy-start.3 = (bf16[32,2,2,128]{3,2,1,0:T(2,128)(2,1)S(1)}, bf16[32,2,2,128]{3,2,1,0:T(2,128)(2,1)}, u32[]{:S(2)}) copy-start(bf16[32,2,2,128]{3,2,1,0:T(2,128)(2,1)} %param.13) | copy-start | bytes 98308
  46.1 6.0 %collective-permute-start.1 = (bf16[6,32,128]{2,1,0:T(8,128)(2,1)S(1)}, bf16[6,32,128]{2,1,0:T(8,128)(2,1)S(1)}, u32[]{:S(2)}, u32[]{:S(2)}) collective-permute-start(bf16[6,32,128]{2,1,0:T(8,128)(2,1)S(1)} %get-tuple-element.30), channel_id=1, source_target_pairs={{16,0},{32,16},{48,32},{64,48},{80,64},{96,80},{112,96},{128,112},... | collective-permute-start | bytes 147464 | tf_op jit(solution)/shard_map/ppermute | solution.py:357
  48.0 8.1 %collective-permute-start = (bf16[6,32,128]{2,1,0:T(8,128)(2,1)S(1)}, bf16[6,32,128]{2,1,0:T(8,128)(2,1)S(1)}, u32[]{:S(2)}, u32[]{:S(2)}) collective-permute-start(bf16[6,32,128]{2,1,0:T(8,128)(2,1)S(1)} %get-tuple-element.29), channel_id=1, source_target_pairs={{0,16},{16,32},{32,48},{48,64},{64,80},{80,96},{96,112},{112,128},... | collective-permute-start | bytes 147464 | tf_op jit(solution)/shard_map/ppermute | solution.py:357
  56.2 6.0 %collective-permute-start.2 = (bf16[16,32,128]{2,1,0:T(8,128)(2,1)S(1)}, bf16[16,32,128]{2,1,0:T(8,128)(2,1)S(1)}, u32[]{:S(2)}, u32[]{:S(2)}) collective-permute-start(bf16[16,32,128]{2,1,0:T(8,128)(2,1)S(1)} %get-tuple-element.26), channel_id=1, source_target_pairs={{0,2},{2,4},{4,6},{6,8},{8,10},{10,12},{12,14},{1,3},{3,5},{5,7},{... | collective-permute-start | bytes 393224 | tf_op jit(solution)/shard_map/ppermute | solution.py:357
  59.7 6.9 %collective-permute-start.3 = (bf16[16,32,128]{2,1,0:T(8,128)(2,1)S(1)}, bf16[16,32,128]{2,1,0:T(8,128)(2,1)S(1)}, u32[]{:S(2)}, u32[]{:S(2)}) collective-permute-start(bf16[16,32,128]{2,1,0:T(8,128)(2,1)S(1)} %get-tuple-element.25), channel_id=1, source_target_pairs={{2,0},{4,2},{6,4},{8,6},{10,8},{12,10},{14,12},{3,1},{5,3},{7,5},{... | collective-permute-start | bytes 393224 | tf_op jit(solution)/shard_map/ppermute | solution.py:357
  70.6 63.7 %copy-start = (bf16[64,128,128]{2,1,0:T(8,128)(2,1)S(1)}, bf16[64,128,128]{2,1,0:T(8,128)(2,1)}, u32[]{:S(2)}) copy-start(bf16[64,128,128]{2,1,0:T(8,128)(2,1)} %get-tuple-element.22.refs_3_) | copy-start | bytes 6291460
  70.6 63.7 %copy-start.1 = (s32[64]{0:T(128)S(1)}, s32[64]{0:T(128)}, u32[]{:S(2)}) copy-start(s32[64]{0:T(128)} %target.3) | copy-start | bytes 772
  89.5 28.0 %all-to-all-start.3 = ((bf16[64,16,128]{2,1,0:T(8,128)(2,1)}), bf16[64,16,128]{2,1,0:T(8,128)(2,1)S(1)}, u32[]{:S(2)}, u32[]{:S(2)}) async-start(bf16[64,16,128]{2,1,0:T(8,128)(2,1)} %bitcast.14), calls=%async_computation.3 | async-start | bytes 524288 | tf_op jit(solution)/shard_map/all_to_all | solution.py:402
  101.3 12.3 %collective-permute-start.4 = (bf16[32,32,128]{2,1,0:T(8,128)(2,1)S(1)}, bf16[32,32,128]{2,1,0:T(8,128)(2,1)S(1)}, u32[]{:S(2)}, u32[]{:S(2)}) collective-permute-start(bf16[32,32,128]{2,1,0:T(8,128)(2,1)S(1)} %bitcast.29), channel_id=1, source_target_pairs={{0,128},{128,0},{256,384},{384,256},{16,144},{144,16},{272,400},{4... | collective-permute-start | bytes 786440 | tf_op jit(solution)/shard_map/ppermute | solution.py:438
  114.5 19.8 %collective-permute-start.5 = (bf16[64,32,128]{2,1,0:T(8,128)(2,1)}, bf16[64,32,128]{2,1,0:T(8,128)(2,1)S(1)}, u32[]{:S(2)}, u32[]{:S(2)}) collective-permute-start(bf16[64,32,128]{2,1,0:T(8,128)(2,1)} %pad_maximum_fusion), channel_id=1, source_target_pairs={{0,256},{128,384},{256,0},{384,128},{16,272},{144,400},{272,16},{4... | collective-permute-start | bytes 1572872 | tf_op jit(solution)/shard_map/ppermute | solution.py:447
  118.3 18.7 %all-to-all-start.4 = ((bf16[32,2,16,128]{3,2,1,0:T(8,128)(2,1)}), bf16[32,2,16,128]{3,2,1,0:T(8,128)(2,1)S(1)}, u32[]{:S(2)}, u32[]{:S(2)}) async-start(bf16[32,2,16,128]{3,2,1,0:T(8,128)(2,1)} %finish.1), calls=%async_computation.4 | async-start | bytes 524288 | tf_op jit(solution)/shard_map/all_to_all | solution.py:402

commit v9 on v8

--- a/solution.py
+++ b/solution.py
@@ -151,6 +151,14 @@
     for part in parts[1:]:
         total = total + part.astype(jnp.float32)
     return total
+
+
+def join_kernel(*refs):
+    *parts, out = refs
+    first = 0
+    for part in parts:
+        out[first : first + part.shape[0]] = part[...]
+        first += part.shape[0]
 
 
 def add_kernel(received, out):
@@ -406,15 +414,15 @@
     def total(value, parts):
         return value.reshape((parts, -1) + value.shape[1:]).astype(jnp.float32).sum(0)
 
+    cot = cotangent.transpose(2, 1, 0, 3)
     part = exchange(send, "dom", same_z)
+    part, wf, wb, cot, low, high = lax.optimization_barrier((part, wf, wb, cot, cot[0], cot[-1]))
     part = in_vmem(add_kernel, "add_x", (part.shape[0] // outer,) + part.shape[1:], part)
     part = exchange(part, "dom", same_x)
-    part, wf, wb = lax.optimization_barrier((part, wf, wb))
     pooled = total(part, inner).astype(jnp.bfloat16)
 
-    cot = cotangent.transpose(2, 1, 0, 3)
     before, after = neighbours(
-        jnp.concatenate([pooled, cot[0]], 0), jnp.concatenate([pooled, cot[-1]], 0), "dom"
+        jnp.concatenate([pooled, low], 0), jnp.concatenate([pooled, high], 0), "dom"
     )
     pooled = jnp.concatenate([before[:width], pooled, after[:width]], 0)
     cot = jnp.concatenate([before[None, width:], cot, after[None, width:]], 0)
@@ -444,7 +452,9 @@
     kgrad = exchange(kgrad, "dom")
     shift = 2
     while shift < outer:
-        parts.append(lax.ppermute(jnp.concatenate(parts, 0), "dom", paired(same_z, shift)))
+        shape = (shift * parts[0].shape[0],) + parts[0].shape[1:]
+        joined = in_vmem(join_kernel, "join", shape, *parts)
+        parts.append(lax.ppermute(joined, "dom", paired(same_z, shift)))
         shift = 2 * shift
     place = (lax.axis_index("dom") // inner).astype(jnp.int32)
     feature_grad = spread(tile_target, place[None], parts, blocks)

time: 139 us -> 137 us (0.986)
  blocking collectives: 38.9 us -> 41 us
  waiting for transfers between devices: 36.2 us -> 34.2 us
    all_to_all x2, blocking collectives: 36.5 us -> 38.6 us  [exchange(): lax.all_to_all(value, axis, split_axis=0, concat_axis=0, tiled=True, axis...]
    all_to_all x3, waiting for transfers between devices: 6.93 us -> 5.08 us  [exchange(): lax.all_to_all(value, axis, split_axis=0, concat_axis=0, tiled=True, axis...]
where the time goes in v9:
time: 137 us
  starting transfers between devices  43.5 us (32%)
  blocking collectives  41 us (30%)
  waiting for transfers between devices  34.2 us (25%)
  Pallas kernels  12.6 us (9%)
  local copies, waits for them, and re-layouts  3.79 us (3%)
  between operations  1.57 us (1%)
    all_to_all x2, blocking collectives, exchange(): lax.all_to_all(value, axis, split_axis=0, concat_axis=0, tiled=True, axis...  38.6 us
    all_to_all x3, starting transfers between devices, exchange(): lax.all_to_all(value, axis, split_axis=0, concat_axis=0, tiled=True, axis...  27.1 us
    ppermute x4, starting transfers between devices, neighbours(): return (lax.ppermute(last, axis, up), lax.ppermute(first, axis, down))  10.6 us
    ppermute x1, waiting for transfers between devices, body(): parts.append(lax.ppermute(joined, 'dom', paired(same_z, shift)))  9.82 us
    ppermute x1, waiting for transfers between devices, body(): parts = [columns, lax.ppermute(columns, 'dom', paired(same_z, 1))]  9.68 us
    ppermute x4, waiting for transfers between devices, neighbours(): return (lax.ppermute(last, axis, up), lax.ppermute(first, axis, down))  9.64 us
    all_to_all x3, waiting for transfers between devices, exchange(): lax.all_to_all(value, axis, split_axis=0, concat_axis=0, tiled=True, axis...  5.08 us
    pallas_call x1, Pallas kernels, pool(): pl.pallas_call(pool_kernel, grid=(tiles // group,), in_specs=[smem, smem,...  4.99 us
  transfers between devices with their start and end apart: 9, of which 7 were waited for; matrix products, arithmetic and copies ran while one was open for 3% of the time, Pallas kernels for 3%

profile of v9, /device:TPU:6, one launch (start us, length us, event | category | flops | bytes accessed | tf_op | source)
XLA Modules:
  0.0 136.8 jit_solution(8602904988298186276)
XLA Ops:
  0.6 0.0 copy-start.2
  1.3 5.0 %pool.1 = (bf16[64,128,128]{2,1,0:T(8,128)(2,1)}, bf16[128,32,128]{2,1,0:T(8,128)(2,1)}) custom-call(s32[64]{0:T(128)} %target.3, s32[1]{0:T(128)S(6)} %copy.34.live, s32[8,8192]{1,0:T(8,128)} %cells.1, f32[8,8192]{1,0:T(8,128)} %weights.1, bf16[32,8192]{1,0:T(8,128)(2,1)} %feats.1), custom_call_target="tpu_custom_call" | custom-call | flops 67108864 | bytes 25165824 | tf_op jit(solution)/shard_map/pool/pallas_call | solution.py:70
  6.3 9.3 %all-to-all-start = ((bf16[128,32,128]{2,1,0:T(8,128)(2,1)}), bf16[128,32,128]{2,1,0:T(8,128)(2,1)S(1)}, u32[]{:S(2)}, u32[]{:S(2)}) async-start(bf16[128,32,128]{2,1,0:T(8,128)(2,1)} %get-tuple-element.17), calls=%async_computation | async-start | bytes 2097152 | tf_op jit(solution)/shard_map/all_to_all | solution.py:410
  15.7 0.0 copy-done.2
  15.7 0.0 copy-start.3
  15.7 0.4 copy.23
  16.1 1.0 copy.22
  17.0 1.6 %rev.3 = bf16[3,3,3,64,64]{4,1,3,2,0:T(4,128)(2,1)S(1)} reverse(bf16[3,3,3,64,64]{4,1,3,2,0:T(4,128)(2,1)S(1)} %copy.23), dimensions={0,1} | reverse | bytes 442368 | tf_op jit(solution)/shard_map/rev | solution.py:401
  18.7 0.1 dynamic-slice_bitcast_fusion
  18.8 0.2 reshape.29.wb
  19.0 0.0 copy-done.3
  19.1 0.4 reshape.28.wf
  19.4 5.1 %all-to-all-done.received = bf16[128,32,128]{2,1,0:T(8,128)(2,1)S(1)} async-done(((bf16[128,32,128]{2,1,0:T(8,128)(2,1)}), bf16[128,32,128]{2,1,0:T(8,128)(2,1)S(1)}, u32[]{:S(2)}, u32[]{:S(2)}) %all-to-all-start) | async-done | bytes 1048608 | tf_op jit(solution)/shard_map/all_to_all | solution.py:410
  24.5 0.1 add_x.1
  24.6 20.4 %all_to_all.25 = bf16[32,32,128]{2,1,0:T(8,128)(2,1)S(1)} all-to-all(bf16[32,32,128]{2,1,0:T(8,128)(2,1)S(1)} %add_x.1), channel_id=1, replica_groups={{0,16,32,48,64,80,96,112},{128,144,160,176,192,208,224,240},{256,272,28..., dimensions={0} | all-to-all | bytes 524288 | tf_op jit(solution)/shard_map/all_to_all | solution.py:410
  45.1 1.9 %collective-permute-start.1 = (bf16[6,32,128]{2,1,0:T(8,128)(2,1)S(1)}, bf16[6,32,128]{2,1,0:T(8,128)(2,1)S(1)}, u32[]{:S(2)}, u32[]{:S(2)}) collective-permute-start(bf16[6,32,128]{2,1,0:T(8,128)(2,1)S(1)} %get-tuple-element.36), channel_id=1, source_target_pairs={{16,0},{32,16},{48,32},{64,48},{80,64},{96,80},{112,96},{128,112},... | collective-permute-start | bytes 147464 | tf_op jit(solution)/shard_map/ppermute | solution.py:365
  47.1 3.9 %collective-permute-start = (bf16[6,32,128]{2,1,0:T(8,128)(2,1)S(1)}, bf16[6,32,128]{2,1,0:T(8,128)(2,1)S(1)}, u32[]{:S(2)}, u32[]{:S(2)}) collective-permute-start(bf16[6,32,128]{2,1,0:T(8,128)(2,1)S(1)} %get-tuple-element.35), channel_id=1, source_target_pairs={{0,16},{16,32},{32,48},{48,64},{64,80},{80,96},{96,112},{112,128},... | collective-permute-start | bytes 147464 | tf_op jit(solution)/shard_map/ppermute | solution.py:365
  51.0 0.1 collective-permute-done.1
  51.1 4.0 %collective-permute-done = bf16[6,32,128]{2,1,0:T(8,128)(2,1)S(1)} collective-permute-done((bf16[6,32,128]{2,1,0:T(8,128)(2,1)S(1)}, bf16[6,32,128]{2,1,0:T(8,128)(2,1)S(1)}, u32[]{:S(2)}, u32[]{:S(2)}) %collective-permute-start) | collective-permute-done | bytes 49184 | tf_op jit(solution)/shard_map/ppermute | solution.py:365
  55.2 3.5 %collective-permute-start.2 = (bf16[16,32,128]{2,1,0:T(8,128)(2,1)S(1)}, bf16[16,32,128]{2,1,0:T(8,128)(2,1)S(1)}, u32[]{:S(2)}, u32[]{:S(2)}) collective-permute-start(bf16[16,32,128]{2,1,0:T(8,128)(2,1)S(1)} %get-tuple-element.32), channel_id=1, source_target_pairs={{0,2},{2,4},{4,6},{6,8},{8,10},{10,12},{12,14},{1,3},{3,5},{5,7},{... | collective-permute-start | bytes 393224 | tf_op jit(solution)/shard_map/ppermute | solution.py:365
  58.7 1.3 collective-permute-start.3
  60.0 1.2 collective-permute-done.2
  61.3 4.3 %collective-permute-done.3 = bf16[16,32,128]{2,1,0:T(8,128)(2,1)S(1)} collective-permute-done((bf16[16,32,128]{2,1,0:T(8,128)(2,1)S(1)}, bf16[16,32,128]{2,1,0:T(8,128)(2,1)S(1)}, u32[]{:S(2)}, u32[]{:S(2)}) %collective-permute-start.3) | collective-permute-done | bytes 131104 | tf_op jit(solution)/shard_map/ppermute | solution.py:365
  65.6 2.4 %all-gather = bf16[104,32,128]{2,1,0:T(8,128)(2,1)S(1)} all-gather(bf16[52,32,128]{2,1,0:T(8,128)(2,1)S(1)} %constant_dynamic-update-slice_fusion), channel_id=2, replica_groups=mesh['dom'=32,'slab'=8,'chan'=2] {'chan'}, dimensions={0}, use_global_device_ids=true | all-gather | bytes 1277952 | tf_op jit(solution)/shard_map/all_gather | solution.py:433
  68.0 1.6 %conv_layer.1 = (bf16[32,2,2,128]{3,2,1,0:T(2,128)(2,1)}, bf16[8,192,128]{2,1,0:T(8,128)(2,1)S(1)}) custom-call(s32[1]{0:T(128)} %bitcast.chan, bf16[2,52,32,128]{3,2,1,0:T(8,128)(2,1)S(1)} %bitcast.28, bf16[3,192,192]{2,1,0:T(8,128)(2,1)S(1)} %reshape.28.wf, bf16[3,96,192]{2,1,0:T(8,128)(2,1)S(1)} %reshape.29.wb), custom_call_target="tpu_custom_call" | custom-call | tf_op jit(solution)/shard_map/conv_layer/pallas_call | solution.py:343
  69.6 0.0 copy-start
  69.6 0.0 copy-start.1
  69.6 18.2 %all_to_all.26.received = bf16[8,192,128]{2,1,0:T(8,128)(2,1)S(1)} all-to-all(bf16[8,192,128]{2,1,0:T(8,128)(2,1)S(1)} %get-tuple-element.25), channel_id=1, replica_groups={{0,16,32,48,64,80,96,112},{128,144,160,176,192,208,224,240},{256,272,28..., dimensions={0} | all-to-all | bytes 786432 | tf_op jit(solution)/shard_map/all_to_all | solution.py:410
  87.8 0.7 split.1
  88.5 11.8 %all-to-all-start.3 = ((bf16[64,16,128]{2,1,0:T(8,128)(2,1)}), bf16[64,16,128]{2,1,0:T(8,128)(2,1)S(1)}, u32[]{:S(2)}, u32[]{:S(2)}) async-start(bf16[64,16,128]{2,1,0:T(8,128)(2,1)} %bitcast.14), calls=%async_computation.3 | async-start | bytes 524288 | tf_op jit(solution)/shard_map/all_to_all | solution.py:410
  100.3 2.7 %collective-permute-start.4 = (bf16[32,32,128]{2,1,0:T(8,128)(2,1)S(1)}, bf16[32,32,128]{2,1,0:T(8,128)(2,1)S(1)}, u32[]{:S(2)}, u32[]{:S(2)}) collective-permute-start(bf16[32,32,128]{2,1,0:T(8,128)(2,1)S(1)} %bitcast.29), channel_id=1, source_target_pairs={{0,128},{128,0},{256,384},{384,256},{16,144},{144,16},{272,400},{4... | collective-permute-start | bytes 786440 | tf_op jit(solution)/shard_map/ppermute | solution.py:446
  103.0 9.7 %collective-permute-done.4.refs_1_ = bf16[32,32,128]{2,1,0:T(8,128)(2,1)S(1)} collective-permute-done((bf16[32,32,128]{2,1,0:T(8,128)(2,1)S(1)}, bf16[32,32,128]{2,1,0:T(8,128)(2,1)S(1)}, u32[]{:S(2)}, u32[]{:S(2)}) %collective-permute-start.4) | collective-permute-done | bytes 262176 | tf_op jit(solution)/shard_map/ppermute | solution.py:446
  112.7 3.1 %collective-permute-start.5 = (bf16[64,32,128]{2,1,0:T(8,128)(2,1)S(1)}, bf16[64,32,128]{2,1,0:T(8,128)(2,1)}, u32[]{:S(2)}, u32[]{:S(2)}) collective-permute-start(bf16[64,32,128]{2,1,0:T(8,128)(2,1)S(1)} %join.1), channel_id=1, source_target_pairs={{0,256},{128,384},{256,0},{384,128},{16,272},{144,400},{272,16},{4... | collective-permute-start | bytes 1572872 | tf_op jit(solution)/shard_map/ppermute | solution.py:457
  115.8 0.0 all-to-all-done.3.received
  115.8 0.8 finish.1
  116.5 6.0 %all-to-all-start.4 = ((bf16[32,2,16,128]{3,2,1,0:T(8,128)(2,1)}), bf16[32,2,16,128]{3,2,1,0:T(8,128)(2,1)S(1)}, u32[]{:S(2)}, u32[]{:S(2)}) async-start(bf16[32,2,16,128]{3,2,1,0:T(8,128)(2,1)} %finish.1), calls=%async_computation.4 | async-start | bytes 524288 | tf_op jit(solution)/shard_map/all_to_all | solution.py:410
  122.6 9.8 %collective-permute-done.5.refs_2_ = bf16[64,32,128]{2,1,0:T(8,128)(2,1)} collective-permute-done((bf16[64,32,128]{2,1,0:T(8,128)(2,1)S(1)}, bf16[64,32,128]{2,1,0:T(8,128)(2,1)}, u32[]{:S(2)}, u32[]{:S(2)}) %collective-permute-start.5) | collective-permute-done | bytes 524320 | tf_op jit(solution)/shard_map/ppermute | solution.py:457
  132.4 0.0 copy-done
  132.4 0.0 copy-done.1
  132.4 3.2 %spread.1 = bf16[32,8192]{1,0:T(8,128)(2,1)} custom-call(s32[64]{0:T(128)S(1)} %copy-done.1, s32[1]{0:T(128)} %bitcast.15.place, bf16[32,32,128]{2,1,0:T(8,128)(2,1)S(1)} %bitcast.31, bf16[32,32,128]{2,1,0:T(8,128)(2,1)S(1)} %collective-permute-done.4.refs_1_, bf16[64,32,128]{2,1,0:T(8,128)(2,1)} %collective-permute-done.5.refs_2_, ...), custom_call_target="tpu_custom_call" | custom-call | flops 67108864 | bytes 6291456 | tf_op jit(solution)/shard_map/spread/pallas_call | solution.py:122
  135.7 0.0 all-to-all-done.4.gathered
  135.7 1.2 unpack.1
  (18 shorter events, 0.2 us)
Async XLA Ops:
  0.6 15.0 %copy-start.2 = (bf16[27,64,64]{2,1,0:T(8,128)(2,1)S(1)}, bf16[27,64,64]{2,1,0:T(8,128)(2,1)}, u32[]{:S(2)}) copy-start(bf16[27,64,64]{2,1,0:T(8,128)(2,1)} %param.12) | copy-start | bytes 663556
  6.3 18.2 %all-to-all-start = ((bf16[128,32,128]{2,1,0:T(8,128)(2,1)}), bf16[128,32,128]{2,1,0:T(8,128)(2,1)S(1)}, u32[]{:S(2)}, u32[]{:S(2)}) async-start(bf16[128,32,128]{2,1,0:T(8,128)(2,1)} %get-tuple-element.17), calls=%async_computation | async-start | bytes 2097152 | tf_op jit(solution)/shard_map/all_to_all | solution.py:410
  15.7 3.4 %copy-start.3 = (bf16[32,2,2,128]{3,2,1,0:T(2,128)(2,1)S(1)}, bf16[32,2,2,128]{3,2,1,0:T(2,128)(2,1)}, u32[]{:S(2)}) copy-start(bf16[32,2,2,128]{3,2,1,0:T(2,128)(2,1)} %param.13) | copy-start | bytes 98308
  45.1 6.0 %collective-permute-start.1 = (bf16[6,32,128]{2,1,0:T(8,128)(2,1)S(1)}, bf16[6,32,128]{2,1,0:T(8,128)(2,1)S(1)}, u32[]{:S(2)}, u32[]{:S(2)}) collective-permute-start(bf16[6,32,128]{2,1,0:T(8,128)(2,1)S(1)} %get-tuple-element.36), channel_id=1, source_target_pairs={{16,0},{32,16},{48,32},{64,48},{80,64},{96,80},{112,96},{128,112},... | collective-permute-start | bytes 147464 | tf_op jit(solution)/shard_map/ppermute | solution.py:365
  47.1 8.1 %collective-permute-start = (bf16[6,32,128]{2,1,0:T(8,128)(2,1)S(1)}, bf16[6,32,128]{2,1,0:T(8,128)(2,1)S(1)}, u32[]{:S(2)}, u32[]{:S(2)}) collective-permute-start(bf16[6,32,128]{2,1,0:T(8,128)(2,1)S(1)} %get-tuple-element.35), channel_id=1, source_target_pairs={{0,16},{16,32},{32,48},{48,64},{64,80},{80,96},{96,112},{112,128},... | collective-permute-start | bytes 147464 | tf_op jit(solution)/shard_map/ppermute | solution.py:365
  55.2 6.0 %collective-permute-start.2 = (bf16[16,32,128]{2,1,0:T(8,128)(2,1)S(1)}, bf16[16,32,128]{2,1,0:T(8,128)(2,1)S(1)}, u32[]{:S(2)}, u32[]{:S(2)}) collective-permute-start(bf16[16,32,128]{2,1,0:T(8,128)(2,1)S(1)} %get-tuple-element.32), channel_id=1, source_target_pairs={{0,2},{2,4},{4,6},{6,8},{8,10},{10,12},{12,14},{1,3},{3,5},{5,7},{... | collective-permute-start | bytes 393224 | tf_op jit(solution)/shard_map/ppermute | solution.py:365
  58.7 6.9 %collective-permute-start.3 = (bf16[16,32,128]{2,1,0:T(8,128)(2,1)S(1)}, bf16[16,32,128]{2,1,0:T(8,128)(2,1)S(1)}, u32[]{:S(2)}, u32[]{:S(2)}) collective-permute-start(bf16[16,32,128]{2,1,0:T(8,128)(2,1)S(1)} %get-tuple-element.31), channel_id=1, source_target_pairs={{2,0},{4,2},{6,4},{8,6},{10,8},{12,10},{14,12},{3,1},{5,3},{7,5},{... | collective-permute-start | bytes 393224 | tf_op jit(solution)/shard_map/ppermute | solution.py:365
  69.6 62.8 %copy-start = (bf16[64,128,128]{2,1,0:T(8,128)(2,1)S(1)}, bf16[64,128,128]{2,1,0:T(8,128)(2,1)}, u32[]{:S(2)}) copy-start(bf16[64,128,128]{2,1,0:T(8,128)(2,1)} %get-tuple-element.28.refs_3_) | copy-start | bytes 6291460
  69.6 62.8 %copy-start.1 = (s32[64]{0:T(128)S(1)}, s32[64]{0:T(128)}, u32[]{:S(2)}) copy-start(s32[64]{0:T(128)} %target.3) | copy-start | bytes 772
  88.5 27.2 %all-to-all-start.3 = ((bf16[64,16,128]{2,1,0:T(8,128)(2,1)}), bf16[64,16,128]{2,1,0:T(8,128)(2,1)S(1)}, u32[]{:S(2)}, u32[]{:S(2)}) async-start(bf16[64,16,128]{2,1,0:T(8,128)(2,1)} %bitcast.14), calls=%async_computation.3 | async-start | bytes 524288 | tf_op jit(solution)/shard_map/all_to_all | solution.py:410
  100.3 12.3 %collective-permute-start.4 = (bf16[32,32,128]{2,1,0:T(8,128)(2,1)S(1)}, bf16[32,32,128]{2,1,0:T(8,128)(2,1)S(1)}, u32[]{:S(2)}, u32[]{:S(2)}) collective-permute-start(bf16[32,32,128]{2,1,0:T(8,128)(2,1)S(1)} %bitcast.29), channel_id=1, source_target_pairs={{0,128},{128,0},{256,384},{384,256},{16,144},{144,16},{272,400},{4... | collective-permute-start | bytes 786440 | tf_op jit(solution)/shard_map/ppermute | solution.py:446
  112.7 19.7 %collective-permute-start.5 = (bf16[64,32,128]{2,1,0:T(8,128)(2,1)S(1)}, bf16[64,32,128]{2,1,0:T(8,128)(2,1)}, u32[]{:S(2)}, u32[]{:S(2)}) collective-permute-start(bf16[64,32,128]{2,1,0:T(8,128)(2,1)S(1)} %join.1), channel_id=1, source_target_pairs={{0,256},{128,384},{256,0},{384,128},{16,272},{144,400},{272,16},{4... | collective-permute-start | bytes 1572872 | tf_op jit(solution)/shard_map/ppermute | solution.py:457
  116.5 19.1 %all-to-all-start.4 = ((bf16[32,2,16,128]{3,2,1,0:T(8,128)(2,1)}), bf16[32,2,16,128]{3,2,1,0:T(8,128)(2,1)S(1)}, u32[]{:S(2)}, u32[]{:S(2)}) async-start(bf16[32,2,16,128]{3,2,1,0:T(8,128)(2,1)} %finish.1), calls=%async_computation.4 | async-start | bytes 524288 | tf_op jit(solution)/shard_map/all_to_all | solution.py:410

commit v10 on v9

--- a/solution.py
+++ b/solution.py
@@ -8,7 +8,7 @@
 from jax.sharding import PartitionSpec as P
 
 POOL_GROUP = 32
-SPREAD_GROUP = 16
+SPREAD_GROUP = 32
 POOL_VMEM = 60 * 1024 * 1024
 VMEM_LIMIT = 16 * 1024 * 1024
 CHUNK = 16

time: 137 us -> 137 us (level)
  no operation moved by 1% of the time
where the time goes in v10:
time: 137 us; the launch traced here: 136 us
  starting transfers between devices  43.5 us (32%)
  blocking collectives  41 us (30%)
  waiting for transfers between devices  34.2 us (25%)
  Pallas kernels  12.1 us (9%)
  local copies, waits for them, and re-layouts  3.79 us (3%)
  between operations  1.57 us (1%)
    all_to_all x2, blocking collectives, exchange(): lax.all_to_all(value, axis, split_axis=0, concat_axis=0, tiled=True, axis...  38.6 us
    all_to_all x3, starting transfers between devices, exchange(): lax.all_to_all(value, axis, split_axis=0, concat_axis=0, tiled=True, axis...  27.1 us
    ppermute x4, starting transfers between devices, neighbours(): return (lax.ppermute(last, axis, up), lax.ppermute(first, axis, down))  10.6 us
    ppermute x1, waiting for transfers between devices, body(): parts.append(lax.ppermute(joined, 'dom', paired(same_z, shift)))  9.82 us
    ppermute x1, waiting for transfers between devices, body(): parts = [columns, lax.ppermute(columns, 'dom', paired(same_z, 1))]  9.68 us
    ppermute x4, waiting for transfers between devices, neighbours(): return (lax.ppermute(last, axis, up), lax.ppermute(first, axis, down))  9.64 us
    all_to_all x3, waiting for transfers between devices, exchange(): lax.all_to_all(value, axis, split_axis=0, concat_axis=0, tiled=True, axis...  5.08 us
    pallas_call x1, Pallas kernels, pool(): pl.pallas_call(pool_kernel, grid=(tiles // group,), in_specs=[smem, smem,...  4.99 us
  transfers between devices with their start and end apart: 9, of which 7 were waited for; matrix products, arithmetic and copies ran while one was open for 3% of the time, Pallas kernels for 3%

profile of v10, /device:TPU:6, one launch (start us, length us, event | category | flops | bytes accessed | tf_op | source)
XLA Modules:
  0.0 136.2 jit_solution(13054026355399267948)
XLA Ops:
  0.6 0.0 copy-start.2
  1.3 5.0 %pool.1 = (bf16[64,128,128]{2,1,0:T(8,128)(2,1)}, bf16[128,32,128]{2,1,0:T(8,128)(2,1)}) custom-call(s32[64]{0:T(128)} %target.3, s32[1]{0:T(128)S(6)} %copy.34.live, s32[8,8192]{1,0:T(8,128)} %cells.1, f32[8,8192]{1,0:T(8,128)} %weights.1, bf16[32,8192]{1,0:T(8,128)(2,1)} %feats.1), custom_call_target="tpu_custom_call" | custom-call | flops 67108864 | bytes 25165824 | tf_op jit(solution)/shard_map/pool/pallas_call | solution.py:70
  6.3 9.3 %all-to-all-start = ((bf16[128,32,128]{2,1,0:T(8,128)(2,1)}), bf16[128,32,128]{2,1,0:T(8,128)(2,1)S(1)}, u32[]{:S(2)}, u32[]{:S(2)}) async-start(bf16[128,32,128]{2,1,0:T(8,128)(2,1)} %get-tuple-element.17), calls=%async_computation | async-start | bytes 2097152 | tf_op jit(solution)/shard_map/all_to_all | solution.py:410
  15.7 0.0 copy-done.2
  15.7 0.0 copy-start.3
  15.7 0.4 copy.23
  16.1 1.0 copy.22
  17.0 1.6 %rev.3 = bf16[3,3,3,64,64]{4,1,3,2,0:T(4,128)(2,1)S(1)} reverse(bf16[3,3,3,64,64]{4,1,3,2,0:T(4,128)(2,1)S(1)} %copy.23), dimensions={0,1} | reverse | bytes 442368 | tf_op jit(solution)/shard_map/rev | solution.py:401
  18.7 0.1 dynamic-slice_bitcast_fusion
  18.8 0.2 reshape.29.wb
  19.0 0.0 copy-done.3
  19.1 0.4 reshape.28.wf
  19.4 5.1 %all-to-all-done.received = bf16[128,32,128]{2,1,0:T(8,128)(2,1)S(1)} async-done(((bf16[128,32,128]{2,1,0:T(8,128)(2,1)}), bf16[128,32,128]{2,1,0:T(8,128)(2,1)S(1)}, u32[]{:S(2)}, u32[]{:S(2)}) %all-to-all-start) | async-done | bytes 1048608 | tf_op jit(solution)/shard_map/all_to_all | solution.py:410
  24.5 0.1 add_x.1
  24.6 20.4 %all_to_all.25 = bf16[32,32,128]{2,1,0:T(8,128)(2,1)S(1)} all-to-all(bf16[32,32,128]{2,1,0:T(8,128)(2,1)S(1)} %add_x.1), channel_id=1, replica_groups={{0,16,32,48,64,80,96,112},{128,144,160,176,192,208,224,240},{256,272,28..., dimensions={0} | all-to-all | bytes 524288 | tf_op jit(solution)/shard_map/all_to_all | solution.py:410
  45.1 1.9 %collective-permute-start.1 = (bf16[6,32,128]{2,1,0:T(8,128)(2,1)S(1)}, bf16[6,32,128]{2,1,0:T(8,128)(2,1)S(1)}, u32[]{:S(2)}, u32[]{:S(2)}) collective-permute-start(bf16[6,32,128]{2,1,0:T(8,128)(2,1)S(1)} %get-tuple-element.36), channel_id=1, source_target_pairs={{16,0},{32,16},{48,32},{64,48},{80,64},{96,80},{112,96},{128,112},... | collective-permute-start | bytes 147464 | tf_op jit(solution)/shard_map/ppermute | solution.py:365
  47.1 3.9 %collective-permute-start = (bf16[6,32,128]{2,1,0:T(8,128)(2,1)S(1)}, bf16[6,32,128]{2,1,0:T(8,128)(2,1)S(1)}, u32[]{:S(2)}, u32[]{:S(2)}) collective-permute-start(bf16[6,32,128]{2,1,0:T(8,128)(2,1)S(1)} %get-tuple-element.35), channel_id=1, source_target_pairs={{0,16},{16,32},{32,48},{48,64},{64,80},{80,96},{96,112},{112,128},... | collective-permute-start | bytes 147464 | tf_op jit(solution)/shard_map/ppermute | solution.py:365
  51.0 0.1 collective-permute-done.1
  51.1 4.0 %collective-permute-done = bf16[6,32,128]{2,1,0:T(8,128)(2,1)S(1)} collective-permute-done((bf16[6,32,128]{2,1,0:T(8,128)(2,1)S(1)}, bf16[6,32,128]{2,1,0:T(8,128)(2,1)S(1)}, u32[]{:S(2)}, u32[]{:S(2)}) %collective-permute-start) | collective-permute-done | bytes 49184 | tf_op jit(solution)/shard_map/ppermute | solution.py:365
  55.2 3.5 %collective-permute-start.2 = (bf16[16,32,128]{2,1,0:T(8,128)(2,1)S(1)}, bf16[16,32,128]{2,1,0:T(8,128)(2,1)S(1)}, u32[]{:S(2)}, u32[]{:S(2)}) collective-permute-start(bf16[16,32,128]{2,1,0:T(8,128)(2,1)S(1)} %get-tuple-element.32), channel_id=1, source_target_pairs={{0,2},{2,4},{4,6},{6,8},{8,10},{10,12},{12,14},{1,3},{3,5},{5,7},{... | collective-permute-start | bytes 393224 | tf_op jit(solution)/shard_map/ppermute | solution.py:365
  58.7 1.3 collective-permute-start.3
  60.0 1.2 collective-permute-done.2
  61.3 4.3 %collective-permute-done.3 = bf16[16,32,128]{2,1,0:T(8,128)(2,1)S(1)} collective-permute-done((bf16[16,32,128]{2,1,0:T(8,128)(2,1)S(1)}, bf16[16,32,128]{2,1,0:T(8,128)(2,1)S(1)}, u32[]{:S(2)}, u32[]{:S(2)}) %collective-permute-start.3) | collective-permute-done | bytes 131104 | tf_op jit(solution)/shard_map/ppermute | solution.py:365
  65.6 2.4 %all-gather = bf16[104,32,128]{2,1,0:T(8,128)(2,1)S(1)} all-gather(bf16[52,32,128]{2,1,0:T(8,128)(2,1)S(1)} %constant_dynamic-update-slice_fusion), channel_id=2, replica_groups=mesh['dom'=32,'slab'=8,'chan'=2] {'chan'}, dimensions={0}, use_global_device_ids=true | all-gather | bytes 1277952 | tf_op jit(solution)/shard_map/all_gather | solution.py:433
  68.0 1.6 %conv_layer.1 = (bf16[32,2,2,128]{3,2,1,0:T(2,128)(2,1)}, bf16[8,192,128]{2,1,0:T(8,128)(2,1)S(1)}) custom-call(s32[1]{0:T(128)} %bitcast.chan, bf16[2,52,32,128]{3,2,1,0:T(8,128)(2,1)S(1)} %bitcast.28, bf16[3,192,192]{2,1,0:T(8,128)(2,1)S(1)} %reshape.28.wf, bf16[3,96,192]{2,1,0:T(8,128)(2,1)S(1)} %reshape.29.wb), custom_call_target="tpu_custom_call" | custom-call | tf_op jit(solution)/shard_map/conv_layer/pallas_call | solution.py:343
  69.6 0.0 copy-start
  69.6 0.0 copy-start.1
  69.6 18.2 %all_to_all.26.received = bf16[8,192,128]{2,1,0:T(8,128)(2,1)S(1)} all-to-all(bf16[8,192,128]{2,1,0:T(8,128)(2,1)S(1)} %get-tuple-element.25), channel_id=1, replica_groups={{0,16,32,48,64,80,96,112},{128,144,160,176,192,208,224,240},{256,272,28..., dimensions={0} | all-to-all | bytes 786432 | tf_op jit(solution)/shard_map/all_to_all | solution.py:410
  87.8 0.7 split.1
  88.5 11.8 %all-to-all-start.3 = ((bf16[64,16,128]{2,1,0:T(8,128)(2,1)}), bf16[64,16,128]{2,1,0:T(8,128)(2,1)S(1)}, u32[]{:S(2)}, u32[]{:S(2)}) async-start(bf16[64,16,128]{2,1,0:T(8,128)(2,1)} %bitcast.14), calls=%async_computation.3 | async-start | bytes 524288 | tf_op jit(solution)/shard_map/all_to_all | solution.py:410
  100.3 2.7 %collective-permute-start.4 = (bf16[32,32,128]{2,1,0:T(8,128)(2,1)S(1)}, bf16[32,32,128]{2,1,0:T(8,128)(2,1)S(1)}, u32[]{:S(2)}, u32[]{:S(2)}) collective-permute-start(bf16[32,32,128]{2,1,0:T(8,128)(2,1)S(1)} %bitcast.29), channel_id=1, source_target_pairs={{0,128},{128,0},{256,384},{384,256},{16,144},{144,16},{272,400},{4... | collective-permute-start | bytes 786440 | tf_op jit(solution)/shard_map/ppermute | solution.py:446
  103.0 9.7 %collective-permute-done.4.refs_1_ = bf16[32,32,128]{2,1,0:T(8,128)(2,1)S(1)} collective-permute-done((bf16[32,32,128]{2,1,0:T(8,128)(2,1)S(1)}, bf16[32,32,128]{2,1,0:T(8,128)(2,1)S(1)}, u32[]{:S(2)}, u32[]{:S(2)}) %collective-permute-start.4) | collective-permute-done | bytes 262176 | tf_op jit(solution)/shard_map/ppermute | solution.py:446
  112.7 3.1 %collective-permute-start.5 = (bf16[64,32,128]{2,1,0:T(8,128)(2,1)S(1)}, bf16[64,32,128]{2,1,0:T(8,128)(2,1)}, u32[]{:S(2)}, u32[]{:S(2)}) collective-permute-start(bf16[64,32,128]{2,1,0:T(8,128)(2,1)S(1)} %join.1), channel_id=1, source_target_pairs={{0,256},{128,384},{256,0},{384,128},{16,272},{144,400},{272,16},{4... | collective-permute-start | bytes 1572872 | tf_op jit(solution)/shard_map/ppermute | solution.py:457
  115.8 0.0 all-to-all-done.3.received
  115.8 0.8 finish.1
  116.5 6.0 %all-to-all-start.4 = ((bf16[32,2,16,128]{3,2,1,0:T(8,128)(2,1)}), bf16[32,2,16,128]{3,2,1,0:T(8,128)(2,1)S(1)}, u32[]{:S(2)}, u32[]{:S(2)}) async-start(bf16[32,2,16,128]{3,2,1,0:T(8,128)(2,1)} %finish.1), calls=%async_computation.4 | async-start | bytes 524288 | tf_op jit(solution)/shard_map/all_to_all | solution.py:410
  122.6 9.8 %collective-permute-done.5.refs_2_ = bf16[64,32,128]{2,1,0:T(8,128)(2,1)} collective-permute-done((bf16[64,32,128]{2,1,0:T(8,128)(2,1)S(1)}, bf16[64,32,128]{2,1,0:T(8,128)(2,1)}, u32[]{:S(2)}, u32[]{:S(2)}) %collective-permute-start.5) | collective-permute-done | bytes 524320 | tf_op jit(solution)/shard_map/ppermute | solution.py:457
  132.4 0.0 copy-done
  132.4 0.0 copy-done.1
  132.4 2.6 %spread.1 = bf16[32,8192]{1,0:T(8,128)(2,1)} custom-call(s32[64]{0:T(128)S(1)} %copy-done.1, s32[1]{0:T(128)} %bitcast.15.place, bf16[32,32,128]{2,1,0:T(8,128)(2,1)S(1)} %bitcast.31, bf16[32,32,128]{2,1,0:T(8,128)(2,1)S(1)} %collective-permute-done.4.refs_1_, bf16[64,32,128]{2,1,0:T(8,128)(2,1)} %collective-permute-done.5.refs_2_, ...), custom_call_target="tpu_custom_call" | custom-call | flops 67108864 | bytes 6291456 | tf_op jit(solution)/shard_map/spread/pallas_call | solution.py:122
  135.1 0.0 all-to-all-done.4.gathered
  135.1 1.2 unpack.1
  (18 shorter events, 0.2 us)
Async XLA Ops:
  0.6 15.0 %copy-start.2 = (bf16[27,64,64]{2,1,0:T(8,128)(2,1)S(1)}, bf16[27,64,64]{2,1,0:T(8,128)(2,1)}, u32[]{:S(2)}) copy-start(bf16[27,64,64]{2,1,0:T(8,128)(2,1)} %param.12) | copy-start | bytes 663556
  6.3 18.2 %all-to-all-start = ((bf16[128,32,128]{2,1,0:T(8,128)(2,1)}), bf16[128,32,128]{2,1,0:T(8,128)(2,1)S(1)}, u32[]{:S(2)}, u32[]{:S(2)}) async-start(bf16[128,32,128]{2,1,0:T(8,128)(2,1)} %get-tuple-element.17), calls=%async_computation | async-start | bytes 2097152 | tf_op jit(solution)/shard_map/all_to_all | solution.py:410
  15.7 3.4 %copy-start.3 = (bf16[32,2,2,128]{3,2,1,0:T(2,128)(2,1)S(1)}, bf16[32,2,2,128]{3,2,1,0:T(2,128)(2,1)}, u32[]{:S(2)}) copy-start(bf16[32,2,2,128]{3,2,1,0:T(2,128)(2,1)} %param.13) | copy-start | bytes 98308
  45.1 6.0 %collective-permute-start.1 = (bf16[6,32,128]{2,1,0:T(8,128)(2,1)S(1)}, bf16[6,32,128]{2,1,0:T(8,128)(2,1)S(1)}, u32[]{:S(2)}, u32[]{:S(2)}) collective-permute-start(bf16[6,32,128]{2,1,0:T(8,128)(2,1)S(1)} %get-tuple-element.36), channel_id=1, source_target_pairs={{16,0},{32,16},{48,32},{64,48},{80,64},{96,80},{112,96},{128,112},... | collective-permute-start | bytes 147464 | tf_op jit(solution)/shard_map/ppermute | solution.py:365
  47.1 8.1 %collective-permute-start = (bf16[6,32,128]{2,1,0:T(8,128)(2,1)S(1)}, bf16[6,32,128]{2,1,0:T(8,128)(2,1)S(1)}, u32[]{:S(2)}, u32[]{:S(2)}) collective-permute-start(bf16[6,32,128]{2,1,0:T(8,128)(2,1)S(1)} %get-tuple-element.35), channel_id=1, source_target_pairs={{0,16},{16,32},{32,48},{48,64},{64,80},{80,96},{96,112},{112,128},... | collective-permute-start | bytes 147464 | tf_op jit(solution)/shard_map/ppermute | solution.py:365
  55.2 6.0 %collective-permute-start.2 = (bf16[16,32,128]{2,1,0:T(8,128)(2,1)S(1)}, bf16[16,32,128]{2,1,0:T(8,128)(2,1)S(1)}, u32[]{:S(2)}, u32[]{:S(2)}) collective-permute-start(bf16[16,32,128]{2,1,0:T(8,128)(2,1)S(1)} %get-tuple-element.32), channel_id=1, source_target_pairs={{0,2},{2,4},{4,6},{6,8},{8,10},{10,12},{12,14},{1,3},{3,5},{5,7},{... | collective-permute-start | bytes 393224 | tf_op jit(solution)/shard_map/ppermute | solution.py:365
  58.7 6.9 %collective-permute-start.3 = (bf16[16,32,128]{2,1,0:T(8,128)(2,1)S(1)}, bf16[16,32,128]{2,1,0:T(8,128)(2,1)S(1)}, u32[]{:S(2)}, u32[]{:S(2)}) collective-permute-start(bf16[16,32,128]{2,1,0:T(8,128)(2,1)S(1)} %get-tuple-element.31), channel_id=1, source_target_pairs={{2,0},{4,2},{6,4},{8,6},{10,8},{12,10},{14,12},{3,1},{5,3},{7,5},{... | collective-permute-start | bytes 393224 | tf_op jit(solution)/shard_map/ppermute | solution.py:365
  69.6 62.8 %copy-start = (bf16[64,128,128]{2,1,0:T(8,128)(2,1)S(1)}, bf16[64,128,128]{2,1,0:T(8,128)(2,1)}, u32[]{:S(2)}) copy-start(bf16[64,128,128]{2,1,0:T(8,128)(2,1)} %get-tuple-element.28.refs_3_) | copy-start | bytes 6291460
  69.6 62.8 %copy-start.1 = (s32[64]{0:T(128)S(1)}, s32[64]{0:T(128)}, u32[]{:S(2)}) copy-start(s32[64]{0:T(128)} %target.3) | copy-start | bytes 772
  88.5 27.2 %all-to-all-start.3 = ((bf16[64,16,128]{2,1,0:T(8,128)(2,1)}), bf16[64,16,128]{2,1,0:T(8,128)(2,1)S(1)}, u32[]{:S(2)}, u32[]{:S(2)}) async-start(bf16[64,16,128]{2,1,0:T(8,128)(2,1)} %bitcast.14), calls=%async_computation.3 | async-start | bytes 524288 | tf_op jit(solution)/shard_map/all_to_all | solution.py:410
  100.3 12.3 %collective-permute-start.4 = (bf16[32,32,128]{2,1,0:T(8,128)(2,1)S(1)}, bf16[32,32,128]{2,1,0:T(8,128)(2,1)S(1)}, u32[]{:S(2)}, u32[]{:S(2)}) collective-permute-start(bf16[32,32,128]{2,1,0:T(8,128)(2,1)S(1)} %bitcast.29), channel_id=1, source_target_pairs={{0,128},{128,0},{256,384},{384,256},{16,144},{144,16},{272,400},{4... | collective-permute-start | bytes 786440 | tf_op jit(solution)/shard_map/ppermute | solution.py:446
  112.7 19.7 %collective-permute-start.5 = (bf16[64,32,128]{2,1,0:T(8,128)(2,1)S(1)}, bf16[64,32,128]{2,1,0:T(8,128)(2,1)}, u32[]{:S(2)}, u32[]{:S(2)}) collective-permute-start(bf16[64,32,128]{2,1,0:T(8,128)(2,1)S(1)} %join.1), channel_id=1, source_target_pairs={{0,256},{128,384},{256,0},{384,128},{16,272},{144,400},{272,16},{4... | collective-permute-start | bytes 1572872 | tf_op jit(solution)/shard_map/ppermute | solution.py:457
  116.5 18.5 %all-to-all-start.4 = ((bf16[32,2,16,128]{3,2,1,0:T(8,128)(2,1)}), bf16[32,2,16,128]{3,2,1,0:T(8,128)(2,1)S(1)}, u32[]{:S(2)}, u32[]{:S(2)}) async-start(bf16[32,2,16,128]{3,2,1,0:T(8,128)(2,1)} %finish.1), calls=%async_computation.4 | async-start | bytes 524288 | tf_op jit(solution)/shard_map/all_to_all | solution.py:410
